TPU v7x, 128 devices: a whole 4x4x4 slice. The times are simulated.
128 devices in a mesh: ty: 16 (over z_hi, y, core), tx: 8 (over z_lo, x).
Axes of the slice: x: 4, y: 4, z: 4 (z_hi: 2, z_lo: 2; z = z_hi * 2 + z_lo), core: 2. Of those that a mesh axis runs over, the one named last changes fastest.
Arguments:
- inputs: bfloat16 [768, 1024, 128], P('ty', 'tx'), may hold values from -6 to 6
- weight_one: bfloat16 [1152, 128], replicated, may hold values from -0.1875 to 0.1875
- weight_two: bfloat16 [1152, 128], replicated, may hold values from -0.1875 to 0.1875
- weight_three: bfloat16 [1152, 256], replicated, may hold values from -0.1875 to 0.1875
- noise_table: float32 [64, 256], replicated, may hold values from -1.5 to 1.5
- frequency: float32 [2, 128], replicated, may hold values from 0.002 to 0.3
- anchor: int32 [2], replicated, may hold values from 0 to 2048
- noise_index: int32 [1], replicated, may hold values from 0 to 63
- cotangent: bfloat16 [192, 256, 256], P('ty', 'tx'), may hold values from -6 to 6
Outputs:
- coarse_out: bfloat16 [192, 256, 256], P('ty', 'tx')
- grad_inputs: bfloat16 [768, 1024, 128], P('ty', 'tx')
- grad_weight_one: float32 [1152, 128], P(('ty', 'tx'))
- grad_weight_two: float32 [1152, 128], P(('ty', 'tx'))
- grad_weight_three: float32 [1152, 256], P(('ty', 'tx'))
Inputs may be any that keep to these rules, and one draw needn't show every extreme that they name: `noise_index`: a row of noise_table.
All inputs are finite; a program needn't handle non-finite values.
Results may differ from a plain program's by a relative error of at most 0.017.
Values may be sent and summed in bfloat16 or wider, within the bound.
No kernel may reach another device: no remote copies, remote signals or barrier semaphores. Data moves between devices by JAX's collectives and lax.ppermute only.
A program may use at most 128 MiB of HBM per device.

v0:
```python
import jax
import jax.numpy as jnp
from jax import lax
from jax.experimental import pallas as pl
from jax.experimental.pallas import tpu as pltpu
from jax.sharding import PartitionSpec as P

BF16 = jnp.bfloat16
F32 = jnp.float32

KO = 32
KP = 40
HALO = 16
ROWS = 48
PAD_ROWS = ROWS + 2 * HALO
PAIRS = PAD_ROWS // 2
LOWS = PAIRS // 2
VMEM_LIMIT = 60 * 1024 * 1024


def any_spec():
    return pl.BlockSpec(memory_space=pl.ANY)


def vmem_spec():
    return pl.BlockSpec(memory_space=pltpu.VMEM)


def smem_spec():
    return pl.BlockSpec(memory_space=pltpu.SMEM)


def pack_kernel(inputs, cot, down, up, right, left, side32):
    last = pl.ds(ROWS - HALO, HALO)
    first = pl.ds(0, HALO)
    body = pl.ds(0, HALO)
    down[body] = inputs[last]
    up[body] = inputs[first]
    for target, start in ((down, 10), (up, 0)):
        for r in range(2):
            for h in range(2):
                target[HALO, pl.ds((r * 2 + h) * 2, 2)] = cot[start + r, :, h * 128 : (h + 1) * 128].reshape(2, 16, 128)
    for target, unit, start in ((right, 7, 30), (left, 0, 0)):
        for r in range(12):
            line = cot[r].astype(F32)
            for h in range(2):
                side32[pl.ds(r * 4 + h * 2, 2)] = line[start : start + 2, h * 128 : (h + 1) * 128]
        side = side32[...].astype(BF16).reshape(3, 16, 128)
        target[pl.ds(1, ROWS)] = inputs[:, unit]
        target[pl.ds(0, 1)] = side[0:1]
        target[pl.ds(1 + ROWS, 3)] = side


def pack(inputs, cot):
    shapes = [(HALO + 1, 8, 16, 128)] * 2 + [(ROWS + 4, 16, 128)] * 2
    return pl.pallas_call(
        pack_kernel,
        out_shape=[jax.ShapeDtypeStruct(s, BF16) for s in shapes],
        in_specs=[vmem_spec()] * 2,
        out_specs=[vmem_spec()] * 4,
        scratch_shapes=[pltpu.VMEM((48, 128), F32)],
        compiler_params=pltpu.CompilerParams(vmem_limit_bytes=VMEM_LIMIT // 4),
        name="pack_halos",
    )(inputs.reshape(ROWS, 8, 16, 128), cot)


def prep_kernel(grid_rows, grid_cols, place, frequency, w1, w2, w3, w1t, w1b, w2t, w2b, w3b, rows_sc, cols_sc):
    zero = jnp.zeros((128, 128), BF16)
    for source, ahead, back in ((w1, w1t, w1b), (w2, w2t, w2b)):
        for u in range(3):
            for v in range(3):
                tap = source[pl.ds((3 * u + v) * 128, 128), :]
                turned = tap.astype(F32).T.astype(BF16)
                for i in range(2):
                    ahead[pl.ds((4 * u + v + i) * 128, 128), i * 128 : (i + 1) * 128] = tap
                    back[pl.ds((4 * (2 - u) + 2 - v + i) * 128, 128), i * 128 : (i + 1) * 128] = turned
            for target in (ahead, back):
                target[pl.ds((4 * u + 3) * 128, 128), 0:128] = zero
                target[pl.ds(4 * u * 128, 128), 128:256] = zero
    for u in range(3):
        for v in range(3):
            for h in range(2):
                tap = w3[pl.ds((3 * u + v) * 128, 128), h * 128 : (h + 1) * 128]
                at = (3 * (2 - u) + 2 - v) * 256 + h * 128
                w3b[pl.ds(at, 128), :] = tap.astype(F32).T.astype(BF16)
    row = lax.broadcasted_iota(jnp.int32, (PAD_ROWS, 128), 0) - HALO + place[0] * ROWS
    angle = (row + place[2]).astype(F32) * frequency[0:1, :]
    keep = jnp.where((row >= 0) & (row < grid_rows), 1.0, 0.0)
    rows_sc[0] = jnp.sin(angle) * keep
    rows_sc[1] = jnp.cos(angle) * keep
    for p in range(4):
        k = lax.broadcasted_iota(jnp.int32, (KP, 128), 0)
        col = 4 * jnp.where(k < KO + 4, k, k - KP) + p + place[1] * (4 * KO)
        angle = (col + place[3]).astype(F32) * frequency[1:2, :]
        keep = jnp.where((col >= 0) & (col < grid_cols), 1.0, 0.0)
        cols_sc[0, p] = jnp.sin(angle) * keep
        cols_sc[1, p] = jnp.cos(angle) * keep


def prep(grid_rows, grid_cols, place, frequency, w1, w2, w3):
    def kernel(*refs):
        prep_kernel(grid_rows, grid_cols, *refs)

    wide = jax.ShapeDtypeStruct((1536, 256), BF16)
    return pl.pallas_call(
        kernel,
        out_shape=[
            wide,
            wide,
            wide,
            wide,
            jax.ShapeDtypeStruct((2304, 128), BF16),
            jax.ShapeDtypeStruct((2, PAD_ROWS, 128), F32),
            jax.ShapeDtypeStruct((2, 4, KP, 128), F32),
        ],
        in_specs=[smem_spec()] + [vmem_spec()] * 4,
        out_specs=[vmem_spec()] * 7,
        compiler_params=pltpu.CompilerParams(vmem_limit_bytes=VMEM_LIMIT),
        name="prepare_weights",
    )(place, frequency, w1, w2, w3)


def stacked(one, two):
    return jnp.concatenate([one[:KO], two[:KO], one[KO:], two[KO:]], axis=0)


def folded(pair):
    return jnp.concatenate([pair[:32] + pair[32:64], pair[64:72] + pair[72:80]], axis=0)


def line_of(pair, s):
    return jnp.concatenate([pair[32 * s : 32 * s + 32], pair[64 + 8 * s : 72 + 8 * s]], axis=0)


def doubled(line):
    return stacked(line, line)


def before(line):
    return pltpu.roll(line, 1, 0)


def after(line):
    return pltpu.roll(line, KP - 1, 0)


def sigmoid(value):
    return 0.5 * jnp.tanh(0.5 * value) + 0.5


def rounded(value):
    return value.astype(BF16).astype(F32)


def lines_kernel(
    low_rows, low_cols,
    place, inputs, cot, top, bot, lef, rig, ctop, cbot,
    w1t, w2t, w2b, w3, w3b, rows_sc, cols_sc, noise,
    coarse, g1p_out, g1s_out, keep_msg, give_msg,
    pf, sf, stage, held, d1, xm, p2, s2, d2, xl, p3, s3, cp, side32, xg3, g3p, g3s, xb2, xg2, g2p, g2s, xt,
    g1p, g1s, held1, acc, acc3, gw, ms, mask, sems,
):
    k = lax.broadcasted_iota(jnp.int32, (KP, 128), 0)
    col = jnp.where(k < KO + 4, k, k - KP) + place[1] * KO
    inside = jnp.where((col >= 0) & (col < low_cols), 1.0, 0.0)

    def mask_step(at, _):
        row = at - 4 + place[0] * 12
        mask[at] = inside * jnp.where((row >= 0) & (row < low_rows), 1.0, 0.0)
        return 0

    lax.fori_loop(0, LOWS, mask_step, 0)
    modulate = noise[pl.ds(place[4], 1), :]
    scale = 1.0 + modulate[:, 0:128]
    shift = modulate[:, 128:256]

    def first_step(load, base, q, _):
        lines = []
        for i in range(4):
            row = 4 * q + i
            own, right, left = load(row)
            stage[i, 0:128] = own.astype(F32)
            stage[i, 128:144] = right.astype(F32)
            stage[i, 144:160] = left.astype(F32)
            sin_row = rows_sc[0, pl.ds(base + row, 1), :]
            cos_row = rows_sc[1, pl.ds(base + row, 1), :]
            planes = []
            for p in range(4):
                value = stage[i, pl.ds(p, KP, stride=4), :]
                planes.append(value + (sin_row * cols_sc[1, p] + cos_row * cols_sc[0, p]))
            lines.append([before(planes[3])] + planes + [after(planes[0])])
        at = base // 2 + 2 * q
        for j in range(6):
            lanes = slice(j * 128, (j + 1) * 128)
            sf[at, :, lanes] = stacked(held[j], lines[0][j]).astype(BF16)
            pf[at, :, lanes] = stacked(lines[0][j], lines[1][j]).astype(BF16)
            sf[at + 1, :, lanes] = stacked(lines[1][j], lines[2][j]).astype(BF16)
            pf[at + 1, :, lanes] = stacked(lines[2][j], lines[3][j]).astype(BF16)
            held[j] = lines[3][j]
        return 0

    def flat(block):
        return block.reshape(128, 128)

    held[...] = jnp.zeros_like(held)
    load_top = lambda r: (flat(top[r]), ctop[19 + r], ctop[r])
    load_own = lambda r: (flat(inputs[r]), rig[1 + r], lef[1 + r])
    load_bot = lambda r: (flat(bot[r]), cbot[18 + r], cbot[1 + r])
    lax.fori_loop(0, 4, lambda q, c: first_step(load_top, 0, q, c), 0)
    lax.fori_loop(0, 12, lambda q, c: first_step(load_own, HALO, q, c), 0)
    lax.fori_loop(0, 4, lambda q, c: first_step(load_bot, HALO + ROWS, q, c), 0)

    def around(s_ref, p_ref, at, count, lanes, lo=0, hi=80):
        parts = [
            s_ref[pl.ds(at, count), lo:hi, lanes],
            p_ref[pl.ds(at, count), lo:hi, lanes],
            s_ref[pl.ds(at + 1, count), lo:hi, lanes],
        ]
        rows = count * (hi - lo)
        return jnp.concatenate([part.reshape(rows, part.shape[-1]) for part in parts], axis=1)

    def conv_one_step(t, _):
        m = 1 + 2 * t
        one = around(sf, pf, m, 2, slice(0, 512))
        two = around(sf, pf, m, 2, slice(256, 768))
        total = jnp.dot(jnp.concatenate([one, two], axis=0), w1t[...], preferred_element_type=F32)
        for s in range(2):
            folds = []
            for p in range(4):
                at = (p // 2) * 160 + s * 80
                gate = total[at : at + 80, (p % 2) * 128 : (p % 2 + 1) * 128] * scale + shift
                sigma = sigmoid(gate)
                act = gate * sigma
                d1[m + s, :, p * 128 : (p + 1) * 128] = scale * (sigma + act * (1.0 - sigma))
                folds.append(folded(rounded(act)))
            keep = 0.25 * mask[(m + s) // 2]
            xm[m + s, 0] = rounded((folds[0] + folds[1]) * keep)
            xm[m + s, 1] = rounded((folds[2] + folds[3]) * keep)
        return 0

    lax.fori_loop(0, 19, conv_one_step, 0)

    def lines_four(x_ref, s_ref, p_ref, j, _):
        lines = []
        for i in range(3):
            zero, one = x_ref[2 * j - 1 + i, 0], x_ref[2 * j - 1 + i, 1]
            lines.append([before(one), zero, one, after(zero)])
        for n in range(4):
            lanes = slice(n * 128, (n + 1) * 128)
            s_ref[j, :, lanes] = stacked(lines[0][n], lines[1][n]).astype(BF16)
            p_ref[j, :, lanes] = stacked(lines[1][n], lines[2][n]).astype(BF16)
        return 0

    xm[39] = jnp.zeros((2, KP, 128), F32)
    lax.fori_loop(1, 20, lambda j, c: lines_four(xm, s2, p2, j, c), 0)

    def conv_two_step(t, _):
        j = 1 + 6 * t
        total = jnp.dot(around(s2, p2, j, 6, slice(0, 512)), w2t[...], preferred_element_type=F32)
        for s in range(6):
            folds = []
            for q in range(2):
                pre = total[s * 80 : (s + 1) * 80, q * 128 : (q + 1) * 128]
                sigma = sigmoid(pre)
                act = pre * sigma
                d2[j + s, :, q * 128 : (q + 1) * 128] = sigma + act * (1.0 - sigma)
                down = p2[j + s, :, (q + 1) * 128 : (q + 2) * 128].astype(F32)
                folds.append(folded(rounded(down + act)))
            xl[j + s] = rounded((folds[0] + folds[1]) * (0.25 * mask[j + s]))
        return 0

    lax.fori_loop(0, 3, conv_two_step, 0)

    xl[19] = jnp.zeros((KP, 128), F32)

    def lines_three(x_ref, s_ref, p_ref, width, i, _):
        lines = []
        for n in range(3):
            line = x_ref[2 * i - 1 + n]
            lines.append([before(line), line, after(line)])
        for n in range(3):
            lanes = slice(n * width, (n + 1) * width)
            s_ref[i, :, lanes] = stacked(lines[0][n], lines[1][n]).astype(BF16)
            p_ref[i, :, lanes] = stacked(lines[1][n], lines[2][n]).astype(BF16)
        return 0

    lax.fori_loop(1, 10, lambda i, c: lines_three(xl, s3, p3, 128, i, c), 0)

    cp[...] = jnp.zeros_like(cp)
    for h in range(2):
        lanes = slice(h * 128, (h + 1) * 128)
        for r in range(2):
            units = pl.ds((r * 2 + h) * 2, 2)
            cp[r, 0:KO, lanes] = top[HALO, units].reshape(KO, 128).astype(F32)
            cp[14 + r, 0:KO, lanes] = bot[HALO, units].reshape(KO, 128).astype(F32)
    for r in range(12):
        cp[2 + r, 0:KO, :] = cot[r].astype(F32)
    for ref, at in ((rig, KO), (lef, KP - 2)):
        side32[...] = ref[pl.ds(ROWS + 1, 3)].reshape(48, 128).astype(F32)
        for h in range(2):
            for r in range(12):
                cp[2 + r, at : at + 2, h * 128 : (h + 1) * 128] = side32[r * 4 + h * 2 : r * 4 + h * 2 + 2]
    for ref, unit, skip, row, at in (
        (ctop, 18, 8, 0, KP - 2),
        (ctop, 37, 8, 0, KO),
        (cbot, 0, 0, 14, KP - 2),
        (cbot, 17, 0, 14, KO),
    ):
        side32[0:16] = ref[unit].astype(F32)
        for h in range(2):
            for r in range(2):
                start = skip + r * 4 + h * 2
                cp[row + r, at : at + 2, h * 128 : (h + 1) * 128] = side32[start : start + 2]

    def conv_three_step(t, _):
        i = 1 + 4 * t
        total = jnp.dot(around(s3, p3, i, 4, slice(0, 384)), w3[...], preferred_element_type=F32)
        for s in range(4):
            pre = total[s * 80 : (s + 1) * 80]
            sigma = sigmoid(pre)
            act = pre * sigma
            slope = sigma + act * (1.0 - sigma)
            for r in range(2):
                row = 2 * (i + s) + r
                keep = mask[row]
                xg3[row] = cp[row - 2] * line_of(slope, r) * jnp.concatenate([keep, keep], axis=1)

                @pl.when((row >= 4) & (row < 16))
                def _():
                    coarse[row - 4] = act[32 * r : 32 * r + 32].astype(BF16)
        return 0

    lax.fori_loop(0, 2, conv_three_step, 0)
    empty = jnp.zeros((KP, 256), F32)
    xg3[1] = empty
    xg3[18] = empty
    xg3[19] = empty
    lax.fori_loop(1, 10, lambda i, c: lines_three(xg3, g3s, g3p, 256, i, c), 0)

    def weight_terms(grad, field):
        return lax.dot_general(grad, field, (((0,), (0,)), ((), ())), preferred_element_type=F32)

    acc3[...] = weight_terms(
        g3p[2:8, 0:64, 256:512].reshape(384, 256), around(s3, p3, 2, 6, slice(0, 384), 0, 64)
    )

    def back_three_step(t, _):
        i = 1 + 4 * t
        total = jnp.dot(around(g3s, g3p, i, 4, slice(0, 768)), w3b[...], preferred_element_type=F32)
        for s in range(4):
            for r in range(2):
                xb2[2 * (i + s) + r] = 0.25 * line_of(total[s * 80 : (s + 1) * 80], r)
        return 0

    lax.fori_loop(0, 2, back_three_step, 0)

    def grad_two_step(j, _):
        slope = xb2[j] * mask[j]
        for s in range(2):
            for q in range(2):
                d = d2[j, :, q * 128 : (q + 1) * 128]
                xg2[2 * j + s, q] = slope * line_of(d, s)
        return 0

    lax.fori_loop(3, 17, grad_two_step, 0)
    blank = jnp.zeros((2, KP, 128), F32)
    xg2[5] = blank
    xg2[34] = blank
    xg2[35] = blank
    lax.fori_loop(3, 18, lambda j, c: lines_four(xg2, g2s, g2p, j, c), 0)

    def fold_weights(at, taps):
        for u in range(3):
            for v in range(3):
                left = (4 * u + v) * 128
                term = acc[0:128, left : left + 128] + acc[128:256, left + 128 : left + 256]
                gw[at, pl.ds((3 * u + v) * 128, 128), :] = term.T

    acc[...] = weight_terms(
        g2p[4:16, 0:64, 128:384].reshape(768, 256), around(s2, p2, 4, 12, slice(0, 512), 0, 64)
    )
    fold_weights(1, None)

    def back_two_step(t, _):
        j = 3 + 7 * t
        total = jnp.dot(around(g2s, g2p, j, 7, slice(0, 512)), w2b[...], preferred_element_type=F32)
        for s in range(7):
            keep = 0.25 * mask[j + s]
            base = xb2[j + s]
            for q in range(2):
                pair = total[s * 80 : (s + 1) * 80, q * 128 : (q + 1) * 128]
                for r in range(2):
                    xt[2 * (j + s) + r, q] = (base + line_of(pair, r)) * keep
        return 0

    lax.fori_loop(0, 2, back_two_step, 0)

    def grad_line(m, s):
        planes = [xt[m, p // 2] * line_of(d1[m, :, p * 128 : (p + 1) * 128], s) for p in range(4)]
        lines = [before(planes[3])] + planes + [after(planes[0])]
        return [line[:KO] for line in lines]

    first_held = grad_line(7, 1)
    for n in range(6):
        held1[n] = first_held[n]

    def grad_one_step(at, _):
        m = at + 8
        even, odd = grad_line(m, 0), grad_line(m, 1)
        for n in range(6):
            lanes = slice(n * 128, (n + 1) * 128)
            g1s[at, :, lanes] = jnp.concatenate([held1[n], even[n]], axis=0).astype(BF16)
            g1p[at, :, lanes] = jnp.concatenate([even[n], odd[n]], axis=0).astype(BF16)
            held1[n] = odd[n]
        return 0

    lax.fori_loop(0, 25, grad_one_step, 0)
    copies = [
        pltpu.make_async_copy(g1p.at[pl.ds(0, 24)], g1p_out, sems.at[0]),
        pltpu.make_async_copy(g1s, g1s_out, sems.at[1]),
    ]
    for copy in copies:
        copy.start()

    acc[...] = jnp.zeros_like(acc)

    def weight_one_step(t, _):
        at = 8 * t
        grads = jnp.concatenate(
            [g1p[pl.ds(at, 8), :, lanes].reshape(512, 256) for lanes in (slice(128, 384), slice(384, 640))], axis=0
        )
        fields = jnp.concatenate(
            [around(sf, pf, at + 8, 8, lanes, 0, 64) for lanes in (slice(0, 512), slice(256, 768))], axis=0
        )
        acc[...] += weight_terms(grads, fields)
        return 0

    lax.fori_loop(0, 3, weight_one_step, 0)
    fold_weights(0, None)
    for tap in range(9):
        turned = acc3[:, tap * 128 : (tap + 1) * 128].T
        gw[2, pl.ds(tap * 128, 128), :] = turned[:, 0:128]
        gw[3, pl.ds(tap * 128, 128), :] = turned[:, 128:256]
    for n in range(10):
        for t in range(4):
            piece = gw[t, pl.ds(n, 128, stride=9), :] if n < 9 else jnp.zeros((128, 128), F32)
            ms[pl.ds(4 * n + t, 128, stride=40), :] = piece

    core = lax.rem(place[0], 2)

    def msg_step(n, _):
        rows = pl.ds(pl.multiple_of(n * 320, 320), 320)
        keep_msg[rows, :] = ms[pl.ds(pl.multiple_of((2 * n + core) * 320, 320), 320), :].astype(BF16)
        give_msg[rows, :] = ms[pl.ds(pl.multiple_of((2 * n + 1 - core) * 320, 320), 320), :].astype(BF16)
        return 0

    lax.fori_loop(0, 8, msg_step, 0)
    for copy in copies:
        copy.wait()


def levels(low_rows, low_cols, *args):
    def kernel(*refs):
        lines_kernel(low_rows, low_cols, *refs)

    vm = pltpu.VMEM
    return pl.pallas_call(
        kernel,
        out_shape=[
            jax.ShapeDtypeStruct((12, KO, 256), BF16),
            jax.ShapeDtypeStruct((24, 64, 768), BF16),
            jax.ShapeDtypeStruct((25, 64, 768), BF16),
            jax.ShapeDtypeStruct((2560, 128), BF16),
            jax.ShapeDtypeStruct((2560, 128), BF16),
        ],
        in_specs=[smem_spec()] + [vmem_spec()] * (len(args) - 1),
        out_specs=[vmem_spec(), any_spec(), any_spec(), vmem_spec(), vmem_spec()],
        scratch_shapes=[
            vm((PAIRS, 80, 768), BF16),
            vm((PAIRS, 80, 768), BF16),
            vm((4, 160, 128), F32),
            vm((6, KP, 128), F32),
            vm((PAIRS, 80, 512), F32),
            vm((PAIRS, 2, KP, 128), F32),
            vm((LOWS, 80, 512), BF16),
            vm((LOWS, 80, 512), BF16),
            vm((LOWS, 80, 256), F32),
            vm((LOWS, KP, 128), F32),
            vm((10, 80, 384), BF16),
            vm((10, 80, 384), BF16),
            vm((16, KP, 256), F32),
            vm((48, 128), F32),
            vm((LOWS, KP, 256), F32),
            vm((10, 80, 768), BF16),
            vm((10, 80, 768), BF16),
            vm((LOWS, KP, 128), F32),
            vm((PAIRS, 2, KP, 128), F32),
            vm((LOWS, 80, 512), BF16),
            vm((LOWS, 80, 512), BF16),
            vm((PAIRS, 2, KP, 128), F32),
            vm((25, 64, 768), BF16),
            vm((25, 64, 768), BF16),
            vm((6, KO, 128), F32),
            vm((256, 1536), F32),
            vm((256, 1152), F32),
            vm((4, 1152, 128), F32),
            vm((5120, 128), F32),
            vm((LOWS, KP, 128), F32),
            pltpu.SemaphoreType.DMA((2,)),
        ],
        compiler_params=pltpu.CompilerParams(vmem_limit_bytes=VMEM_LIMIT),
        name="encoder_levels",
    )(*args)


def input_kernel(g1p, g1s, w1b, out, stage):
    def step(t, _):
        at = 2 * t
        halves = []
        for lanes in (slice(0, 512), slice(256, 768)):
            parts = [g1s[pl.ds(at, 2), :, lanes], g1p[pl.ds(at, 2), :, lanes], g1s[pl.ds(at + 1, 2), :, lanes]]
            halves.append(jnp.concatenate([part.reshape(128, 512) for part in parts], axis=1))
        total = jnp.dot(jnp.concatenate(halves, axis=0), w1b[...], preferred_element_type=F32)
        for r in range(4):
            for p in range(4):
                rows = (p // 2) * 128 + r * 32
                value = total[rows : rows + 32, (p % 2) * 128 : (p % 2 + 1) * 128]
                stage[r, pl.ds(p, 32, stride=4), :] = value
            out[4 * t + r] = stage[r].astype(BF16)
        return 0

    lax.fori_loop(0, 12, step, 0)


def input_grad(g1p, g1s, w1b):
    return pl.pallas_call(
        input_kernel,
        out_shape=jax.ShapeDtypeStruct((ROWS, 128, 128), BF16),
        in_specs=[vmem_spec()] * 3,
        out_specs=vmem_spec(),
        scratch_shapes=[pltpu.VMEM((4, 128, 128), F32)],
        compiler_params=pltpu.CompilerParams(vmem_limit_bytes=VMEM_LIMIT),
        cost_estimate=pl.CostEstimate(flops=2 * 6144 * 1152 * 128, bytes_accessed=8 * 1024 * 1024, transcendentals=0),
        name="input_grad",
    )(g1p, g1s, w1b)


def collect_kernel(got, one, two, three, total):
    total[...] = got[...].astype(F32).sum(axis=0)
    one[...] = total[pl.ds(0, 9, stride=4), :]
    two[...] = total[pl.ds(1, 9, stride=4), :]
    three[:, 0:128] = total[pl.ds(2, 9, stride=4), :]
    three[:, 128:256] = total[pl.ds(3, 9, stride=4), :]


def collect(got):
    return pl.pallas_call(
        collect_kernel,
        out_shape=[
            jax.ShapeDtypeStruct((9, 128), F32),
            jax.ShapeDtypeStruct((9, 128), F32),
            jax.ShapeDtypeStruct((9, 256), F32),
        ],
        in_specs=[vmem_spec()],
        out_specs=[vmem_spec()] * 3,
        scratch_shapes=[pltpu.VMEM((40, 128), F32)],
        name="collect_weights",
    )(got)


ROW_AXES = ("chip", "core")


def shifted(block, axis, step):
    devices = lax.axis_size(axis)
    pairs = [(i, i + step) for i in range(devices) if 0 <= i + step < devices]
    return lax.ppermute(block, axis, pairs)


def body(inputs, weight_one, weight_two, weight_three, noise_table, frequency, anchor, noise_index, cotangent):
    rows, cols = (lax.axis_size(ROW_AXES), lax.axis_size("tx"))
    place = jnp.concatenate(
        [jnp.stack([lax.axis_index(ROW_AXES), lax.axis_index("tx")]).astype(jnp.int32), anchor, noise_index]
    )
    down, up, right, left = pack(inputs, cotangent)
    lef = shifted(right, "tx", 1)
    rig = shifted(left, "tx", -1)
    top = shifted(down, ROW_AXES, 1)
    bot = shifted(up, ROW_AXES, -1)
    ctop = shifted(jnp.concatenate([lef[33:52], rig[33:52]], axis=0), ROW_AXES, 1)
    cbot = shifted(jnp.concatenate([lef[0:17], rig[0:17]], axis=0), ROW_AXES, -1)
    w1t, w1b, w2t, w2b, w3b, rows_sc, cols_sc = prep(
        rows * ROWS, cols * 4 * KO, place, frequency, weight_one, weight_two, weight_three
    )
    coarse, g1p, g1s, keep_msg, give_msg = levels(
        rows * 12, cols * KO,
        place, inputs.reshape(ROWS, 8, 16, 128), cotangent, top, bot, lef, rig, ctop, cbot,
        w1t, w2t, w2b, weight_three, w3b, rows_sc, cols_sc, noise_table,
    )
    other = lax.ppermute(give_msg, "core", [(0, 1), (1, 0)])
    msg = (keep_msg.astype(F32) + other.astype(F32)).astype(BF16).reshape(64, 40, 128)
    got = lax.all_to_all(msg, ("chip", "tx"), 0, 0, tiled=True)
    grad_inputs = input_grad(g1p, g1s, w1b)
    return (coarse, grad_inputs, *collect(got))


def solution(mesh):
    halves = jax.sharding.Mesh(mesh.devices.reshape(-1, 2, mesh.devices.shape[1]), ("chip", "core", "tx"))
    placed = (P(ROW_AXES, "tx", None), P(), P(), P(), P(), P(), P(), P(), P(ROW_AXES, "tx", None))
    return jax.shard_map(
        body,
        mesh=halves,
        in_specs=placed,
        out_specs=(
            P(ROW_AXES, "tx", None),
            P(ROW_AXES, "tx", None),
            P((*ROW_AXES, "tx"), None),
            P((*ROW_AXES, "tx"), None),
            P((*ROW_AXES, "tx"), None),
        ),
        check_vma=False,
    )
```

profile of v0, /device:TPU:0, one launch (start us, length us, event | category | flops | bytes accessed | tf_op | source)
XLA Modules:
  0.0 96.1 jit_solution(5155825078208609214)
XLA Ops:
  0.6 0.0 copy-start
  0.7 1.4 %copy-done = bf16[48,128,128]{2,1,0:T(8,128)(2,1)S(1)} copy-done((bf16[48,128,128]{2,1,0:T(8,128)(2,1)S(1)}, bf16[48,128,128]{2,1,0:T(8,128)(2,1)}, u32[]{:S(2)}) %copy-start) | copy-done | bytes 1572888
  2.1 0.9 copy-done.1
  3.0 0.1 pack_halos.1
  3.1 3.5 %collective-permute-start.2 = (bf16[52,16,128]{2,1,0:T(8,128)(2,1)S(1)}, bf16[52,16,128]{2,1,0:T(8,128)(2,1)S(1)}, u32[]{:S(2)}, u32[]{:S(2)}) collective-permute-start(bf16[52,16,128]{2,1,0:T(8,128)(2,1)S(1)} %get-tuple-element.26), channel_id=1, source_target_pairs={{0,1},{1,2},{2,3},{3,4},{4,5},{5,6},{6,7},{8,9},{9,10},{10,11},{11... | collective-permute-start | bytes 638984 | tf_op jit(solution)/shard_map/ppermute | solution.py:577
  6.6 1.3 %collective-permute-start.3 = (bf16[52,16,128]{2,1,0:T(8,128)(2,1)S(1)}, bf16[52,16,128]{2,1,0:T(8,128)(2,1)S(1)}, u32[]{:S(2)}, u32[]{:S(2)}) collective-permute-start(bf16[52,16,128]{2,1,0:T(8,128)(2,1)S(1)} %get-tuple-element.27), channel_id=1, source_target_pairs={{1,0},{2,1},{3,2},{4,3},{5,4},{6,5},{7,6},{9,8},{10,9},{11,10},{12... | collective-permute-start | bytes 638984 | tf_op jit(solution)/shard_map/ppermute | solution.py:577
  7.9 1.5 %collective-permute-start = (bf16[17,8,16,128]{3,2,1,0:T(8,128)(2,1)S(1)}, bf16[17,8,16,128]{3,2,1,0:T(8,128)(2,1)S(1)}, u32[]{:S(2)}, u32[]{:S(2)}) collective-permute-start(bf16[17,8,16,128]{3,2,1,0:T(8,128)(2,1)S(1)} %get-tuple-element.24), channel_id=1, source_target_pairs={{0,8},{8,16},{16,24},{24,32},{32,40},{40,48},{48,56},{56,64},{64,7... | collective-permute-start | bytes 1671176 | tf_op jit(solution)/shard_map/ppermute | solution.py:577
  9.4 1.3 %collective-permute-start.1 = (bf16[17,8,16,128]{3,2,1,0:T(8,128)(2,1)S(1)}, bf16[17,8,16,128]{3,2,1,0:T(8,128)(2,1)S(1)}, u32[]{:S(2)}, u32[]{:S(2)}) collective-permute-start(bf16[17,8,16,128]{3,2,1,0:T(8,128)(2,1)S(1)} %get-tuple-element.25), channel_id=1, source_target_pairs={{8,0},{16,8},{24,16},{32,24},{40,32},{48,40},{56,48},{64,56},{72,6... | collective-permute-start | bytes 1671176 | tf_op jit(solution)/shard_map/ppermute | solution.py:577
  10.7 0.4 collective-permute-done.2.refs_5_
  11.1 4.1 %collective-permute-done.3.refs_6_ = bf16[52,16,128]{2,1,0:T(8,128)(2,1)S(1)} collective-permute-done((bf16[52,16,128]{2,1,0:T(8,128)(2,1)S(1)}, bf16[52,16,128]{2,1,0:T(8,128)(2,1)S(1)}, u32[]{:S(2)}, u32[]{:S(2)}) %collective-permute-start.3) | collective-permute-done | bytes 213024 | tf_op jit(solution)/shard_map/ppermute | solution.py:577
  15.3 1.3 %collective-permute-start.4 = (bf16[38,16,128]{2,1,0:T(8,128)(2,1)S(1)}, bf16[38,16,128]{2,1,0:T(8,128)(2,1)S(1)}, u32[]{:S(2)}, u32[]{:S(2)}) collective-permute-start(bf16[38,16,128]{2,1,0:T(8,128)(2,1)S(1)} %pad_maximum_fusion), channel_id=1, source_target_pairs={{0,8},{8,16},{16,24},{24,32},{32,40},{40,48},{48,56},{56,64},{64,7... | collective-permute-start | bytes 466952 | tf_op jit(solution)/shard_map/ppermute | solution.py:577
  16.6 1.3 %collective-permute-start.5 = (bf16[34,16,128]{2,1,0:T(8,128)(2,1)S(1)}, bf16[34,16,128]{2,1,0:T(8,128)(2,1)S(1)}, u32[]{:S(2)}, u32[]{:S(2)}) collective-permute-start(bf16[34,16,128]{2,1,0:T(8,128)(2,1)S(1)} %pad_maximum_fusion.1), channel_id=1, source_target_pairs={{8,0},{16,8},{24,16},{32,24},{40,32},{48,40},{56,48},{64,56},{72,6... | collective-permute-start | bytes 417800 | tf_op jit(solution)/shard_map/ppermute | solution.py:577
  18.6 0.0 copy-done.9
  18.6 0.6 pad_add_fusion.refs_0_
  19.2 3.6 %prepare_weights.1 = (bf16[1536,256]{1,0:T(8,128)(2,1)}, bf16[1536,256]{1,0:T(8,128)(2,1)}, bf16[1536,256]{1,0:T(8,128)(2,1)}, bf16[1536,256]{1,0:T(8,128)(2,1)}...) custom-call(s32[5]{0:T(128)} %pad_add_fusion.refs_0_, f32[2,128]{1,0:T(2,128)} %refs_1_.1, ...), custom_call_target="tpu_custom_call" | custom-call | tf_op jit(solution)/shard_map/prepare_weights/pallas_call | solution.py:105
  22.8 0.0 collective-permute-done.5.refs_8_
  22.8 0.0 collective-permute-done.4.refs_7_
  22.8 0.0 collective-permute-done.refs_3_
  22.8 0.0 collective-permute-done.1.refs_4_
  22.9 0.6 copy-done.8
  23.4 0.1 copy-done.7
  23.5 0.2 copy-done.5
  23.7 0.2 copy-done.6
  23.9 30.8 %encoder_levels.1 = (bf16[12,32,256]{2,1,0:T(8,128)(2,1)}, bf16[24,64,768]{2,1,0:T(8,128)(2,1)}, bf16[25,64,768]{2,1,0:T(8,128)(2,1)}, bf16[2560,128]{1,0:T(8,128)(2,1)}, bf16[2560,128]{1,0:T(8,128)(2,1)}) custom-call(s32[5]{0:T(128)} %pad_add_fusion.refs_0_, bf16[48,8,16,128]{3,2,1,0:T(8,128)(2,1)} %bitcast.4, bf16[12,32,256]{2,1,0:T(8,128)(2,1)} %refs_2_.3, ...), custom_call_target="tpu_custom_call" | custom-call | tf_op jit(solution)/shard_map/encoder_levels/pallas_call | solution.py:467
  54.6 3.0 %collective-permute-start.6 = (bf16[2560,128]{1,0:T(8,128)(2,1)}, bf16[2560,128]{1,0:T(8,128)(2,1)S(1)}, u32[]{:S(2)}, u32[]{:S(2)}) collective-permute-start(bf16[2560,128]{1,0:T(8,128)(2,1)} %get-tuple-element.39), channel_id=1, source_target_pairs={{0,8},{8,0},{1,9},{9,1},{2,10},{10,2},{3,11},{11,3},{4,12},{12,4},... | collective-permute-start | bytes 1966088 | tf_op jit(solution)/shard_map/ppermute | solution.py:600
  57.7 1.9 %collective-permute-done.6 = bf16[2560,128]{1,0:T(8,128)(2,1)S(1)} collective-permute-done((bf16[2560,128]{1,0:T(8,128)(2,1)}, bf16[2560,128]{1,0:T(8,128)(2,1)S(1)}, u32[]{:S(2)}, u32[]{:S(2)}) %collective-permute-start.6) | collective-permute-done | bytes 655392 | tf_op jit(solution)/shard_map/ppermute | solution.py:600
  59.6 2.1 %add_convert_fusion = bf16[2560,128]{1,0:T(8,128)(2,1)} fusion(bf16[2560,128]{1,0:T(8,128)(2,1)S(1)} %collective-permute-done.6, bf16[2560,128]{1,0:T(8,128)(2,1)} %get-tuple-element.38), kind=kLoop, calls=%fused_computation | loop fusion | flops 1310720 | bytes 1966080 | tf_op jit(solution)/shard_map/convert_element_type | solution.py:601
  61.7 16.5 %all-to-all-start = ((bf16[64,40,128]{2,1,0:T(8,128)(2,1)}), bf16[64,40,128]{2,1,0:T(8,128)(2,1)S(1)}, u32[]{:S(2)}, u32[]{:S(2)}) async-start(bf16[64,40,128]{2,1,0:T(8,128)(2,1)} %bitcast.3), calls=%async_computation | async-start | bytes 1310720 | tf_op jit(solution)/shard_map/all_to_all | solution.py:602
  78.2 8.4 %input_grad.1 = bf16[48,128,128]{2,1,0:T(8,128)(2,1)} custom-call(bf16[24,64,768]{2,1,0:T(8,128)(2,1)} %get-tuple-element.35.g1p, bf16[25,64,768]{2,1,0:T(8,128)(2,1)} %get-tuple-element.36.g1s, bf16[1536,256]{1,0:T(8,128)(2,1)} %get-tuple-element.37.w1b), custom_call_target="tpu_custom_call" | custom-call | flops 1811939328 | bytes 8388608 | tf_op jit(solution)/shard_map/input_grad/pallas_call | solution.py:536
  86.6 6.8 %all-to-all-done.got = bf16[64,40,128]{2,1,0:T(8,128)(2,1)S(1)} async-done(((bf16[64,40,128]{2,1,0:T(8,128)(2,1)}), bf16[64,40,128]{2,1,0:T(8,128)(2,1)S(1)}, u32[]{:S(2)}, u32[]{:S(2)}) %all-to-all-start) | async-done | bytes 655392 | tf_op jit(solution)/shard_map/all_to_all | solution.py:602
  93.4 0.9 copy-done.2
  94.3 1.8 %collect_weights.1 = (f32[9,128]{1,0:T(8,128)}, f32[9,128]{1,0:T(8,128)}, f32[9,256]{1,0:T(8,128)}) custom-call(bf16[64,40,128]{2,1,0:T(8,128)(2,1)} %copy-done.2), custom_call_target="tpu_custom_call" | custom-call | tf_op jit(solution)/shard_map/collect_weights/pallas_call | solution.py:557
  (17 shorter events, 0.1 us)
Async XLA Ops:
  0.6 17.9 %copy-start.9 = (s32[2]{0:T(128)S(1)}, s32[2]{0:T(128)}, u32[]{:S(2)}) copy-start(s32[2]{0:T(128)} %param.15) | copy-start | bytes 28
  0.6 1.4 %copy-start = (bf16[48,128,128]{2,1,0:T(8,128)(2,1)S(1)}, bf16[48,128,128]{2,1,0:T(8,128)(2,1)}, u32[]{:S(2)}) copy-start(bf16[48,128,128]{2,1,0:T(8,128)(2,1)} %param.9) | copy-start | bytes 4718596
  2.1 0.9 copy-start.1
  3.1 8.0 %collective-permute-start.2 = (bf16[52,16,128]{2,1,0:T(8,128)(2,1)S(1)}, bf16[52,16,128]{2,1,0:T(8,128)(2,1)S(1)}, u32[]{:S(2)}, u32[]{:S(2)}) collective-permute-start(bf16[52,16,128]{2,1,0:T(8,128)(2,1)S(1)} %get-tuple-element.26), channel_id=1, source_target_pairs={{0,1},{1,2},{2,3},{3,4},{4,5},{5,6},{6,7},{8,9},{9,10},{10,11},{11... | collective-permute-start | bytes 638984 | tf_op jit(solution)/shard_map/ppermute | solution.py:577
  6.6 8.6 %collective-permute-start.3 = (bf16[52,16,128]{2,1,0:T(8,128)(2,1)S(1)}, bf16[52,16,128]{2,1,0:T(8,128)(2,1)S(1)}, u32[]{:S(2)}, u32[]{:S(2)}) collective-permute-start(bf16[52,16,128]{2,1,0:T(8,128)(2,1)S(1)} %get-tuple-element.27), channel_id=1, source_target_pairs={{1,0},{2,1},{3,2},{4,3},{5,4},{6,5},{7,6},{9,8},{10,9},{11,10},{12... | collective-permute-start | bytes 638984 | tf_op jit(solution)/shard_map/ppermute | solution.py:577
  7.9 14.9 %collective-permute-start = (bf16[17,8,16,128]{3,2,1,0:T(8,128)(2,1)S(1)}, bf16[17,8,16,128]{3,2,1,0:T(8,128)(2,1)S(1)}, u32[]{:S(2)}, u32[]{:S(2)}) collective-permute-start(bf16[17,8,16,128]{3,2,1,0:T(8,128)(2,1)S(1)} %get-tuple-element.24), channel_id=1, source_target_pairs={{0,8},{8,16},{16,24},{24,32},{32,40},{40,48},{48,56},{56,64},{64,7... | collective-permute-start | bytes 1671176 | tf_op jit(solution)/shard_map/ppermute | solution.py:577
  9.4 13.4 %collective-permute-start.1 = (bf16[17,8,16,128]{3,2,1,0:T(8,128)(2,1)S(1)}, bf16[17,8,16,128]{3,2,1,0:T(8,128)(2,1)S(1)}, u32[]{:S(2)}, u32[]{:S(2)}) collective-permute-start(bf16[17,8,16,128]{3,2,1,0:T(8,128)(2,1)S(1)} %get-tuple-element.25), channel_id=1, source_target_pairs={{8,0},{16,8},{24,16},{32,24},{40,32},{48,40},{56,48},{64,56},{72,6... | collective-permute-start | bytes 1671176 | tf_op jit(solution)/shard_map/ppermute | solution.py:577
  11.1 11.8 %copy-start.3 = (bf16[52,16,128]{2,1,0:T(8,128)(2,1)}, bf16[52,16,128]{2,1,0:T(8,128)(2,1)S(1)}, u32[]{:S(2)}) copy-start(bf16[52,16,128]{2,1,0:T(8,128)(2,1)S(1)} %collective-permute-done.2.refs_5_) | copy-start | bytes 638980
  15.2 7.6 %copy-start.4 = (bf16[52,16,128]{2,1,0:T(8,128)(2,1)}, bf16[52,16,128]{2,1,0:T(8,128)(2,1)S(1)}, u32[]{:S(2)}) copy-start(bf16[52,16,128]{2,1,0:T(8,128)(2,1)S(1)} %collective-permute-done.3.refs_6_) | copy-start | bytes 638980
  15.3 7.5 %collective-permute-start.4 = (bf16[38,16,128]{2,1,0:T(8,128)(2,1)S(1)}, bf16[38,16,128]{2,1,0:T(8,128)(2,1)S(1)}, u32[]{:S(2)}, u32[]{:S(2)}) collective-permute-start(bf16[38,16,128]{2,1,0:T(8,128)(2,1)S(1)} %pad_maximum_fusion), channel_id=1, source_target_pairs={{0,8},{8,16},{16,24},{24,32},{32,40},{40,48},{48,56},{56,64},{64,7... | collective-permute-start | bytes 466952 | tf_op jit(solution)/shard_map/ppermute | solution.py:577
  16.6 6.2 %collective-permute-start.5 = (bf16[34,16,128]{2,1,0:T(8,128)(2,1)S(1)}, bf16[34,16,128]{2,1,0:T(8,128)(2,1)S(1)}, u32[]{:S(2)}, u32[]{:S(2)}) collective-permute-start(bf16[34,16,128]{2,1,0:T(8,128)(2,1)S(1)} %pad_maximum_fusion.1), channel_id=1, source_target_pairs={{8,0},{16,8},{24,16},{32,24},{40,32},{48,40},{56,48},{64,56},{72,6... | collective-permute-start | bytes 417800 | tf_op jit(solution)/shard_map/ppermute | solution.py:577
  22.8 0.6 copy-start.8
  22.8 0.7 copy-start.7
  22.8 0.9 copy-start.5
  22.8 1.0 %copy-start.6 = (bf16[17,8,16,128]{3,2,1,0:T(8,128)(2,1)}, bf16[17,8,16,128]{3,2,1,0:T(8,128)(2,1)S(1)}, u32[]{:S(2)}) copy-start(bf16[17,8,16,128]{3,2,1,0:T(8,128)(2,1)S(1)} %collective-permute-done.1.refs_4_) | copy-start | bytes 1671172
  54.6 4.9 %collective-permute-start.6 = (bf16[2560,128]{1,0:T(8,128)(2,1)}, bf16[2560,128]{1,0:T(8,128)(2,1)S(1)}, u32[]{:S(2)}, u32[]{:S(2)}) collective-permute-start(bf16[2560,128]{1,0:T(8,128)(2,1)} %get-tuple-element.39), channel_id=1, source_target_pairs={{0,8},{8,0},{1,9},{9,1},{2,10},{10,2},{3,11},{11,3},{4,12},{12,4},... | collective-permute-start | bytes 1966088 | tf_op jit(solution)/shard_map/ppermute | solution.py:600
  61.7 31.7 %all-to-all-start = ((bf16[64,40,128]{2,1,0:T(8,128)(2,1)}), bf16[64,40,128]{2,1,0:T(8,128)(2,1)S(1)}, u32[]{:S(2)}, u32[]{:S(2)}) async-start(bf16[64,40,128]{2,1,0:T(8,128)(2,1)} %bitcast.3), calls=%async_computation | async-start | bytes 1310720 | tf_op jit(solution)/shard_map/all_to_all | solution.py:602
  93.4 0.9 copy-start.2
where the time goes:
time: 96.6 us; the launch traced here: 96.1 us
  Pallas kernels  44.8 us (46%)
  starting transfers between devices  29.6 us (31%)
  waiting for transfers between devices  13.3 us (14%)
  local copies, waits for them, and re-layouts  4.25 us (4%)
  other arithmetic  2.73 us (3%)
  between operations  1.49 us (2%)
    pallas_call x1, Pallas kernels, levels(): pl.pallas_call(kernel, out_shape=[jax.ShapeDtypeStruct((12, KO, 256), BF1...  30.8 us
    all_to_all x1, starting transfers between devices, body(): got = lax.all_to_all(msg, ('chip', 'tx'), 0, 0, tiled=True)  16.5 us
    ppermute x6, starting transfers between devices, shifted(): return lax.ppermute(block, axis, pairs)  10.2 us
    pallas_call x1, Pallas kernels, input_grad(): pl.pallas_call(input_kernel, out_shape=jax.ShapeDtypeStruct((ROWS, 128, 1...  8.45 us
    all_to_all x1, waiting for transfers between devices, body(): got = lax.all_to_all(msg, ('chip', 'tx'), 0, 0, tiled=True)  6.82 us
    ppermute x6, waiting for transfers between devices, shifted(): return lax.ppermute(block, axis, pairs)  4.5 us
    unnamed x20, local copies, waits for them, and re-layouts  4.22 us
    pallas_call x1, Pallas kernels, prep(): pl.pallas_call(kernel, out_shape=[wide, wide, wide, wide, jax.ShapeDtypeS...  3.61 us
  transfers between devices with their start and end apart: 8, of which 4 were waited for; matrix products, arithmetic and copies ran while one was open for 1% of the time, Pallas kernels for 13%

commit v1 on v0

v1 whole, which is shorter than its diff:
```python
import jax
import jax.numpy as jnp
from jax import lax
from jax.experimental import pallas as pl
from jax.experimental.pallas import tpu as pltpu
from jax.sharding import PartitionSpec as P

BF16 = jnp.bfloat16
F32 = jnp.float32

KO = 32
KP = 40
HALO = 16
ROWS = 48
PAD_ROWS = ROWS + 2 * HALO
PAIRS = PAD_ROWS // 2
LOWS = PAIRS // 2
VMEM_LIMIT = 60 * 1024 * 1024


def any_spec():
    return pl.BlockSpec(memory_space=pl.ANY)


def vmem_spec():
    return pl.BlockSpec(memory_space=pltpu.VMEM)


def smem_spec():
    return pl.BlockSpec(memory_space=pltpu.SMEM)


ROW_AXES = ("chip", "core")


def own_place():
    return lax.axis_index(ROW_AXES), lax.axis_index("tx")


def side_kernel(inputs, cot, right, left, cots, side32, sems):
    copies = [
        pltpu.make_async_copy(inputs.at[:, 7], right.at[pl.ds(1, ROWS)], sems.at[0]),
        pltpu.make_async_copy(inputs.at[:, 0], left.at[pl.ds(1, ROWS)], sems.at[1]),
    ]
    for copy in copies:
        copy.start()
    for target, start in ((right, 30), (left, 0)):
        for r in range(12):
            line = cot[r].astype(F32)
            for h in range(2):
                side32[pl.ds(r * 4 + h * 2, 2)] = line[start : start + 2, h * 128 : (h + 1) * 128]
        side = side32[...].astype(BF16).reshape(3, 16, 128)
        target[pl.ds(0, 1)] = side[0:1]
        target[pl.ds(1 + ROWS, 3)] = side
    for at, start in ((0, 10), (1, 0)):
        for r in range(2):
            for h in range(2):
                cots[at, pl.ds((r * 2 + h) * 2, 2)] = cot[start + r, :, h * 128 : (h + 1) * 128].reshape(2, 16, 128)
    for copy in copies:
        copy.wait()


def sides(inputs, cot):
    return pl.pallas_call(
        side_kernel,
        out_shape=[jax.ShapeDtypeStruct((ROWS + 4, 16, 128), BF16)] * 2 + [jax.ShapeDtypeStruct((2, 8, 16, 128), BF16)],
        in_specs=[any_spec(), vmem_spec()],
        out_specs=[vmem_spec()] * 3,
        scratch_shapes=[pltpu.VMEM((48, 128), F32), pltpu.SemaphoreType.DMA((2,))],
        name="pack_columns",
    )(inputs, cot)


def rim(inputs, cots, lef, rig, row, cot_unit):
    sides = [side[1 + row : 3 + row, None] for side in (rig, lef)]
    cells = jnp.concatenate([inputs[row : row + 2], *sides], axis=1)
    units = jnp.concatenate([cots, rig[cot_unit : cot_unit + 1], lef[cot_unit : cot_unit + 1]], axis=0)
    return jnp.concatenate([cells, units[None]], axis=0)


def weight_forms(w1, w2, w3, w1t, w1b, w2t, w2b, w3b):
    zero = jnp.zeros((128, 128), BF16)
    for source, ahead, back in ((w1, w1t, w1b), (w2, w2t, w2b)):
        for u in range(3):
            for v in range(3):
                tap = source[pl.ds((3 * u + v) * 128, 128), :]
                for i in range(2):
                    side = slice(i * 128, (i + 1) * 128)
                    ahead[pl.ds((4 * u + v + i) * 128, 128), side] = tap
                    at = (4 * (2 - u) + 2 - v + i) * 128
                    back[side, at : at + 128] = tap
            for i, j in ((0, 3), (1, 0)):
                at = (4 * u + j) * 128
                side = slice(i * 128, (i + 1) * 128)
                ahead[pl.ds(at, 128), side] = zero
                back[side, at : at + 128] = zero
    for u in range(3):
        for v in range(3):
            at = (3 * (2 - u) + 2 - v) * 256
            w3b[:, at : at + 256] = w3[pl.ds((3 * u + v) * 128, 128), :]


def wave_tables(grid_rows, grid_cols, anchor, frequency, rows_sc, cols_sc):
    own_row, own_col = own_place()
    row = lax.broadcasted_iota(jnp.int32, (PAD_ROWS, 128), 0) - HALO + own_row * ROWS
    angle = (row + anchor[0]).astype(F32) * frequency[0:1, :]
    keep = jnp.where((row >= 0) & (row < grid_rows), 1.0, 0.0)
    rows_sc[0] = jnp.sin(angle) * keep
    rows_sc[1] = jnp.cos(angle) * keep
    for p in range(4):
        k = lax.broadcasted_iota(jnp.int32, (KP, 128), 0)
        col = 4 * jnp.where(k < KO + 4, k, k - KP) + p + own_col * (4 * KO)
        angle = (col + anchor[1]).astype(F32) * frequency[1:2, :]
        keep = jnp.where((col >= 0) & (col < grid_cols), 1.0, 0.0)
        cols_sc[0, p] = jnp.sin(angle) * keep
        cols_sc[1, p] = jnp.cos(angle) * keep


def prep_kernel(grid_rows, grid_cols, anchor, w1, w2, w3, frequency, w1t, w1b, w2t, w2b, w3b, rows_sc, cols_sc):
    weight_forms(w1, w2, w3, w1t, w1b, w2t, w2b, w3b)
    wave_tables(grid_rows, grid_cols, anchor, frequency, rows_sc, cols_sc)


def prep(grid_rows, grid_cols, anchor, w1, w2, w3, frequency):
    def kernel(*refs):
        prep_kernel(grid_rows, grid_cols, *refs)

    shape = jax.ShapeDtypeStruct
    return pl.pallas_call(
        kernel,
        out_shape=[
            shape((1536, 256), BF16),
            shape((256, 1536), BF16),
            shape((1536, 256), BF16),
            shape((256, 1536), BF16),
            shape((128, 2304), BF16),
            shape((2, PAD_ROWS, 128), F32),
            shape((2, 4, KP, 128), F32),
        ],
        in_specs=[smem_spec()] + [vmem_spec()] * 4,
        out_specs=[vmem_spec()] * 7,
        compiler_params=pltpu.CompilerParams(vmem_limit_bytes=VMEM_LIMIT),
        name="weight_forms",
    )(anchor, w1, w2, w3, frequency)


def fill_mask(low_rows, low_cols, mask):
    own_row, own_col = own_place()
    k = lax.broadcasted_iota(jnp.int32, (KP, 128), 0)
    col = jnp.where(k < KO + 4, k, k - KP) + own_col * KO
    inside = jnp.where((col >= 0) & (col < low_cols), 1.0, 0.0)

    def step(at, _):
        row = at - 4 + own_row * 12
        mask[at] = inside * jnp.where((row >= 0) & (row < low_rows), 1.0, 0.0)
        return 0

    lax.fori_loop(0, LOWS, step, 0)


def stacked(one, two):
    return jnp.concatenate([one[:KO], two[:KO], one[KO:], two[KO:]], axis=0)


def folded(pair):
    return jnp.concatenate([pair[:32] + pair[32:64], pair[64:72] + pair[72:80]], axis=0)


def line_of(pair, s):
    return jnp.concatenate([pair[32 * s : 32 * s + 32], pair[64 + 8 * s : 72 + 8 * s]], axis=0)


def doubled(line):
    return stacked(line, line)


def before(line):
    return pltpu.roll(line, 1, 0)


def after(line):
    return pltpu.roll(line, KP - 1, 0)


def silu_parts(half):
    th = jnp.tanh(half)
    act = half + half * th
    return act, (1.0 + act) + th * (1.0 - act)


def rounded(value):
    return value.astype(BF16).astype(F32)


def flat(block):
    return block.reshape(128, 128)


def modulation(noise, noise_index):
    modulate = noise[pl.ds(noise_index[0], 1), :]
    return 1.0 + modulate[:, 0:128], modulate[:, 128:256]


def first_lines(load, base, at, tables, stage, held, sf, pf):
    rows_sc, cols_sc = tables
    lines = []
    for i in range(4):
        own, right, left = load(i)
        stage[i, 0:128] = own.astype(F32)
        stage[i, 128:144] = right.astype(F32)
        stage[i, 144:160] = left.astype(F32)
        sin_row = rows_sc[0, pl.ds(base + i, 1), :]
        cos_row = rows_sc[1, pl.ds(base + i, 1), :]
        planes = []
        for p in range(4):
            value = stage[i, pl.ds(p, KP, stride=4), :]
            planes.append(value + (sin_row * cols_sc[1, p] + cos_row * cols_sc[0, p]))
        lines.append([before(planes[3])] + planes + [after(planes[0])])
    for j in range(6):
        lanes = slice(j * 128, (j + 1) * 128)
        sf[at, :, lanes] = stacked(held[j], lines[0][j]).astype(BF16)
        pf[at, :, lanes] = stacked(lines[0][j], lines[1][j]).astype(BF16)
        sf[at + 1, :, lanes] = stacked(lines[1][j], lines[2][j]).astype(BF16)
        pf[at + 1, :, lanes] = stacked(lines[2][j], lines[3][j]).astype(BF16)
        held[j] = lines[3][j]


def around(s_ref, p_ref, at, count, lanes, lo=0, hi=80):
    parts = [
        s_ref[pl.ds(at, count), lo:hi, lanes],
        p_ref[pl.ds(at, count), lo:hi, lanes],
        s_ref[pl.ds(at + 1, count), lo:hi, lanes],
    ]
    rows = count * (hi - lo)
    return jnp.concatenate([part.reshape(rows, part.shape[-1]) for part in parts], axis=1)


def product(left, right):
    return jnp.dot(left, right, preferred_element_type=F32)


def product_turned(left, right):
    return lax.dot_general(left, right, (((1,), (1,)), ((), ())), preferred_element_type=F32)


def weight_terms(grad, field):
    return lax.dot_general(grad, field, (((0,), (0,)), ((), ())), preferred_element_type=F32)


def pipeline(steps, dot, post, z0, z1):
    def put(z, t):
        total = dot(t)
        z[0 : total.shape[0], :] = total

    put(z0, 0)

    def two(i, _):
        put(z1, 2 * i + 1)
        post(2 * i, z0)
        put(z0, 2 * i + 2)
        post(2 * i + 1, z1)
        return 0

    if steps > 2:
        lax.fori_loop(0, (steps - 1) // 2, two, 0)
    if steps % 2 == 0:
        put(z1, steps - 1)
        post(steps - 2, z0)
        post(steps - 1, z1)
    else:
        post(steps - 1, z0)


def conv_one_dot(sf, pf, m, w1t):
    one = around(sf, pf, m, 2, slice(0, 512))
    two = around(sf, pf, m, 2, slice(256, 768))
    return product(jnp.concatenate([one, two], axis=0), w1t[...])


def conv_one_post(z, scale, shift, keeps, xm, d1, at):
    for s in range(2):
        folds = []
        for p in range(4):
            rows = (p // 2) * 160 + s * 80
            half = z[rows : rows + 80, (p % 2) * 128 : (p % 2 + 1) * 128] * (0.5 * scale) + 0.5 * shift
            act, slope = silu_parts(half)
            d1[at + s, :, p * 128 : (p + 1) * 128] = (0.5 * scale) * slope
            folds.append(folded(rounded(act)))
        keep = 0.25 * keeps[s]
        xm[at + s, 0] = rounded((folds[0] + folds[1]) * keep)
        xm[at + s, 1] = rounded((folds[2] + folds[3]) * keep)


def own_kernel(
    grid_rows, grid_cols,
    noise_index, inputs, lef, rig, top, bot, w1t, rows_sc, cols_sc, noise,
    pf_out, sf_out, d1_out, xm_out, low_msg, high_msg,
    pf, sf, stage, held, d1, xm, mask, z0, z1, sems,
):
    fill_mask(grid_rows // 4, grid_cols // 4, mask)
    scale, shift = modulation(noise, noise_index)
    held[...] = jnp.zeros_like(held)

    def own(r):
        return flat(inputs[r]), rig[1 + r], lef[1 + r]

    def rim_row(ref, r):
        return flat(ref[r, 0:8]), ref[r, 8], ref[r, 9]

    def fill(load, q):
        first_lines(load, HALO - 2 + 4 * q, 2 * q, (rows_sc, cols_sc), stage, held, sf, pf)

    def first_step(q, _):
        fill(lambda i: own(4 * q - 2 + i), q)
        return 0

    fill(lambda i: rim_row(top, i) if i < 2 else own(i - 2), 0)
    lax.fori_loop(1, 12, first_step, 0)
    fill(lambda i: own(ROWS - 2 + i) if i < 2 else rim_row(bot, i - 2), 12)
    for j in range(6):
        sf[26, :, j * 128 : (j + 1) * 128] = stacked(held[j], jnp.zeros((KP, 128), F32)).astype(BF16)
    copies = [
        pltpu.make_async_copy(pf.at[pl.ds(1, 24), pl.ds(0, 64)], pf_out, sems.at[0]),
        pltpu.make_async_copy(sf.at[pl.ds(1, 25), pl.ds(0, 64)], sf_out, sems.at[1]),
    ]
    for copy in copies:
        copy.start()

    def post(t, z):
        low = [(7 + 2 * t) // 2, (8 + 2 * t) // 2]
        conv_one_post(z, scale, shift, [mask[low[0]], mask[low[1]]], xm, d1, 2 * t)
        part = pl.ds(2 * t, 2)
        pltpu.make_async_copy(d1.at[part], d1_out.at[part], sems.at[2]).start()

    pipeline(13, lambda t: conv_one_dot(sf, pf, 2 * t, w1t), post, z0, z1)
    last = pltpu.make_async_copy(xm.at[pl.ds(1, 24)], xm_out, sems.at[3])
    last.start()
    low_msg[...] = xm[1:8].astype(BF16)
    high_msg[...] = xm[18:25].astype(BF16)
    for copy in copies:
        copy.wait()
    pltpu.make_async_copy(d1, d1_out, sems.at[2]).wait()
    last.wait()


def own_rows(grid_rows, grid_cols, *args):
    def kernel(*refs):
        own_kernel(grid_rows, grid_cols, *refs)

    vm = pltpu.VMEM
    shape = jax.ShapeDtypeStruct
    return pl.pallas_call(
        kernel,
        out_shape=[
            shape((24, 64, 768), BF16),
            shape((25, 64, 768), BF16),
            shape((26, 80, 512), F32),
            shape((24, 2, KP, 128), F32),
            shape((7, 2, KP, 128), BF16),
            shape((7, 2, KP, 128), BF16),
        ],
        in_specs=[smem_spec()] + [vmem_spec()] * (len(args) - 1),
        out_specs=[any_spec()] * 4 + [vmem_spec()] * 2,
        scratch_shapes=[
            vm((26, 80, 768), BF16),
            vm((27, 80, 768), BF16),
            vm((4, 160, 128), F32),
            vm((6, KP, 128), F32),
            vm((26, 80, 512), F32),
            vm((26, 2, KP, 128), F32),
            vm((LOWS, KP, 128), F32),
            vm((320, 256), F32),
            vm((320, 256), F32),
            pltpu.SemaphoreType.DMA((4,)),
        ],
        compiler_params=pltpu.CompilerParams(vmem_limit_bytes=VMEM_LIMIT),
        cost_estimate=pl.CostEstimate(flops=4 * 10**9, bytes_accessed=30 * 10**6, transcendentals=0),
        name="own_rows",
    )(*args)


def lines_kernel(
    grid_rows, grid_cols,
    cot, top, bot, lef, rig, above, below,
    w2t_in, w2b_in, w3_in, w3b_in, pf_in, sf_in, d1_in, xm_in,
    coarse, g1p_out, g1s_out, keep_msg, give_msg,
    pf, sf, d1, xm, p2, s2, d2, xl, p3, s3, cp, side32, xg3, g3p, g3s, xb2, xg2, g2p, g2s, xt,
    g1p, g1s, held1, acc, acc3, gw, ms, mask, z0, z1, w2t, w2b, w3, w3b, sems,
):
    def fetch(source, target, at):
        copy = pltpu.make_async_copy(source, target, sems.at[at])
        copy.start()
        return copy

    got_xm = fetch(xm_in, xm.at[pl.ds(8, 24)], 2)
    got_w2t = fetch(w2t_in, w2t, 3)
    got_w3 = [fetch(w3_in, w3, 4), fetch(w3b_in, w3b, 5)]
    got_w2b = fetch(w2b_in, w2b, 6)
    got_d1 = fetch(d1_in, d1, 7)
    got_first = [fetch(pf_in, pf, 8), fetch(sf_in, sf, 9)]
    fill_mask(grid_rows // 4, grid_cols // 4, mask)
    xm[1:8] = above[...].astype(F32)
    xm[32:39] = below[...].astype(F32)

    def lines_four(x_ref, s_ref, p_ref, j, _):
        lines = []
        for i in range(3):
            zero, one = x_ref[2 * j - 1 + i, 0], x_ref[2 * j - 1 + i, 1]
            lines.append([before(one), zero, one, after(zero)])
        for n in range(4):
            lanes = slice(n * 128, (n + 1) * 128)
            s_ref[j, :, lanes] = stacked(lines[0][n], lines[1][n]).astype(BF16)
            p_ref[j, :, lanes] = stacked(lines[1][n], lines[2][n]).astype(BF16)
        return 0

    xm[39] = jnp.zeros((2, KP, 128), F32)
    got_xm.wait()
    lax.fori_loop(1, 20, lambda j, c: lines_four(xm, s2, p2, j, c), 0)
    got_w2t.wait()

    def conv_two_post(t, z):
        j = 1 + 3 * t
        for s in range(3):
            folds = []
            for q in range(2):
                half = 0.5 * z[s * 80 : (s + 1) * 80, q * 128 : (q + 1) * 128]
                act, slope = silu_parts(half)
                d2[j + s, :, q * 128 : (q + 1) * 128] = 0.5 * slope
                down = p2[j + s, :, (q + 1) * 128 : (q + 2) * 128].astype(F32)
                folds.append(folded(rounded(down + act)))
            xl[j + s] = rounded((folds[0] + folds[1]) * (0.25 * mask[j + s]))

    pipeline(
        6, lambda t: product(around(s2, p2, 1 + 3 * t, 3, slice(0, 512)), w2t[...]), conv_two_post, z0, z1
    )
    xl[19] = jnp.zeros((KP, 128), F32)

    def lines_three(x_ref, s_ref, p_ref, width, i, _):
        lines = []
        for n in range(3):
            line = x_ref[2 * i - 1 + n]
            lines.append([before(line), line, after(line)])
        for n in range(3):
            lanes = slice(n * width, (n + 1) * width)
            s_ref[i, :, lanes] = stacked(lines[0][n], lines[1][n]).astype(BF16)
            p_ref[i, :, lanes] = stacked(lines[1][n], lines[2][n]).astype(BF16)
        return 0

    lax.fori_loop(1, 10, lambda i, c: lines_three(xl, s3, p3, 128, i, c), 0)

    cp[...] = jnp.zeros_like(cp)
    for h in range(2):
        lanes = slice(h * 128, (h + 1) * 128)
        for r in range(2):
            units = pl.ds((r * 2 + h) * 2, 2)
            cp[r, 0:KO, lanes] = top[2, units].reshape(KO, 128).astype(F32)
            cp[14 + r, 0:KO, lanes] = bot[2, units].reshape(KO, 128).astype(F32)
    for r in range(12):
        cp[2 + r, 0:KO, :] = cot[r].astype(F32)
    for ref, at in ((rig, KO), (lef, KP - 2)):
        side32[...] = ref[pl.ds(ROWS + 1, 3)].reshape(48, 128).astype(F32)
        for h in range(2):
            for r in range(12):
                cp[2 + r, at : at + 2, h * 128 : (h + 1) * 128] = side32[r * 4 + h * 2 : r * 4 + h * 2 + 2]
    for ref, unit, skip, row, at in (
        (top, 9, 8, 0, KP - 2),
        (top, 8, 8, 0, KO),
        (bot, 9, 0, 14, KP - 2),
        (bot, 8, 0, 14, KO),
    ):
        side32[0:16] = ref[2, unit].astype(F32)
        for h in range(2):
            for r in range(2):
                start = skip + r * 4 + h * 2
                cp[row + r, at : at + 2, h * 128 : (h + 1) * 128] = side32[start : start + 2]
    for copy in got_w3:
        copy.wait()

    def conv_three_post(t, z):
        i = 1 + 2 * t
        for s in range(2):
            act, slope = silu_parts(0.5 * z[s * 80 : (s + 1) * 80, :])
            for r in range(2):
                row = 2 * (i + s) + r
                keep = 0.5 * mask[row]
                xg3[row] = cp[row - 2] * line_of(slope, r) * jnp.concatenate([keep, keep], axis=1)

                @pl.when((row >= 4) & (row < 16))
                def _():
                    coarse[row - 4] = act[32 * r : 32 * r + 32].astype(BF16)

    pipeline(
        4, lambda t: product(around(s3, p3, 1 + 2 * t, 2, slice(0, 384)), w3[...]), conv_three_post, z0, z1
    )
    empty = jnp.zeros((KP, 256), F32)
    xg3[1] = empty
    xg3[18] = empty
    xg3[19] = empty
    lax.fori_loop(1, 10, lambda i, c: lines_three(xg3, g3s, g3p, 256, i, c), 0)
    acc3[...] = weight_terms(
        g3p[2:8, 0:64, 256:512].reshape(384, 256), around(s3, p3, 2, 6, slice(0, 384), 0, 64)
    )
    total = product_turned(around(g3s, g3p, 1, 8, slice(0, 768)), w3b[...])
    for i in range(8):
        for r in range(2):
            xb2[2 * i + 2 + r] = 0.25 * line_of(total[i * 80 : (i + 1) * 80], r)

    def grad_two_step(j, _):
        slope = xb2[j] * mask[j]
        for s in range(2):
            for q in range(2):
                d = d2[j, :, q * 128 : (q + 1) * 128]
                xg2[2 * j + s, q] = slope * line_of(d, s)
        return 0

    lax.fori_loop(3, 17, grad_two_step, 0)
    blank = jnp.zeros((2, KP, 128), F32)
    xg2[5] = blank
    xg2[34] = blank
    xg2[35] = blank
    lax.fori_loop(3, 18, lambda j, c: lines_four(xg2, g2s, g2p, j, c), 0)
    got_w2b.wait()

    def fold_weights(at):
        for u in range(3):
            for v in range(3):
                left = (4 * u + v) * 128
                term = acc[0:128, left : left + 128] + acc[128:256, left + 128 : left + 256]
                gw[at, pl.ds((3 * u + v) * 128, 128), :] = term.T

    acc[...] = weight_terms(
        g2p[4:16, 0:64, 128:384].reshape(768, 256), around(s2, p2, 4, 12, slice(0, 512), 0, 64)
    )
    fold_weights(1)
    for tap in range(9):
        turned = acc3[:, tap * 128 : (tap + 1) * 128].T
        gw[2, pl.ds(tap * 128, 128), :] = turned[:, 0:128]
        gw[3, pl.ds(tap * 128, 128), :] = turned[:, 128:256]

    def back_two_post(t, z):
        j = 3 + 2 * t
        for s in range(2):
            keep = 0.25 * mask[j + s]
            base = xb2[j + s]
            for q in range(2):
                pair = z[s * 80 : (s + 1) * 80, q * 128 : (q + 1) * 128]
                for r in range(2):
                    xt[2 * (j + s) + r, q] = (base + line_of(pair, r)) * keep

    pipeline(
        7, lambda t: product_turned(around(g2s, g2p, 3 + 2 * t, 2, slice(0, 512)), w2b[...]), back_two_post, z0, z1
    )
    got_d1.wait()

    def grad_line(m, s):
        planes = [xt[m, p // 2] * line_of(d1[m - 7, :, p * 128 : (p + 1) * 128], s) for p in range(4)]
        lines = [before(planes[3])] + planes + [after(planes[0])]
        return [line[:KO] for line in lines]

    first_held = grad_line(7, 1)
    for n in range(6):
        held1[n] = first_held[n]

    def grad_one_step(at, _):
        m = at + 8
        even, odd = grad_line(m, 0), grad_line(m, 1)
        for n in range(6):
            lanes = slice(n * 128, (n + 1) * 128)
            g1s[at, :, lanes] = jnp.concatenate([held1[n], even[n]], axis=0).astype(BF16)
            g1p[at, :, lanes] = jnp.concatenate([even[n], odd[n]], axis=0).astype(BF16)
            held1[n] = odd[n]
        return 0

    lax.fori_loop(0, 25, grad_one_step, 0)
    copies = [
        pltpu.make_async_copy(g1p.at[pl.ds(0, 24)], g1p_out, sems.at[0]),
        pltpu.make_async_copy(g1s, g1s_out, sems.at[1]),
    ]
    for copy in copies:
        copy.start()
    for copy in got_first:
        copy.wait()
    acc[...] = jnp.zeros_like(acc)

    def weight_one_step(t, _):
        at = 8 * t
        grads = jnp.concatenate(
            [g1p[pl.ds(at, 8), :, lanes].reshape(512, 256) for lanes in (slice(128, 384), slice(384, 640))], axis=0
        )
        fields = jnp.concatenate(
            [around(sf, pf, at, 8, lanes, 0, 64) for lanes in (slice(0, 512), slice(256, 768))], axis=0
        )
        acc[...] += weight_terms(grads, fields)
        return 0

    lax.fori_loop(0, 3, weight_one_step, 0)
    fold_weights(0)
    for n in range(10):
        for t in range(4):
            piece = gw[t, pl.ds(n, 128, stride=9), :] if n < 9 else jnp.zeros((128, 128), F32)
            ms[pl.ds(4 * n + t, 128, stride=40), :] = piece
    core = lax.axis_index("core")

    def msg_step(n, _):
        rows = pl.ds(pl.multiple_of(n * 320, 320), 320)
        keep_msg[rows, :] = ms[pl.ds(pl.multiple_of((2 * n + core) * 320, 320), 320), :].astype(BF16)
        give_msg[rows, :] = ms[pl.ds(pl.multiple_of((2 * n + 1 - core) * 320, 320), 320), :].astype(BF16)
        return 0

    lax.fori_loop(0, 8, msg_step, 0)
    for copy in copies:
        copy.wait()


def levels(grid_rows, grid_cols, *args):
    def kernel(*refs):
        lines_kernel(grid_rows, grid_cols, *refs)

    vm = pltpu.VMEM
    return pl.pallas_call(
        kernel,
        out_shape=[
            jax.ShapeDtypeStruct((12, KO, 256), BF16),
            jax.ShapeDtypeStruct((24, 64, 768), BF16),
            jax.ShapeDtypeStruct((25, 64, 768), BF16),
            jax.ShapeDtypeStruct((2560, 128), BF16),
            jax.ShapeDtypeStruct((2560, 128), BF16),
        ],
        in_specs=[vmem_spec()] * 7 + [any_spec()] * 8,
        out_specs=[vmem_spec(), any_spec(), any_spec(), vmem_spec(), vmem_spec()],
        scratch_shapes=[
            vm((24, 64, 768), BF16),
            vm((25, 64, 768), BF16),
            vm((26, 80, 512), F32),
            vm((PAIRS, 2, KP, 128), F32),
            vm((LOWS, 80, 512), BF16),
            vm((LOWS, 80, 512), BF16),
            vm((LOWS, 80, 256), F32),
            vm((LOWS, KP, 128), F32),
            vm((10, 80, 384), BF16),
            vm((10, 80, 384), BF16),
            vm((16, KP, 256), F32),
            vm((48, 128), F32),
            vm((LOWS, KP, 256), F32),
            vm((10, 80, 768), BF16),
            vm((10, 80, 768), BF16),
            vm((LOWS, KP, 128), F32),
            vm((PAIRS, 2, KP, 128), F32),
            vm((LOWS, 80, 512), BF16),
            vm((LOWS, 80, 512), BF16),
            vm((PAIRS, 2, KP, 128), F32),
            vm((25, 64, 768), BF16),
            vm((25, 64, 768), BF16),
            vm((6, KO, 128), F32),
            vm((256, 1536), F32),
            vm((256, 1152), F32),
            vm((4, 1152, 128), F32),
            vm((5120, 128), F32),
            vm((LOWS, KP, 128), F32),
            vm((320, 256), F32),
            vm((320, 256), F32),
            vm((1536, 256), BF16),
            vm((256, 1536), BF16),
            vm((1152, 256), BF16),
            vm((128, 2304), BF16),
            pltpu.SemaphoreType.DMA((10,)),
        ],
        compiler_params=pltpu.CompilerParams(vmem_limit_bytes=VMEM_LIMIT),
        name="encoder_levels",
    )(*args)


def input_kernel(g1p, g1s, g1s_next, w1b, out, stage):
    for t in range(2):
        halves = []
        for lanes in (slice(0, 512), slice(256, 768)):
            after_last = g1s[3:4, :, lanes] if t == 0 else g1s_next[:, :, lanes]
            parts = [
                g1s[2 * t : 2 * t + 2, :, lanes],
                g1p[2 * t : 2 * t + 2, :, lanes],
                g1s[1:3, :, lanes] if t == 0 else jnp.concatenate([g1s[3:4, :, lanes], after_last], axis=0),
            ]
            halves.append(jnp.concatenate([part.reshape(128, 512) for part in parts], axis=1))
        total = product_turned(jnp.concatenate(halves, axis=0), w1b[...])
        for r in range(4):
            for p in range(4):
                rows = (p // 2) * 128 + r * 32
                value = total[rows : rows + 32, (p % 2) * 128 : (p % 2 + 1) * 128]
                stage[4 * t + r, pl.ds(p, 32, stride=4), :] = value
            out[4 * t + r] = stage[4 * t + r].astype(BF16)


def input_grad(g1p, g1s, w1b):
    return pl.pallas_call(
        input_kernel,
        grid=(6,),
        out_shape=jax.ShapeDtypeStruct((ROWS, 128, 128), BF16),
        in_specs=[
            pl.BlockSpec((4, 64, 768), lambda i: (i, 0, 0)),
            pl.BlockSpec((4, 64, 768), lambda i: (i, 0, 0)),
            pl.BlockSpec((1, 64, 768), lambda i: (4 * i + 4, 0, 0)),
            pl.BlockSpec((256, 1536), lambda i: (0, 0)),
        ],
        out_specs=pl.BlockSpec((8, 128, 128), lambda i: (i, 0, 0)),
        scratch_shapes=[pltpu.VMEM((8, 128, 128), F32)],
        compiler_params=pltpu.CompilerParams(vmem_limit_bytes=VMEM_LIMIT),
        cost_estimate=pl.CostEstimate(flops=2 * 6144 * 1152 * 128, bytes_accessed=8 * 1024 * 1024, transcendentals=0),
        name="input_grad",
    )(g1p, g1s, g1s, w1b)


def add_kernel(keep, other, out):
    out[...] = (keep[...].astype(F32) + other[...].astype(F32)).astype(BF16)


def add(keep, other):
    return pl.pallas_call(
        add_kernel,
        out_shape=jax.ShapeDtypeStruct(keep.shape, BF16),
        in_specs=[vmem_spec()] * 2,
        out_specs=vmem_spec(),
        name="add_core_terms",
    )(keep, other)


def collect(got):
    sums = got.astype(F32).sum(axis=0)[0:36].reshape(9, 4, 128)
    return sums[:, 0], sums[:, 1], jnp.concatenate([sums[:, 2], sums[:, 3]], axis=1)


def shifted(block, axis, step):
    devices = lax.axis_size(axis)
    pairs = [(i, i + step) for i in range(devices) if 0 <= i + step < devices]
    return lax.ppermute(block, axis, pairs)


def body(inputs, weight_one, weight_two, weight_three, noise_table, frequency, anchor, noise_index, cotangent):
    grid = (lax.axis_size(ROW_AXES) * ROWS, lax.axis_size("tx") * 4 * KO)
    inputs = inputs.reshape(ROWS, 8, 16, 128)
    right, left, cots = sides(inputs, cotangent)
    lef = shifted(right, "tx", 1)
    rig = shifted(left, "tx", -1)
    w1t, w1b, w2t, w2b, w3b, rows_sc, cols_sc = prep(*grid, anchor, weight_one, weight_two, weight_three, frequency)
    lef, rig, rows_sc = lax.optimization_barrier((lef, rig, rows_sc))
    top = shifted(rim(inputs, cots[0], lef, rig, ROWS - 2, 3 + ROWS), ROW_AXES, 1)
    bot = shifted(rim(inputs, cots[1], lef, rig, 0, 0), ROW_AXES, -1)
    pf, sf, d1, xm, low_msg, high_msg = own_rows(
        *grid, noise_index, inputs, lef, rig, top, bot, w1t, rows_sc, cols_sc, noise_table
    )
    above = shifted(high_msg, ROW_AXES, 1)
    below = shifted(low_msg, ROW_AXES, -1)
    coarse, g1p, g1s, keep_msg, give_msg = levels(
        *grid, cotangent, top, bot, lef, rig, above, below, w2t, w2b, weight_three, w3b, pf, sf, d1, xm
    )
    other = lax.ppermute(give_msg, "core", [(0, 1), (1, 0)])
    msg = add(keep_msg, other).reshape(64, 40, 128)
    got = lax.all_to_all(msg, ("chip", "tx"), 0, 0, tiled=True)
    grad_inputs = input_grad(g1p, g1s, w1b)
    return (coarse, grad_inputs, *collect(got))


def solution(mesh):
    halves = jax.sharding.Mesh(mesh.devices.reshape(-1, 2, mesh.devices.shape[1]), ("chip", "core", "tx"))
    placed = (P(ROW_AXES, "tx", None), P(), P(), P(), P(), P(), P(), P(), P(ROW_AXES, "tx", None))
    return jax.shard_map(
        body,
        mesh=halves,
        in_specs=placed,
        out_specs=(
            P(ROW_AXES, "tx", None),
            P(ROW_AXES, "tx", None),
            P((*ROW_AXES, "tx"), None),
            P((*ROW_AXES, "tx"), None),
            P((*ROW_AXES, "tx"), None),
        ),
        check_vma=False,
    )
```

time: 96.6 us -> 108 us (1.12)
  starting transfers between devices: 29.6 us -> 36.1 us
  waiting for transfers between devices: 13.3 us -> 17.5 us
  other arithmetic: 2.73 us -> 0.79 us
  Pallas kernels: 44.8 us -> 46.4 us
    pallas_call x4 -> x5, Pallas kernels: 14 us -> 27.1 us  [the longest x1 11.3 us: own_rows(): pl.pallas_call(kernel, out_shape=[shape((24, 64, 768), BF16), shape((25,...]
    pallas_call x1, Pallas kernels: 30.8 us -> 19.3 us  [levels(): pl.pallas_call(kernel, out_shape=[jax.ShapeDtypeStruct((12, KO, 256), BF1...]
    ppermute x6, starting transfers between devices: 10.2 us -> 14 us  [shifted(): return lax.ppermute(block, axis, pairs)]
    ppermute x6, waiting for transfers between devices: 4.5 us -> 7.62 us  [shifted(): return lax.ppermute(block, axis, pairs)]
    all_to_all x1, starting transfers between devices: 16.5 us -> 18.9 us  [body(): got = lax.all_to_all(msg, ('chip', 'tx'), 0, 0, tiled=True)]
    convert_element_type x1 -> x0, other arithmetic: 2.11 us -> none  [body(): (keep_msg.astype(F32) + other.astype(F32)).astype(BF16).reshape(64, 40, 128)]
    all_to_all x1, waiting for transfers between devices: 6.82 us -> 7.95 us  [body(): got = lax.all_to_all(msg, ('chip', 'tx'), 0, 0, tiled=True)]
    unnamed x20 -> x18, local copies, waits for them, and re-layouts: 4.22 us -> 3.34 us
  transfers between devices with their start and end apart: 8 -> 8, of which waited for: 4 -> 5; matrix products, arithmetic and copies ran while one was open for 1% -> 2% of each run, Pallas kernels for 13% -> 10%
where the time goes in v1:
time: 108 us; the launch traced here: 107 us
  Pallas kernels  46.4 us (43%)
  starting transfers between devices  36.1 us (33%)
  waiting for transfers between devices  17.5 us (16%)
  local copies, waits for them, and re-layouts  5.03 us (5%)
  between operations  1.48 us (1%)
    pallas_call x1, Pallas kernels, levels(): pl.pallas_call(kernel, out_shape=[jax.ShapeDtypeStruct((12, KO, 256), BF1...  19.3 us
    all_to_all x1, starting transfers between devices, body(): got = lax.all_to_all(msg, ('chip', 'tx'), 0, 0, tiled=True)  18.9 us
    ppermute x6, starting transfers between devices, shifted(): return lax.ppermute(block, axis, pairs)  14 us
    pallas_call x1, Pallas kernels, own_rows(): pl.pallas_call(kernel, out_shape=[shape((24, 64, 768), BF16), shape((25,...  11.3 us
    all_to_all x1, waiting for transfers between devices, body(): got = lax.all_to_all(msg, ('chip', 'tx'), 0, 0, tiled=True)  7.95 us
    ppermute x6, waiting for transfers between devices, shifted(): return lax.ppermute(block, axis, pairs)  7.62 us
    pallas_call x1, Pallas kernels, input_grad(): pl.pallas_call(input_kernel, grid=(6,), out_shape=jax.ShapeDtypeStruct((R...  7.32 us
    pallas_call x1, Pallas kernels, prep(): pl.pallas_call(kernel, out_shape=[shape((1536, 256), BF16), shape((256, 1...  3.44 us
  transfers between devices with their start and end apart: 8, of which 5 were waited for; matrix products, arithmetic and copies ran while one was open for 2% of the time, Pallas kernels for 10%

profile of v1, /device:TPU:0, one launch (start us, length us, event | category | flops | bytes accessed | tf_op | source)
XLA Modules:
  0.0 107.3 jit_solution(11893166031028989891)
XLA Ops:
  0.6 2.7 %pack_columns.1 = (bf16[52,16,128]{2,1,0:T(8,128)(2,1)}, bf16[52,16,128]{2,1,0:T(8,128)(2,1)}, bf16[2,8,16,128]{3,2,1,0:T(8,128)(2,1)}) custom-call(bf16[48,8,16,128]{3,2,1,0:T(8,128)(2,1)} %bitcast.42, bf16[12,32,256]{2,1,0:T(8,128)(2,1)} %refs_0_.4), custom_call_target="tpu_custom_call" | custom-call | tf_op jit(solution)/shard_map/pack_columns/pallas_call | solution.py:64
  3.4 3.5 %collective-permute-start = (bf16[52,16,128]{2,1,0:T(8,128)(2,1)}, bf16[52,16,128]{2,1,0:T(8,128)(2,1)S(1)}, u32[]{:S(2)}, u32[]{:S(2)}) collective-permute-start(bf16[52,16,128]{2,1,0:T(8,128)(2,1)} %get-tuple-element.29), channel_id=1, source_target_pairs={{0,1},{1,2},{2,3},{3,4},{4,5},{5,6},{6,7},{8,9},{9,10},{10,11},{11... | collective-permute-start | bytes 638984 | tf_op jit(solution)/shard_map/ppermute | solution.py:734
  6.9 1.3 %collective-permute-start.1 = (bf16[52,16,128]{2,1,0:T(8,128)(2,1)}, bf16[52,16,128]{2,1,0:T(8,128)(2,1)S(1)}, u32[]{:S(2)}, u32[]{:S(2)}) collective-permute-start(bf16[52,16,128]{2,1,0:T(8,128)(2,1)} %get-tuple-element.30), channel_id=1, source_target_pairs={{1,0},{2,1},{3,2},{4,3},{5,4},{6,5},{7,6},{9,8},{10,9},{11,10},{12... | collective-permute-start | bytes 638984 | tf_op jit(solution)/shard_map/ppermute | solution.py:734
  8.2 0.9 fusion
  9.1 3.4 %weight_forms.1 = (bf16[1536,256]{1,0:T(8,128)(2,1)}, bf16[256,1536]{1,0:T(8,128)(2,1)}, bf16[1536,256]{1,0:T(8,128)(2,1)}, bf16[256,1536]{1,0:T(8,128)(2,1)}, b...) custom-call(s32[2]{0:T(128)} %refs_0_.3, bf16[1152,128]{1,0:T(8,128)(2,1)} %refs_1_.1, ...), custom_call_target="tpu_custom_call" | custom-call | tf_op jit(solution)/shard_map/weight_forms/pallas_call | solution.py:129
  12.5 0.8 slice_bitcast_fusion
  13.3 0.0 collective-permute-done.refs_2_.refs_3_
  13.3 2.4 %collective-permute-done.1.refs_3_.refs_4_ = bf16[52,16,128]{2,1,0:T(8,128)(2,1)S(1)} collective-permute-done((bf16[52,16,128]{2,1,0:T(8,128)(2,1)}, bf16[52,16,128]{2,1,0:T(8,128)(2,1)S(1)}, u32[]{:S(2)}, u32[]{:S(2)}) %collective-permute-start.1) | collective-permute-done | bytes 213024 | tf_op jit(solution)/shard_map/ppermute | solution.py:734
  15.7 1.3 %collective-permute-start.2 = (bf16[3,10,16,128]{3,2,1,0:T(8,128)(2,1)S(1)}, bf16[3,10,16,128]{3,2,1,0:T(8,128)(2,1)S(1)}, u32[]{:S(2)}, u32[]{:S(2)}) collective-permute-start(bf16[3,10,16,128]{3,2,1,0:T(8,128)(2,1)S(1)} %pad_maximum_fusion), channel_id=1, source_target_pairs={{0,8},{8,16},{16,24},{24,32},{32,40},{40,48},{48,56},{56,64},{64,7... | collective-permute-start | bytes 368648 | tf_op jit(solution)/shard_map/ppermute | solution.py:734
  17.1 1.3 %collective-permute-start.3 = (bf16[3,10,16,128]{3,2,1,0:T(8,128)(2,1)S(1)}, bf16[3,10,16,128]{3,2,1,0:T(8,128)(2,1)S(1)}, u32[]{:S(2)}, u32[]{:S(2)}) collective-permute-start(bf16[3,10,16,128]{3,2,1,0:T(8,128)(2,1)S(1)} %pad_maximum_fusion.1), channel_id=1, source_target_pairs={{8,0},{16,8},{24,16},{32,24},{40,32},{48,40},{56,48},{64,56},{72,6... | collective-permute-start | bytes 368648 | tf_op jit(solution)/shard_map/ppermute | solution.py:734
  19.0 0.0 collective-permute-done.2.refs_4_.refs_1_
  19.1 3.1 %collective-permute-done.3.refs_5_.refs_2_ = bf16[3,10,16,128]{3,2,1,0:T(8,128)(2,1)S(1)} collective-permute-done((bf16[3,10,16,128]{3,2,1,0:T(8,128)(2,1)S(1)}, bf16[3,10,16,128]{3,2,1,0:T(8,128)(2,1)S(1)}, u32[]{:S(2)}, u32[]{:S(2)}) %collective-permute-start.3) | collective-permute-done | bytes 122912 | tf_op jit(solution)/shard_map/ppermute | solution.py:734
  22.1 0.0 copy-done.1
  22.1 0.6 copy-done.6
  22.8 11.3 %own_rows.1 = (bf16[24,64,768]{2,1,0:T(8,128)(2,1)}, bf16[25,64,768]{2,1,0:T(8,128)(2,1)}, f32[26,80,512]{2,1,0:T(8,128)}, f32[24,2,40,128]{3,2,1,0:T(8,128)}, b...) custom-call(s32[1]{0:T(128)S(6)} %copy.35.refs_0_, bf16[48,8,16,128]{3,2,1,0:T(8,128)(2,1)} %bitcast.43, ...), custom_call_target="tpu_custom_call" | custom-call | flops 4000000000 | bytes 30000000 | tf_op jit(solution)/shard_map/own_rows/pallas_call | solution.py:352
  34.1 5.4 %collective-permute-start.4 = (bf16[7,2,40,128]{3,2,1,0:T(8,128)(2,1)}, bf16[7,2,40,128]{3,2,1,0:T(8,128)(2,1)S(1)}, u32[]{:S(2)}, u32[]{:S(2)}) collective-permute-start(bf16[7,2,40,128]{3,2,1,0:T(8,128)(2,1)} %get-tuple-element.38), channel_id=1, source_target_pairs={{0,8},{8,16},{16,24},{24,32},{32,40},{40,48},{48,56},{56,64},{64,7... | collective-permute-start | bytes 430088 | tf_op jit(solution)/shard_map/ppermute | solution.py:734
  39.5 1.3 %collective-permute-start.5 = (bf16[7,2,40,128]{3,2,1,0:T(8,128)(2,1)}, bf16[7,2,40,128]{3,2,1,0:T(8,128)(2,1)S(1)}, u32[]{:S(2)}, u32[]{:S(2)}) collective-permute-start(bf16[7,2,40,128]{3,2,1,0:T(8,128)(2,1)} %get-tuple-element.39), channel_id=1, source_target_pairs={{8,0},{16,8},{24,16},{32,24},{40,32},{48,40},{56,48},{64,56},{72,6... | collective-permute-start | bytes 430088 | tf_op jit(solution)/shard_map/ppermute | solution.py:734
  40.8 0.0 collective-permute-done.4.refs_5_
  40.8 2.1 %collective-permute-done.5.refs_6_ = bf16[7,2,40,128]{3,2,1,0:T(8,128)(2,1)S(1)} collective-permute-done((bf16[7,2,40,128]{3,2,1,0:T(8,128)(2,1)}, bf16[7,2,40,128]{3,2,1,0:T(8,128)(2,1)S(1)}, u32[]{:S(2)}, u32[]{:S(2)}) %collective-permute-start.5) | collective-permute-done | bytes 143392 | tf_op jit(solution)/shard_map/ppermute | solution.py:734
  42.9 0.6 copy-done.4
  43.6 19.3 %encoder_levels.1 = (bf16[12,32,256]{2,1,0:T(8,128)(2,1)}, bf16[24,64,768]{2,1,0:T(8,128)(2,1)}, bf16[25,64,768]{2,1,0:T(8,128)(2,1)}, bf16[2560,128]{1,0:T(8,128)(2,1)}, bf16[2560,128]{1,0:T(8,128)(2,1)}) custom-call(bf16[12,32,256]{2,1,0:T(8,128)(2,1)} %refs_0_.4, bf16[3,10,16,128]{3,2,1,0:T(8,128)(2,1)} %copy-done.5, bf16[3,10,16,128]{3,2,1,0:T(8,128)(2,1)} %copy-done.6, ...), custom_call_target="tpu_custom_call" | custom-call | tf_op jit(solution)/shard_map/encoder_levels/pallas_call | solution.py:620
  62.9 3.2 %collective-permute-start.6 = (bf16[2560,128]{1,0:T(8,128)(2,1)}, bf16[2560,128]{1,0:T(8,128)(2,1)S(1)}, u32[]{:S(2)}, u32[]{:S(2)}) collective-permute-start(bf16[2560,128]{1,0:T(8,128)(2,1)} %get-tuple-element.52), channel_id=1, source_target_pairs={{0,8},{8,0},{1,9},{9,1},{2,10},{10,2},{3,11},{11,3},{4,12},{12,4},... | collective-permute-start | bytes 1966088 | tf_op jit(solution)/shard_map/ppermute | solution.py:755
  66.1 1.9 %collective-permute-done.6.other = bf16[2560,128]{1,0:T(8,128)(2,1)S(1)} collective-permute-done((bf16[2560,128]{1,0:T(8,128)(2,1)}, bf16[2560,128]{1,0:T(8,128)(2,1)S(1)}, u32[]{:S(2)}, u32[]{:S(2)}) %collective-permute-start.6) | collective-permute-done | bytes 655392 | tf_op jit(solution)/shard_map/ppermute | solution.py:755
  68.1 0.8 copy-done
  68.9 2.3 %add_core_terms.1 = bf16[2560,128]{1,0:T(8,128)(2,1)} custom-call(bf16[2560,128]{1,0:T(8,128)(2,1)} %get-tuple-element.51.keep, bf16[2560,128]{1,0:T(8,128)(2,1)} %copy-done), custom_call_target="tpu_custom_call" | custom-call | tf_op jit(solution)/shard_map/add_core_terms/pallas_call | solution.py:717
  71.2 18.9 %all-to-all-start = ((bf16[64,40,128]{2,1,0:T(8,128)(2,1)}), bf16[64,40,128]{2,1,0:T(8,128)(2,1)S(1)}, u32[]{:S(2)}, u32[]{:S(2)}) async-start(bf16[64,40,128]{2,1,0:T(8,128)(2,1)} %bitcast.41), calls=%async_computation | async-start | bytes 1310720 | tf_op jit(solution)/shard_map/all_to_all | solution.py:757
  90.1 7.3 %input_grad.1 = bf16[48,128,128]{2,1,0:T(8,128)(2,1)} custom-call(bf16[24,64,768]{2,1,0:T(8,128)(2,1)} %get-tuple-element.48.g1p, bf16[25,64,768]{2,1,0:T(8,128)(2,1)} %get-tuple-element.49.g1s.g1s_next, bf16[25,64,768]{2,1,0:T(8,128)(2,1)} %get-tuple-element.49.g1s.g1s_next, bf16[256,1536]{1,0:T(8,128)(2,1)} %get-tuple-element.50.w1b), custom_call_target="tpu_custom_call" | custom-call | flops 1811939328 | bytes 8388608 | tf_op jit(solution)/shard_map/input_grad/pallas_call | solution.py:694
  97.4 7.9 %all-to-all-done = bf16[64,40,128]{2,1,0:T(8,128)(2,1)S(1)} async-done(((bf16[64,40,128]{2,1,0:T(8,128)(2,1)}), bf16[64,40,128]{2,1,0:T(8,128)(2,1)S(1)}, u32[]{:S(2)}, u32[]{:S(2)}) %all-to-all-start) | async-done | bytes 655392 | tf_op jit(solution)/shard_map/all_to_all | solution.py:757
  105.3 0.1 convert_reduce_fusion
  105.5 0.6 copy.33
  106.1 0.6 copy.34
  106.7 0.6 pad_maximum_fusion.2
  (20 shorter events, 0.1 us)
Async XLA Ops:
  3.4 9.9 %collective-permute-start = (bf16[52,16,128]{2,1,0:T(8,128)(2,1)}, bf16[52,16,128]{2,1,0:T(8,128)(2,1)S(1)}, u32[]{:S(2)}, u32[]{:S(2)}) collective-permute-start(bf16[52,16,128]{2,1,0:T(8,128)(2,1)} %get-tuple-element.29), channel_id=1, source_target_pairs={{0,1},{1,2},{2,3},{3,4},{4,5},{5,6},{6,7},{8,9},{9,10},{10,11},{11... | collective-permute-start | bytes 638984 | tf_op jit(solution)/shard_map/ppermute | solution.py:734
  6.9 8.8 %collective-permute-start.1 = (bf16[52,16,128]{2,1,0:T(8,128)(2,1)}, bf16[52,16,128]{2,1,0:T(8,128)(2,1)S(1)}, u32[]{:S(2)}, u32[]{:S(2)}) collective-permute-start(bf16[52,16,128]{2,1,0:T(8,128)(2,1)} %get-tuple-element.30), channel_id=1, source_target_pairs={{1,0},{2,1},{3,2},{4,3},{5,4},{6,5},{7,6},{9,8},{10,9},{11,10},{12... | collective-permute-start | bytes 638984 | tf_op jit(solution)/shard_map/ppermute | solution.py:734
  13.3 8.8 %copy-start.1 = (bf16[52,16,128]{2,1,0:T(8,128)(2,1)}, bf16[52,16,128]{2,1,0:T(8,128)(2,1)S(1)}, u32[]{:S(2)}) copy-start(bf16[52,16,128]{2,1,0:T(8,128)(2,1)S(1)} %collective-permute-done.refs_2_.refs_3_) | copy-start | bytes 638980
  15.7 6.4 %copy-start.2 = (bf16[52,16,128]{2,1,0:T(8,128)(2,1)}, bf16[52,16,128]{2,1,0:T(8,128)(2,1)S(1)}, u32[]{:S(2)}) copy-start(bf16[52,16,128]{2,1,0:T(8,128)(2,1)S(1)} %collective-permute-done.1.refs_3_.refs_4_) | copy-start | bytes 638980
  15.7 3.3 %collective-permute-start.2 = (bf16[3,10,16,128]{3,2,1,0:T(8,128)(2,1)S(1)}, bf16[3,10,16,128]{3,2,1,0:T(8,128)(2,1)S(1)}, u32[]{:S(2)}, u32[]{:S(2)}) collective-permute-start(bf16[3,10,16,128]{3,2,1,0:T(8,128)(2,1)S(1)} %pad_maximum_fusion), channel_id=1, source_target_pairs={{0,8},{8,16},{16,24},{24,32},{32,40},{40,48},{48,56},{56,64},{64,7... | collective-permute-start | bytes 368648 | tf_op jit(solution)/shard_map/ppermute | solution.py:734
  17.1 5.0 %collective-permute-start.3 = (bf16[3,10,16,128]{3,2,1,0:T(8,128)(2,1)S(1)}, bf16[3,10,16,128]{3,2,1,0:T(8,128)(2,1)S(1)}, u32[]{:S(2)}, u32[]{:S(2)}) collective-permute-start(bf16[3,10,16,128]{3,2,1,0:T(8,128)(2,1)S(1)} %pad_maximum_fusion.1), channel_id=1, source_target_pairs={{8,0},{16,8},{24,16},{32,24},{40,32},{48,40},{56,48},{64,56},{72,6... | collective-permute-start | bytes 368648 | tf_op jit(solution)/shard_map/ppermute | solution.py:734
  19.0 3.1 %copy-start.5 = (bf16[3,10,16,128]{3,2,1,0:T(8,128)(2,1)}, bf16[3,10,16,128]{3,2,1,0:T(8,128)(2,1)S(1)}, u32[]{:S(2)}) copy-start(bf16[3,10,16,128]{3,2,1,0:T(8,128)(2,1)S(1)} %collective-permute-done.2.refs_4_.refs_1_) | copy-start | bytes 368644
  22.1 0.6 copy-start.6
  34.1 6.7 %collective-permute-start.4 = (bf16[7,2,40,128]{3,2,1,0:T(8,128)(2,1)}, bf16[7,2,40,128]{3,2,1,0:T(8,128)(2,1)S(1)}, u32[]{:S(2)}, u32[]{:S(2)}) collective-permute-start(bf16[7,2,40,128]{3,2,1,0:T(8,128)(2,1)} %get-tuple-element.38), channel_id=1, source_target_pairs={{0,8},{8,16},{16,24},{24,32},{32,40},{40,48},{48,56},{56,64},{64,7... | collective-permute-start | bytes 430088 | tf_op jit(solution)/shard_map/ppermute | solution.py:734
  39.5 3.5 %collective-permute-start.5 = (bf16[7,2,40,128]{3,2,1,0:T(8,128)(2,1)}, bf16[7,2,40,128]{3,2,1,0:T(8,128)(2,1)S(1)}, u32[]{:S(2)}, u32[]{:S(2)}) collective-permute-start(bf16[7,2,40,128]{3,2,1,0:T(8,128)(2,1)} %get-tuple-element.39), channel_id=1, source_target_pairs={{8,0},{16,8},{24,16},{32,24},{40,32},{48,40},{56,48},{64,56},{72,6... | collective-permute-start | bytes 430088 | tf_op jit(solution)/shard_map/ppermute | solution.py:734
  40.8 2.2 %copy-start.3 = (bf16[7,2,40,128]{3,2,1,0:T(8,128)(2,1)}, bf16[7,2,40,128]{3,2,1,0:T(8,128)(2,1)S(1)}, u32[]{:S(2)}) copy-start(bf16[7,2,40,128]{3,2,1,0:T(8,128)(2,1)S(1)} %collective-permute-done.4.refs_5_) | copy-start | bytes 430084
  42.9 0.7 copy-start.4
  62.9 5.2 %collective-permute-start.6 = (bf16[2560,128]{1,0:T(8,128)(2,1)}, bf16[2560,128]{1,0:T(8,128)(2,1)S(1)}, u32[]{:S(2)}, u32[]{:S(2)}) collective-permute-start(bf16[2560,128]{1,0:T(8,128)(2,1)} %get-tuple-element.52), channel_id=1, source_target_pairs={{0,8},{8,0},{1,9},{9,1},{2,10},{10,2},{3,11},{11,3},{4,12},{12,4},... | collective-permute-start | bytes 1966088 | tf_op jit(solution)/shard_map/ppermute | solution.py:755
  68.1 0.8 copy-start
  71.2 34.1 %all-to-all-start = ((bf16[64,40,128]{2,1,0:T(8,128)(2,1)}), bf16[64,40,128]{2,1,0:T(8,128)(2,1)S(1)}, u32[]{:S(2)}, u32[]{:S(2)}) async-start(bf16[64,40,128]{2,1,0:T(8,128)(2,1)} %bitcast.41), calls=%async_computation | async-start | bytes 1310720 | tf_op jit(solution)/shard_map/all_to_all | solution.py:757

commit v2 on v1

v2 whole, which is shorter than its diff:
```python
import jax
import jax.numpy as jnp
from jax import lax
from jax.experimental import pallas as pl
from jax.experimental.pallas import tpu as pltpu
from jax.sharding import PartitionSpec as P

BF16 = jnp.bfloat16
F32 = jnp.float32

KO = 32
KP = 40
KW = 48
HALO = 16
ROWS = 48
PAD_ROWS = ROWS + 2 * HALO
PAIRS = PAD_ROWS // 2
LOWS = PAIRS // 2
VMEM_LIMIT = 60 * 1024 * 1024


def any_spec():
    return pl.BlockSpec(memory_space=pl.ANY)


def vmem_spec():
    return pl.BlockSpec(memory_space=pltpu.VMEM)


def smem_spec():
    return pl.BlockSpec(memory_space=pltpu.SMEM)


ROW_AXES = ("chip", "core")


def own_place():
    return lax.axis_index(ROW_AXES), lax.axis_index("tx")


def odd_column():
    return lax.rem(lax.axis_index("tx"), 2)


def side_kernel(inputs, cot, one, two, cots, side32, sems):
    odd = odd_column()
    copies = [
        pltpu.make_async_copy(inputs.at[:, 7 - 7 * odd], one.at[pl.ds(1, ROWS)], sems.at[0]),
        pltpu.make_async_copy(inputs.at[:, 7 * odd], two.at[pl.ds(1, ROWS)], sems.at[1]),
    ]
    for copy in copies:
        copy.start()
    for target, at_left in ((one, odd == 1), (two, odd == 0)):
        for r in range(12):
            line = cot[r].astype(F32)
            for h in range(2):
                lanes = slice(h * 128, (h + 1) * 128)
                side32[pl.ds(r * 4 + h * 2, 2)] = jnp.where(at_left, line[0:2, lanes], line[30:32, lanes])
        side = side32[...].astype(BF16).reshape(3, 16, 128)
        target[pl.ds(0, 1)] = side[0:1]
        target[pl.ds(1 + ROWS, 3)] = side
    for at, start in ((0, 10), (1, 0)):
        for r in range(2):
            for h in range(2):
                cots[at, pl.ds((r * 2 + h) * 2, 2)] = cot[start + r, :, h * 128 : (h + 1) * 128].reshape(2, 16, 128)
    for copy in copies:
        copy.wait()


def sides(inputs, cot):
    return pl.pallas_call(
        side_kernel,
        out_shape=[jax.ShapeDtypeStruct((ROWS + 4, 16, 128), BF16)] * 2 + [jax.ShapeDtypeStruct((2, 8, 16, 128), BF16)],
        in_specs=[any_spec(), vmem_spec()],
        out_specs=[vmem_spec()] * 3,
        scratch_shapes=[pltpu.VMEM((48, 128), F32), pltpu.SemaphoreType.DMA((2,))],
        name="pack_columns",
    )(inputs, cot)


def rim_kernel(inputs, cots, one, two, _, off, near, sems):
    core = lax.axis_index("core")
    copies = []

    def fetch(source, target):
        copy = pltpu.make_async_copy(source, target, sems.at[len(copies)])
        copy.start()
        copies.append(copy)

    body = pl.ds(0, HALO)
    for target, low in ((off, core), (near, 1 - core)):
        row = (ROWS - HALO) * low
        fetch(inputs.at[pl.ds(row, HALO)], target.at[body, pl.ds(0, 8)])
        fetch(cots.at[1 - low], target.at[HALO, pl.ds(0, 8)])
        for unit, side in ((8, one), (9, two)):
            fetch(side.at[pl.ds(1 + row, HALO)], target.at[body, unit])
            fetch(side.at[(3 + ROWS) * low], target.at[HALO, unit])
    for copy in copies:
        copy.wait()


def rims(*args):
    return pl.pallas_call(
        rim_kernel,
        out_shape=[jax.ShapeDtypeStruct((HALO + 1, 10, 16, 128), BF16)] * 2,
        in_specs=[any_spec()] * len(args),
        out_specs=[vmem_spec()] * 2,
        scratch_shapes=[pltpu.SemaphoreType.DMA((12,))],
        name="pack_rows",
    )(*args)


def weight_forms(w1, w2, w3, w1t, w1b, w2t, w2b, w3b):
    zero = jnp.zeros((128, 128), BF16)
    for source, ahead, back in ((w1, w1t, w1b), (w2, w2t, w2b)):
        for u in range(3):
            for v in range(3):
                tap = source[pl.ds((3 * u + v) * 128, 128), :]
                for i in range(2):
                    side = slice(i * 128, (i + 1) * 128)
                    ahead[pl.ds((4 * u + v + i) * 128, 128), side] = tap
                    at = (4 * (2 - u) + 2 - v + i) * 128
                    back[side, at : at + 128] = tap
            for i, j in ((0, 3), (1, 0)):
                at = (4 * u + j) * 128
                side = slice(i * 128, (i + 1) * 128)
                ahead[pl.ds(at, 128), side] = zero
                back[side, at : at + 128] = zero
    for u in range(3):
        for v in range(3):
            at = (3 * (2 - u) + 2 - v) * 256
            w3b[:, at : at + 256] = w3[pl.ds((3 * u + v) * 128, 128), :]


def wave_tables(grid_rows, grid_cols, anchor, frequency, rows_sc, cols_sc):
    own_row, own_col = own_place()
    row = lax.broadcasted_iota(jnp.int32, (PAD_ROWS, 128), 0) - HALO + own_row * ROWS
    angle = (row + anchor[0]).astype(F32) * frequency[0:1, :]
    keep = jnp.where((row >= 0) & (row < grid_rows), 1.0, 0.0)
    rows_sc[0] = jnp.sin(angle) * keep
    rows_sc[1] = jnp.cos(angle) * keep
    for p in range(4):
        k = lax.broadcasted_iota(jnp.int32, (KP, 128), 0)
        col = 4 * jnp.where(k < KO + 4, k, k - KP) + p + own_col * (4 * KO)
        angle = (col + anchor[1]).astype(F32) * frequency[1:2, :]
        keep = jnp.where((col >= 0) & (col < grid_cols), 1.0, 0.0)
        cols_sc[0, p] = jnp.sin(angle) * keep
        cols_sc[1, p] = jnp.cos(angle) * keep


def prep_kernel(grid_rows, grid_cols, anchor, w1, w2, w3, frequency, w1t, w1b, w2t, w2b, w3b, rows_sc, cols_sc):
    weight_forms(w1, w2, w3, w1t, w1b, w2t, w2b, w3b)
    wave_tables(grid_rows, grid_cols, anchor, frequency, rows_sc, cols_sc)


def prep(grid_rows, grid_cols, anchor, w1, w2, w3, frequency):
    def kernel(*refs):
        prep_kernel(grid_rows, grid_cols, *refs)

    shape = jax.ShapeDtypeStruct
    return pl.pallas_call(
        kernel,
        out_shape=[
            shape((1536, 256), BF16),
            shape((256, 1536), BF16),
            shape((1536, 256), BF16),
            shape((256, 1536), BF16),
            shape((128, 2304), BF16),
            shape((2, PAD_ROWS, 128), F32),
            shape((2, 4, KP, 128), F32),
        ],
        in_specs=[smem_spec()] + [vmem_spec()] * 4,
        out_specs=[vmem_spec()] * 7,
        compiler_params=pltpu.CompilerParams(vmem_limit_bytes=VMEM_LIMIT),
        name="weight_forms",
    )(anchor, w1, w2, w3, frequency)


def fill_mask(low_rows, low_cols, mask):
    own_row, own_col = own_place()
    k = lax.broadcasted_iota(jnp.int32, (KP, 128), 0)
    col = jnp.where(k < KO + 4, k, k - KP) + own_col * KO
    inside = jnp.where((col >= 0) & (col < low_cols), 1.0, 0.0)

    def step(at, _):
        row = at - 4 + own_row * 12
        mask[at] = inside * jnp.where((row >= 0) & (row < low_rows), 1.0, 0.0)
        return 0

    lax.fori_loop(0, LOWS, step, 0)


def widened(line):
    rest = jnp.zeros((KW - KP, line.shape[1]), F32)
    return jnp.concatenate([line, rest], axis=0).astype(BF16)


def put_line(ref, row, planes):
    width = planes[0].shape[1]
    for n, plane in enumerate(planes):
        ref[row, :, n * width : (n + 1) * width] = widened(plane)


def before(line):
    return pltpu.roll(line, 1, 0)


def after(line):
    return pltpu.roll(line, KP - 1, 0)


def silu_parts(half):
    th = jnp.tanh(half)
    act = half + half * th
    return act, (1.0 + act) + th * (1.0 - act)


def rounded(value):
    return value.astype(BF16).astype(F32)


def flat(block):
    return block.reshape(128, 128)


def modulation(noise, noise_index):
    modulate = noise[pl.ds(noise_index[0], 1), :]
    return 1.0 + modulate[:, 0:128], modulate[:, 128:256]


def first_lines(load, base, at, tables, stage, x1):
    rows_sc, cols_sc = tables
    for i in range(4):
        own, right, left = load(i)
        stage[i, 0:128] = own.astype(F32)
        stage[i, 128:144] = right.astype(F32)
        stage[i, 144:160] = left.astype(F32)
        sin_row = rows_sc[0, pl.ds(base + i, 1), :]
        cos_row = rows_sc[1, pl.ds(base + i, 1), :]
        planes = []
        for p in range(4):
            value = stage[i, pl.ds(p, KP, stride=4), :]
            planes.append(value + (sin_row * cols_sc[1, p] + cos_row * cols_sc[0, p]))
        put_line(x1, at + i, [before(planes[3])] + planes + [after(planes[0])])


def around(ref, at, count, lanes, cols=KW):
    parts = [ref[pl.ds(at - 1 + u, count), 0:cols, lanes] for u in range(3)]
    return jnp.concatenate([part.reshape(count * cols, part.shape[-1]) for part in parts], axis=1)


def product(left, right):
    return jnp.dot(left, right, preferred_element_type=F32)


def product_turned(left, right):
    return lax.dot_general(left, right, (((1,), (1,)), ((), ())), preferred_element_type=F32)


def weight_terms(grad, field):
    return lax.dot_general(grad, field, (((0,), (0,)), ((), ())), preferred_element_type=F32)


def pipeline(steps, dot, post, z0, z1):
    def put(z, t):
        total = dot(t)
        z[0 : total.shape[0], :] = total

    put(z0, 0)

    def two(i, _):
        put(z1, 2 * i + 1)
        post(2 * i, z0)
        put(z0, 2 * i + 2)
        post(2 * i + 1, z1)
        return 0

    if steps > 2:
        lax.fori_loop(0, (steps - 1) // 2, two, 0)
    if steps % 2 == 0:
        put(z1, steps - 1)
        post(steps - 2, z0)
        post(steps - 1, z1)
    else:
        post(steps - 1, z0)


def conv_one_dot(x1, row, w1t):
    one = around(x1, row, 4, slice(0, 512))
    two = around(x1, row, 4, slice(256, 768))
    return product(jnp.concatenate([one, two], axis=0), w1t[...])


def conv_one_post(z, scale, shift, keeps, d1, d1_row, x2, x2_row):
    for s in range(2):
        halves = []
        for q in range(2):
            total = None
            for p in (2 * q, 2 * q + 1):
                for r in range(2):
                    at = q * 4 * KW + (2 * s + r) * KW
                    half = z[at : at + KP, (p % 2) * 128 : (p % 2 + 1) * 128] * (0.5 * scale) + 0.5 * shift
                    act, slope = silu_parts(half)
                    d1[d1_row + 2 * s + r, :, p * 128 : (p + 1) * 128] = (0.5 * scale) * slope
                    act = rounded(act)
                    total = act if total is None else total + act
            halves.append(total * (0.25 * keeps[s]))
        put_line(x2, x2_row + s, [before(halves[1]), halves[0], halves[1], after(halves[0])])


def own_kernel(
    grid_rows, grid_cols,
    noise_index, inputs, one, two, w1t, rows_sc, cols_sc, noise,
    x1_out, d1_out, x2_out,
    x1, stage, d1, x2, mask, side, z0, z1, sems,
):
    odd = odd_column()
    halos = [
        pltpu.make_async_copy(one, side.at[1 - odd], sems.at[0]),
        pltpu.make_async_copy(two, side.at[odd], sems.at[1]),
    ]
    for copy in halos:
        copy.start()
    fill_mask(grid_rows // 4, grid_cols // 4, mask)
    scale, shift = modulation(noise, noise_index)
    for copy in halos:
        copy.wait()

    def first(q):
        def load(i):
            row = 4 * q + i
            return flat(inputs[row]), side[1, 1 + row], side[0, 1 + row]

        first_lines(load, HALO + 4 * q, 4 * q, (rows_sc, cols_sc), stage, x1)
        part = pl.ds(4 * q, 4)
        pltpu.make_async_copy(x1.at[part], x1_out.at[part], sems.at[2]).start()

    def dot(t):
        return conv_one_dot(x1, 4 * t + 2, w1t)

    def post(t, z):
        keeps = [mask[(9 + 2 * t) // 2], mask[(10 + 2 * t) // 2]]
        conv_one_post(z, scale, shift, keeps, d1, 4 * t, x2, 2 * t)
        part = pl.ds(4 * t, 4)
        pltpu.make_async_copy(d1.at[part], d1_out.at[part], sems.at[3]).start()

    first(0)
    first(1)
    z0[...] = dot(0)
    first(2)

    def two_steps(i, _):
        t = 2 * i + 1
        z1[...] = dot(t)
        first(t + 2)
        post(t - 1, z0)
        z0[...] = dot(t + 1)
        first(t + 3)
        post(t, z1)
        return 0

    lax.fori_loop(0, 4, two_steps, 0)
    z1[...] = dot(9)
    first(11)
    post(8, z0)
    z0[...] = dot(10)
    post(9, z1)
    post(10, z0)
    last = pltpu.make_async_copy(x2, x2_out, sems.at[4])
    last.start()
    pltpu.make_async_copy(x1, x1_out, sems.at[2]).wait()
    pltpu.make_async_copy(d1, d1_out, sems.at[3]).wait()
    last.wait()


def own_rows(grid_rows, grid_cols, *args):
    def kernel(*refs):
        own_kernel(grid_rows, grid_cols, *refs)

    vm = pltpu.VMEM
    shape = jax.ShapeDtypeStruct
    return pl.pallas_call(
        kernel,
        out_shape=[shape((48, KW, 768), BF16), shape((44, KP, 512), F32), shape((22, KW, 512), BF16)],
        in_specs=[smem_spec(), vmem_spec(), any_spec(), any_spec()] + [vmem_spec()] * 4,
        out_specs=[any_spec()] * 3,
        scratch_shapes=[
            vm((48, KW, 768), BF16),
            vm((4, 160, 128), F32),
            vm((44, KP, 512), F32),
            vm((22, KW, 512), BF16),
            vm((LOWS, KP, 128), F32),
            vm((2, ROWS + 4, 16, 128), BF16),
            vm((8 * KW, 256), F32),
            vm((8 * KW, 256), F32),
            pltpu.SemaphoreType.DMA((5,)),
        ],
        compiler_params=pltpu.CompilerParams(vmem_limit_bytes=VMEM_LIMIT),
        cost_estimate=pl.CostEstimate(flops=4 * 10**9, bytes_accessed=30 * 10**6, transcendentals=0),
        name="own_rows",
    )(*args)


def lines_kernel(
    grid_rows, grid_cols,
    noise_index, cot, w1t, rows_sc, cols_sc, noise,
    off, near, one, two, w2t_in, w2b_in, w3_in, w3b_in, x1_in, d1_in, x2_in,
    coarse_out, g1_out, keep_msg, give_msg,
    rim, stage, x1, d1, x2, d2, x3, cp, side, side32, g3, xb2, g2, g1, coarse,
    acc, acc3, gw, ms, mask, z0, z1, w2t, w2b, w3, w3b, sems,
):
    core = lax.axis_index("core")
    odd = odd_column()

    def fetch(source, target, at):
        copy = pltpu.make_async_copy(source, target, sems.at[at])
        copy.start()
        return copy

    got_rims = [fetch(off, rim.at[core], 0), fetch(near, rim.at[1 - core], 1)]
    got_edges = [
        fetch(x1_in.at[pl.ds(0, 4)], x1.at[pl.ds(16, 4)], 2),
        fetch(x1_in.at[pl.ds(44, 4)], x1.at[pl.ds(60, 4)], 3),
    ]
    got_x2 = fetch(x2_in, x2.at[pl.ds(9, 22)], 4)
    units = pl.ds(ROWS + 1, 3)
    got_sides = [fetch(one.at[units], side.at[1 - odd], 5), fetch(two.at[units], side.at[odd], 6)]
    got_w2t = fetch(w2t_in, w2t, 7)
    got_w3 = [fetch(w3_in, w3, 8), fetch(w3b_in, w3b, 9)]
    got_w2b = fetch(w2b_in, w2b, 10)
    got_d1 = fetch(d1_in, d1.at[pl.ds(18, 44)], 11)
    got_x1 = fetch(x1_in.at[pl.ds(4, 40)], x1.at[pl.ds(20, 40)], 12)
    fill_mask(grid_rows // 4, grid_cols // 4, mask)
    scale, shift = modulation(noise, noise_index)
    for copy in got_rims:
        copy.wait()

    def first(n):
        below = n // 4
        start = 4 * (n % 4)
        base = start + (HALO + ROWS) * below

        def load(i):
            row = start + i
            return flat(rim[below, row, 0:8]), rim[below, row, 8 + odd], rim[below, row, 9 - odd]

        first_lines(load, base, base, (rows_sc, cols_sc), stage, x1)

    def mid_of(t):
        return jnp.where(t < 4, 1 + 2 * t, 23 + 2 * t)

    def dot(t):
        return conv_one_dot(x1, 2 * mid_of(t), w1t)

    def post(t, z):
        m = mid_of(t)
        conv_one_post(z, scale, shift, [mask[m // 2], mask[(m + 1) // 2]], d1, 2 * m, x2, m)

    first(0)
    first(1)
    for copy in got_edges:
        copy.wait()
    z0[...] = dot(0)
    first(2)

    def two_steps(i, _):
        t = 2 * i + 1
        z1[...] = dot(t)
        first(t + 2)
        post(t - 1, z0)
        z0[...] = dot(t + 1)
        first(t + 3)
        post(t, z1)
        return 0

    lax.fori_loop(0, 2, two_steps, 0)
    z1[...] = dot(5)
    first(7)
    post(4, z0)
    z0[...] = dot(6)
    post(5, z1)
    z1[...] = dot(7)
    post(6, z0)
    post(7, z1)
    got_x2.wait()
    got_w2t.wait()

    def conv_two_post(t, z):
        for s in range(3):
            low = 1 + 3 * t + s
            total = None
            for q in range(2):
                lanes = slice(q * 128, (q + 1) * 128)
                for r in range(2):
                    row, at = 2 * low + r, (2 * s + r) * KW
                    act, slope = silu_parts(0.5 * z[at : at + KP, lanes])
                    d2[row, :, lanes] = 0.5 * slope
                    down = x2[row, :, (q + 1) * 128 : (q + 2) * 128].astype(F32)[:KP]
                    act = rounded(down + act)
                    total = act if total is None else total + act
            line = total * (0.25 * mask[low])
            put_line(x3, low, [before(line), line, after(line)])

    pipeline(6, lambda t: product(around(x2, 2 + 6 * t, 6, slice(0, 512)), w2t[...]), conv_two_post, z0, z1)

    cp[...] = jnp.zeros_like(cp)
    for copy in got_sides:
        copy.wait()
    for h in range(2):
        lanes = slice(h * 128, (h + 1) * 128)
        for r in range(2):
            units = pl.ds((r * 2 + h) * 2, 2)
            cp[r, 0:KO, lanes] = rim[0, HALO, units].reshape(KO, 128).astype(F32)
            cp[14 + r, 0:KO, lanes] = rim[1, HALO, units].reshape(KO, 128).astype(F32)
    for r in range(12):
        cp[2 + r, 0:KO, :] = cot[r].astype(F32)
    for which, at in ((1, KO), (0, KP - 2)):
        side32[...] = side[which].reshape(48, 128).astype(F32)
        for h in range(2):
            for r in range(12):
                cp[2 + r, at : at + 2, h * 128 : (h + 1) * 128] = side32[r * 4 + h * 2 : r * 4 + h * 2 + 2]
    for below, skip, row in ((0, 8, 0), (1, 0, 14)):
        for unit, at in ((9 - odd, KP - 2), (8 + odd, KO)):
            side32[0:16] = rim[below, HALO, unit].astype(F32)
            for h in range(2):
                for r in range(2):
                    start = skip + r * 4 + h * 2
                    cp[row + r, at : at + 2, h * 128 : (h + 1) * 128] = side32[start : start + 2]
    for copy in got_w3:
        copy.wait()
    g3[1] = jnp.zeros((KW, 768), BF16)
    g3[18] = jnp.zeros((KW, 768), BF16)

    def conv_three_post(t, z):
        for i in range(4):
            row = 2 + 4 * t + i
            act, slope = silu_parts(0.5 * z[i * KW : i * KW + KP, :])
            keep = 0.5 * mask[row]
            line = cp[row - 2] * slope * jnp.concatenate([keep, keep], axis=1)
            put_line(g3, row, [before(line), line, after(line)])
            coarse[row - 2] = act[:KO].astype(BF16)

    pipeline(4, lambda t: product(around(x3, 2 + 4 * t, 4, slice(0, 384)), w3[...]), conv_three_post, z0, z1)
    put_coarse = fetch(coarse.at[pl.ds(2, 12)], coarse_out, 0)

    def back_three_post(t, z):
        for i in range(4):
            low = 2 + 4 * t + i
            line = 0.25 * z[i * KW : i * KW + KP, 0:128]
            xb2[low] = line
            line = line * mask[low]
            for r in range(2):
                row = 2 * low + r
                zero, one = (line * d2[row, :, q * 128 : (q + 1) * 128] for q in range(2))
                put_line(g2, row, [before(one), zero, one, after(zero)])

    def back_three_dot(t):
        total = product_turned(around(g3, 2 + 4 * t, 4, slice(0, 768)), w3b[...])
        return jnp.concatenate([total, total], axis=1)

    pipeline(4, back_three_dot, back_three_post, z0, z1)
    acc3[...] = weight_terms(
        g3[4:16, 0:KO, 256:512].reshape(12 * KO, 256), around(x3, 4, 12, slice(0, 384), KO)
    )
    acc[...] = weight_terms(
        g2[8:32, 0:KO, 128:384].reshape(24 * KO, 256), around(x2, 8, 24, slice(0, 512), KO)
    )
    got_w2b.wait()
    got_d1.wait()

    def back_two_post(t, z):
        for i in range(4):
            m = 6 + 4 * t + i
            low = m // 2
            keep = 0.25 * mask[low]
            base = xb2[low]
            both = [(base + z[i * KW : i * KW + KP, q * 128 : (q + 1) * 128]) * keep for q in range(2)]
            for r in range(2):
                row = 2 * m + r
                planes = [both[p // 2] * d1[row, :, p * 128 : (p + 1) * 128] for p in range(4)]
                for n, line in enumerate([before(planes[3])] + planes + [after(planes[0])]):
                    g1[row - 12, :, n * 128 : (n + 1) * 128] = line[:KO].astype(BF16)

    pipeline(
        7, lambda t: product_turned(around(g2, 6 + 4 * t, 4, slice(0, 512)), w2b[...]), back_two_post, z0, z1
    )
    put_g1 = fetch(g1.at[pl.ds(3, 50)], g1_out, 1)
    got_x1.wait()

    def fold_weights(at):
        for u in range(3):
            for v in range(3):
                left = (4 * u + v) * 128
                term = acc[0:128, left : left + 128] + acc[128:256, left + 128 : left + 256]
                gw[at, pl.ds((3 * u + v) * 128, 128), :] = term.T

    def nines(t):
        for owner in range(128):
            at = owner * 40 + t * 9
            ms[at : at + 9, :] = gw[t, owner * 9 : owner * 9 + 9, :]

    def one_chunk(t):
        grads = jnp.concatenate(
            [g1[4 + 16 * t : 20 + 16 * t, :, lanes].reshape(512, 256) for lanes in (slice(128, 384), slice(384, 640))],
            axis=0,
        )
        fields = jnp.concatenate(
            [around(x1, 16 + 16 * t, 16, lanes, KO) for lanes in (slice(0, 512), slice(256, 768))], axis=0
        )
        return weight_terms(grads, fields)

    fold_weights(1)
    acc[...] = one_chunk(0)
    for tap in range(9):
        turned = acc3[:, tap * 128 : (tap + 1) * 128].T
        gw[2, pl.ds(tap * 128, 128), :] = turned[:, 0:128]
        gw[3, pl.ds(tap * 128, 128), :] = turned[:, 128:256]
    nines(1)
    acc[...] += one_chunk(1)
    nines(2)
    nines(3)
    acc[...] += one_chunk(2)
    for owner in range(128):
        ms[owner * 40 + 36 : owner * 40 + 40, :] = jnp.zeros((4, 128), F32)
    fold_weights(0)
    nines(0)

    def msg_step(n, _):
        rows = pl.ds(pl.multiple_of(n * 320, 320), 320)
        keep_msg[rows, :] = ms[pl.ds(pl.multiple_of((2 * n + core) * 320, 320), 320), :].astype(BF16)
        give_msg[rows, :] = ms[pl.ds(pl.multiple_of((2 * n + 1 - core) * 320, 320), 320), :].astype(BF16)
        return 0

    lax.fori_loop(0, 8, msg_step, 0)
    put_coarse.wait()
    put_g1.wait()


def levels(grid_rows, grid_cols, *args):
    def kernel(*refs):
        lines_kernel(grid_rows, grid_cols, *refs)

    vm = pltpu.VMEM
    return pl.pallas_call(
        kernel,
        out_shape=[
            jax.ShapeDtypeStruct((12, KO, 256), BF16),
            jax.ShapeDtypeStruct((50, KO, 768), BF16),
            jax.ShapeDtypeStruct((2560, 128), BF16),
            jax.ShapeDtypeStruct((2560, 128), BF16),
        ],
        in_specs=[smem_spec()] + [vmem_spec()] * 5 + [any_spec()] * 11,
        out_specs=[any_spec(), any_spec(), vmem_spec(), vmem_spec()],
        scratch_shapes=[
            vm((2, HALO + 1, 10, 16, 128), BF16),
            vm((4, 160, 128), F32),
            vm((PAD_ROWS, KW, 768), BF16),
            vm((PAD_ROWS, KP, 512), F32),
            vm((PAIRS, KW, 512), BF16),
            vm((PAIRS, KP, 256), F32),
            vm((LOWS, KW, 384), BF16),
            vm((16, KP, 256), F32),
            vm((2, 3, 16, 128), BF16),
            vm((48, 128), F32),
            vm((LOWS, KW, 768), BF16),
            vm((LOWS, KP, 128), F32),
            vm((PAIRS, KW, 512), BF16),
            vm((56, KO, 768), BF16),
            vm((16, KO, 256), BF16),
            vm((256, 1536), F32),
            vm((256, 1152), F32),
            vm((4, 1152, 128), F32),
            vm((5120, 128), F32),
            vm((LOWS, KP, 128), F32),
            vm((8 * KW, 256), F32),
            vm((8 * KW, 256), F32),
            vm((1536, 256), BF16),
            vm((256, 1536), BF16),
            vm((1152, 256), BF16),
            vm((128, 2304), BF16),
            pltpu.SemaphoreType.DMA((13,)),
        ],
        compiler_params=pltpu.CompilerParams(vmem_limit_bytes=VMEM_LIMIT),
        name="encoder_levels",
    )(*args)


def input_kernel(g1, g1_next, w1b, out, stage):
    for t in range(2):
        halves = []
        for lanes in (slice(0, 512), slice(256, 768)):
            rows = jnp.concatenate([g1[:, :, lanes], g1_next[:, :, lanes]], axis=0)
            parts = [rows[4 * t + u : 4 * t + u + 4].reshape(128, 512) for u in range(3)]
            halves.append(jnp.concatenate(parts, axis=1))
        total = product_turned(jnp.concatenate(halves, axis=0), w1b[...])
        for r in range(4):
            for p in range(4):
                rows = (p // 2) * 128 + r * 32
                value = total[rows : rows + 32, (p % 2) * 128 : (p % 2 + 1) * 128]
                stage[4 * t + r, pl.ds(p, 32, stride=4), :] = value
            out[4 * t + r] = stage[4 * t + r].astype(BF16)


def input_grad(g1, w1b):
    return pl.pallas_call(
        input_kernel,
        grid=(6,),
        out_shape=jax.ShapeDtypeStruct((ROWS, 128, 128), BF16),
        in_specs=[
            pl.BlockSpec((8, KO, 768), lambda i: (i, 0, 0)),
            pl.BlockSpec((2, KO, 768), lambda i: (4 * i + 4, 0, 0)),
            pl.BlockSpec((256, 1536), lambda i: (0, 0)),
        ],
        out_specs=pl.BlockSpec((8, 128, 128), lambda i: (i, 0, 0)),
        scratch_shapes=[pltpu.VMEM((8, 128, 128), F32)],
        compiler_params=pltpu.CompilerParams(vmem_limit_bytes=VMEM_LIMIT),
        cost_estimate=pl.CostEstimate(flops=2 * 6144 * 1152 * 128, bytes_accessed=8 * 1024 * 1024, transcendentals=0),
        name="input_grad",
    )(g1, g1, w1b)


def add_kernel(keep, other, out):
    out[...] = (keep[...].astype(F32) + other[...].astype(F32)).astype(BF16)


def add(keep, other):
    return pl.pallas_call(
        add_kernel,
        out_shape=jax.ShapeDtypeStruct(keep.shape, BF16),
        in_specs=[vmem_spec()] * 2,
        out_specs=vmem_spec(),
        name="add_core_terms",
    )(keep, other)


def collect(got):
    sums = got.astype(F32).sum(axis=0)
    return sums[0:9], sums[9:18], jnp.concatenate([sums[18:27], sums[27:36]], axis=1)


def swapped(block, axis, odd_first):
    devices = lax.axis_size(axis)
    pairs = []
    for i in range(1 if odd_first else 0, devices - 1, 2):
        pairs += [(i, i + 1), (i + 1, i)]
    return lax.ppermute(block, axis, pairs)


def body(inputs, weight_one, weight_two, weight_three, noise_table, frequency, anchor, noise_index, cotangent):
    grid = (lax.axis_size(ROW_AXES) * ROWS, lax.axis_size("tx") * 4 * KO)
    inputs = inputs.reshape(ROWS, 8, 16, 128)
    one, two, cots = sides(inputs, cotangent)
    one = swapped(one, "tx", False)
    two = swapped(two, "tx", True)
    w1t, w1b, w2t, w2b, w3b, rows_sc, cols_sc = prep(*grid, anchor, weight_one, weight_two, weight_three, frequency)
    off, near = rims(inputs, cots, one, two, rows_sc)
    off = swapped(off, ROW_AXES, True)
    near = lax.ppermute(near, "core", [(0, 1), (1, 0)])
    x1, d1, x2 = own_rows(*grid, noise_index, inputs, one, two, w1t, rows_sc, cols_sc, noise_table)
    coarse, g1, keep_msg, give_msg = levels(
        *grid, noise_index, cotangent, w1t, rows_sc, cols_sc, noise_table,
        off, near, one, two, w2t, w2b, weight_three, w3b, x1, d1, x2,
    )
    other = lax.ppermute(give_msg, "core", [(0, 1), (1, 0)])
    msg = add(keep_msg, other).reshape(64, 40, 128)
    got = lax.all_to_all(msg, ("chip", "tx"), 0, 0, tiled=True)
    grad_inputs = input_grad(g1, w1b)
    return (coarse, grad_inputs, *collect(got))


def solution(mesh):
    halves = jax.sharding.Mesh(mesh.devices.reshape(-1, 2, mesh.devices.shape[1]), ("chip", "core", "tx"))
    placed = (P(ROW_AXES, "tx", None), P(), P(), P(), P(), P(), P(), P(), P(ROW_AXES, "tx", None))
    return jax.shard_map(
        body,
        mesh=halves,
        in_specs=placed,
        out_specs=(
            P(ROW_AXES, "tx", None),
            P(ROW_AXES, "tx", None),
            P((*ROW_AXES, "tx"), None),
            P((*ROW_AXES, "tx"), None),
            P((*ROW_AXES, "tx"), None),
        ),
        check_vma=False,
    )
```

time: 108 us -> 86.7 us (0.80)
  starting transfers between devices: 36.1 us -> 21.5 us
  waiting for transfers between devices: 17.5 us -> 11.8 us
  local copies, waits for them, and re-layouts: 5.03 us -> 3.29 us
  Pallas kernels: 46.4 us -> 47.5 us
    ppermute x6 -> x4, starting transfers between devices: 14 us -> 6.24 us  [the longest x1 3.22 us: body(): near = lax.ppermute(near, 'core', [(0, 1), (1, 0)])]
    ppermute x6 -> x4, waiting for transfers between devices: 7.62 us -> 1.4 us  [the longest x3 1.39 us: swapped(): return lax.ppermute(block, axis, pairs)]
    all_to_all x1, starting transfers between devices: 18.9 us -> 15.2 us  [body(): got = lax.all_to_all(msg, ('chip', 'tx'), 0, 0, tiled=True)]
    ppermute x1, starting transfers between devices: 3.24 us -> 0.08 us  [body(): other = lax.ppermute(give_msg, 'core', [(0, 1), (1, 0)])]
    pallas_call x1 -> x2, Pallas kernels: 11.3 us -> 12.1 us  [the longest x1 9.65 us: own_rows(): pl.pallas_call(kernel, out_shape=[shape((48, KW, 768), BF16), shape((44,...]
    unnamed x18 -> x10, local copies, waits for them, and re-layouts: 3.34 us -> 2.68 us
  transfers between devices with their start and end apart: 8 -> 6, of which waited for: 5 -> 3; matrix products, arithmetic and copies ran while one was open for 2% -> 0% of each run, Pallas kernels for 10% -> 23%
where the time goes in v2:
time: 86.7 us; the launch traced here: 86.2 us
  Pallas kernels  47.5 us (55%)
  starting transfers between devices  21.5 us (25%)
  waiting for transfers between devices  11.8 us (14%)
  local copies, waits for them, and re-layouts  3.29 us (4%)
  between operations  1.39 us (2%)
    pallas_call x1, Pallas kernels, levels(): pl.pallas_call(kernel, out_shape=[jax.ShapeDtypeStruct((12, KO, 256), BF1...  20 us
    all_to_all x1, starting transfers between devices, body(): got = lax.all_to_all(msg, ('chip', 'tx'), 0, 0, tiled=True)  15.2 us
    pallas_call x1, Pallas kernels, own_rows(): pl.pallas_call(kernel, out_shape=[shape((48, KW, 768), BF16), shape((44,...  9.65 us
    all_to_all x1, waiting for transfers between devices, body(): got = lax.all_to_all(msg, ('chip', 'tx'), 0, 0, tiled=True)  8.13 us
    pallas_call x1, Pallas kernels, input_grad(): pl.pallas_call(input_kernel, grid=(6,), out_shape=jax.ShapeDtypeStruct((R...  6.91 us
    pallas_call x1, Pallas kernels, prep(): pl.pallas_call(kernel, out_shape=[shape((1536, 256), BF16), shape((256, 1...  3.4 us
    ppermute x1, starting transfers between devices, body(): near = lax.ppermute(near, 'core', [(0, 1), (1, 0)])  3.22 us
    ppermute x3, starting transfers between devices, swapped(): return lax.ppermute(block, axis, pairs)  3.02 us
  transfers between devices with their start and end apart: 6, of which 3 were waited for; matrix products, arithmetic and copies ran while one was open for 0% of the time, Pallas kernels for 23%

profile of v2, /device:TPU:0, one launch (start us, length us, event | category | flops | bytes accessed | tf_op | source)
XLA Modules:
  0.0 86.2 jit_solution(10745948735074352708)
XLA Ops:
  0.6 2.8 %pack_columns.1 = (bf16[52,16,128]{2,1,0:T(8,128)(2,1)}, bf16[52,16,128]{2,1,0:T(8,128)(2,1)}, bf16[2,8,16,128]{3,2,1,0:T(8,128)(2,1)}) custom-call(bf16[48,8,16,128]{3,2,1,0:T(8,128)(2,1)} %bitcast.2, bf16[12,32,256]{2,1,0:T(8,128)(2,1)} %refs_1_.3), custom_call_target="tpu_custom_call" | custom-call | tf_op jit(solution)/shard_map/pack_columns/pallas_call | solution.py:71
  3.4 1.7 %collective-permute-start = (bf16[52,16,128]{2,1,0:T(8,128)(2,1)}, bf16[52,16,128]{2,1,0:T(8,128)(2,1)S(1)}, u32[]{:S(2)}, u32[]{:S(2)}) collective-permute-start(bf16[52,16,128]{2,1,0:T(8,128)(2,1)} %get-tuple-element.28), channel_id=1, source_target_pairs={{0,1},{1,0},{2,3},{3,2},{4,5},{5,4},{6,7},{7,6},{8,9},{9,8},{10,11... | collective-permute-start | bytes 638984 | tf_op jit(solution)/shard_map/ppermute | solution.py:746
  5.0 0.7 collective-permute-start.1
  5.7 3.4 %weight_forms.1 = (bf16[1536,256]{1,0:T(8,128)(2,1)}, bf16[256,1536]{1,0:T(8,128)(2,1)}, bf16[1536,256]{1,0:T(8,128)(2,1)}, bf16[256,1536]{1,0:T(8,128)(2,1)}, b...) custom-call(s32[2]{0:T(128)} %refs_0_.3, bf16[1152,128]{1,0:T(8,128)(2,1)} %refs_1_.2, ...), custom_call_target="tpu_custom_call" | custom-call | tf_op jit(solution)/shard_map/weight_forms/pallas_call | solution.py:161
  9.1 1.4 %collective-permute-done.one.refs_2_.refs_8_ = bf16[52,16,128]{2,1,0:T(8,128)(2,1)S(1)} collective-permute-done((bf16[52,16,128]{2,1,0:T(8,128)(2,1)}, bf16[52,16,128]{2,1,0:T(8,128)(2,1)S(1)}, u32[]{:S(2)}, u32[]{:S(2)}) %collective-permute-start) | collective-permute-done | bytes 213024 | tf_op jit(solution)/shard_map/ppermute | solution.py:746
  10.5 0.0 copy-start
  10.5 0.0 collective-permute-done.1.two.refs_3_.refs_9_
  10.5 0.0 copy-start.1
  10.5 0.7 copy-done
  11.2 0.1 copy-done.1
  11.3 2.5 %pack_rows.1 = (bf16[17,10,16,128]{3,2,1,0:T(8,128)(2,1)}, bf16[17,10,16,128]{3,2,1,0:T(8,128)(2,1)}) custom-call(bf16[48,8,16,128]{3,2,1,0:T(8,128)(2,1)} %bitcast.3, bf16[2,8,16,128]{3,2,1,0:T(8,128)(2,1)} %get-tuple-element.27.cots, bf16[52,16,128]{2,1,0:T(8,128)(2,1)} %copy-done, bf16[52,16,128]{2,1,0:T(8,128)(2,1)} %copy-done.1, ...), custom_call_target="tpu_custom_call" | custom-call | tf_op jit(solution)/shard_map/pack_rows/pallas_call | solution.py:103
  13.8 0.7 collective-permute-start.2
  14.5 3.2 %collective-permute-start.3 = (bf16[17,10,16,128]{3,2,1,0:T(8,128)(2,1)}, bf16[17,10,16,128]{3,2,1,0:T(8,128)(2,1)S(1)}, u32[]{:S(2)}, u32[]{:S(2)}) collective-permute-start(bf16[17,10,16,128]{3,2,1,0:T(8,128)(2,1)} %get-tuple-element.31), channel_id=1, source_target_pairs={{0,8},{8,0},{1,9},{9,1},{2,10},{10,2},{3,11},{11,3},{4,12},{12,4},... | collective-permute-start | bytes 2088968 | tf_op jit(solution)/shard_map/ppermute | solution.py:758
  18.4 9.7 %own_rows.1 = (bf16[48,48,768]{2,1,0:T(8,128)(2,1)}, f32[44,40,512]{2,1,0:T(8,128)}, bf16[22,48,512]{2,1,0:T(8,128)(2,1)}) custom-call(s32[1]{0:T(128)S(6)} %copy.14.refs_0_, bf16[48,8,16,128]{3,2,1,0:T(8,128)(2,1)} %bitcast.4, bf16[52,16,128]{2,1,0:T(8,128)(2,1)} %copy-done, bf16[52,16,128]{2,1,0:T(8,128)(2,1)} %copy-done.1, ...), custom_call_target="tpu_custom_call" | custom-call | flops 4000000000 | bytes 30000000 | tf_op jit(solution)/shard_map/own_rows/pallas_call | solution.py:382
  28.0 0.0 collective-permute-done.2.refs_6_
  28.0 0.0 copy-start.2
  28.0 0.0 collective-permute-done.3.refs_7_
  28.0 0.0 copy-start.3
  28.1 0.9 %copy-done.2 = bf16[17,10,16,128]{3,2,1,0:T(8,128)(2,1)} copy-done((bf16[17,10,16,128]{3,2,1,0:T(8,128)(2,1)}, bf16[17,10,16,128]{3,2,1,0:T(8,128)(2,1)S(1)}, u32[]{:S(2)}) %copy-start.2) | copy-done | bytes 696344
  28.9 0.2 copy-done.3
  29.1 20.0 %encoder_levels.1 = (bf16[12,32,256]{2,1,0:T(8,128)(2,1)}, bf16[50,32,768]{2,1,0:T(8,128)(2,1)}, bf16[2560,128]{1,0:T(8,128)(2,1)}, bf16[2560,128]{1,0:T(8,128)(2,1)}) custom-call(s32[1]{0:T(128)S(6)} %copy.14.refs_0_, bf16[12,32,256]{2,1,0:T(8,128)(2,1)} %refs_1_.3, bf16[1536,256]{1,0:T(8,128)(2,1)} %get-tuple-element.24.refs_4_.refs_2_, ...), custom_call_target="tpu_custom_call" | custom-call | tf_op jit(solution)/shard_map/encoder_levels/pallas_call | solution.py:644
  49.1 0.1 collective-permute-start.4
  49.2 2.3 %collective-permute-done.4.other = bf16[2560,128]{1,0:T(8,128)(2,1)S(1)} collective-permute-done((bf16[2560,128]{1,0:T(8,128)(2,1)}, bf16[2560,128]{1,0:T(8,128)(2,1)S(1)}, u32[]{:S(2)}, u32[]{:S(2)}) %collective-permute-start.4) | collective-permute-done | bytes 655392 | tf_op jit(solution)/shard_map/ppermute | solution.py:764
  51.5 0.0 copy-start.4
  51.5 0.8 copy-done.4
  52.4 2.3 %add_core_terms.1 = bf16[2560,128]{1,0:T(8,128)(2,1)} custom-call(bf16[2560,128]{1,0:T(8,128)(2,1)} %get-tuple-element.41.keep, bf16[2560,128]{1,0:T(8,128)(2,1)} %copy-done.4), custom_call_target="tpu_custom_call" | custom-call | tf_op jit(solution)/shard_map/add_core_terms/pallas_call | solution.py:727
  54.6 15.2 %all-to-all-start = ((bf16[64,40,128]{2,1,0:T(8,128)(2,1)}), bf16[64,40,128]{2,1,0:T(8,128)(2,1)S(1)}, u32[]{:S(2)}, u32[]{:S(2)}) async-start(bf16[64,40,128]{2,1,0:T(8,128)(2,1)} %bitcast.5), calls=%async_computation | async-start | bytes 1310720 | tf_op jit(solution)/shard_map/all_to_all | solution.py:766
  69.8 6.9 %input_grad.1 = bf16[48,128,128]{2,1,0:T(8,128)(2,1)} custom-call(bf16[50,32,768]{2,1,0:T(8,128)(2,1)} %get-tuple-element.39.g1.g1_next, bf16[50,32,768]{2,1,0:T(8,128)(2,1)} %get-tuple-element.39.g1.g1_next, bf16[256,1536]{1,0:T(8,128)(2,1)} %get-tuple-element.40.w1b), custom_call_target="tpu_custom_call" | custom-call | flops 1811939328 | bytes 8388608 | tf_op jit(solution)/shard_map/input_grad/pallas_call | solution.py:705
  76.7 8.1 %all-to-all-done = bf16[64,40,128]{2,1,0:T(8,128)(2,1)S(1)} async-done(((bf16[64,40,128]{2,1,0:T(8,128)(2,1)}), bf16[64,40,128]{2,1,0:T(8,128)(2,1)S(1)}, u32[]{:S(2)}, u32[]{:S(2)}) %all-to-all-start) | async-done | bytes 655392 | tf_op jit(solution)/shard_map/all_to_all | solution.py:766
  84.8 0.1 convert_reduce_fusion
  85.0 0.6 fusion
  85.6 0.6 pad_maximum_fusion
Async XLA Ops:
  3.4 7.1 %collective-permute-start = (bf16[52,16,128]{2,1,0:T(8,128)(2,1)}, bf16[52,16,128]{2,1,0:T(8,128)(2,1)S(1)}, u32[]{:S(2)}, u32[]{:S(2)}) collective-permute-start(bf16[52,16,128]{2,1,0:T(8,128)(2,1)} %get-tuple-element.28), channel_id=1, source_target_pairs={{0,1},{1,0},{2,3},{3,2},{4,5},{5,4},{6,7},{7,6},{8,9},{9,8},{10,11... | collective-permute-start | bytes 638984 | tf_op jit(solution)/shard_map/ppermute | solution.py:746
  5.0 5.5 %collective-permute-start.1 = (bf16[52,16,128]{2,1,0:T(8,128)(2,1)}, bf16[52,16,128]{2,1,0:T(8,128)(2,1)S(1)}, u32[]{:S(2)}, u32[]{:S(2)}) collective-permute-start(bf16[52,16,128]{2,1,0:T(8,128)(2,1)} %get-tuple-element.29), channel_id=1, source_target_pairs={{1,2},{2,1},{3,4},{4,3},{5,6},{6,5},{9,10},{10,9},{11,12},{12,11},... | collective-permute-start | bytes 638984 | tf_op jit(solution)/shard_map/ppermute | solution.py:746
  10.5 0.7 copy-start
  10.5 0.8 copy-start.1
  13.8 14.3 %collective-permute-start.2 = (bf16[17,10,16,128]{3,2,1,0:T(8,128)(2,1)}, bf16[17,10,16,128]{3,2,1,0:T(8,128)(2,1)S(1)}, u32[]{:S(2)}, u32[]{:S(2)}) collective-permute-start(bf16[17,10,16,128]{3,2,1,0:T(8,128)(2,1)} %get-tuple-element.30), channel_id=1, source_target_pairs={{8,16},{16,8},{24,32},{32,24},{40,48},{48,40},{56,64},{64,56},{72,... | collective-permute-start | bytes 2088968 | tf_op jit(solution)/shard_map/ppermute | solution.py:746
  14.5 13.6 %collective-permute-start.3 = (bf16[17,10,16,128]{3,2,1,0:T(8,128)(2,1)}, bf16[17,10,16,128]{3,2,1,0:T(8,128)(2,1)S(1)}, u32[]{:S(2)}, u32[]{:S(2)}) collective-permute-start(bf16[17,10,16,128]{3,2,1,0:T(8,128)(2,1)} %get-tuple-element.31), channel_id=1, source_target_pairs={{0,8},{8,0},{1,9},{9,1},{2,10},{10,2},{3,11},{11,3},{4,12},{12,4},... | collective-permute-start | bytes 2088968 | tf_op jit(solution)/shard_map/ppermute | solution.py:758
  28.0 0.9 %copy-start.2 = (bf16[17,10,16,128]{3,2,1,0:T(8,128)(2,1)}, bf16[17,10,16,128]{3,2,1,0:T(8,128)(2,1)S(1)}, u32[]{:S(2)}) copy-start(bf16[17,10,16,128]{3,2,1,0:T(8,128)(2,1)S(1)} %collective-permute-done.2.refs_6_) | copy-start | bytes 2088964
  28.0 1.1 %copy-start.3 = (bf16[17,10,16,128]{3,2,1,0:T(8,128)(2,1)}, bf16[17,10,16,128]{3,2,1,0:T(8,128)(2,1)S(1)}, u32[]{:S(2)}) copy-start(bf16[17,10,16,128]{3,2,1,0:T(8,128)(2,1)S(1)} %collective-permute-done.3.refs_7_) | copy-start | bytes 2088964
  49.1 2.4 %collective-permute-start.4 = (bf16[2560,128]{1,0:T(8,128)(2,1)}, bf16[2560,128]{1,0:T(8,128)(2,1)S(1)}, u32[]{:S(2)}, u32[]{:S(2)}) collective-permute-start(bf16[2560,128]{1,0:T(8,128)(2,1)} %get-tuple-element.42), channel_id=1, source_target_pairs={{0,8},{8,0},{1,9},{9,1},{2,10},{10,2},{3,11},{11,3},{4,12},{12,4},... | collective-permute-start | bytes 1966088 | tf_op jit(solution)/shard_map/ppermute | solution.py:764
  51.5 0.8 copy-start.4
  54.6 30.2 %all-to-all-start = ((bf16[64,40,128]{2,1,0:T(8,128)(2,1)}), bf16[64,40,128]{2,1,0:T(8,128)(2,1)S(1)}, u32[]{:S(2)}, u32[]{:S(2)}) async-start(bf16[64,40,128]{2,1,0:T(8,128)(2,1)} %bitcast.5), calls=%async_computation | async-start | bytes 1310720 | tf_op jit(solution)/shard_map/all_to_all | solution.py:766

commit v3 on v2

--- a/solution.py
+++ b/solution.py
@@ -74,6 +74,7 @@
         in_specs=[any_spec(), vmem_spec()],
         out_specs=[vmem_spec()] * 3,
         scratch_shapes=[pltpu.VMEM((48, 128), F32), pltpu.SemaphoreType.DMA((2,))],
+        compiler_params=pltpu.CompilerParams(vmem_limit_bytes=VMEM_LIMIT),
         name="pack_columns",
     )(inputs, cot)
 
@@ -106,6 +107,7 @@
         in_specs=[any_spec()] * len(args),
         out_specs=[vmem_spec()] * 2,
         scratch_shapes=[pltpu.SemaphoreType.DMA((12,))],
+        compiler_params=pltpu.CompilerParams(vmem_limit_bytes=VMEM_LIMIT),
         name="pack_rows",
     )(*args)
 
@@ -292,38 +294,44 @@
 
 
 def conv_one_post(z, scale, shift, keeps, d1, d1_row, x2, x2_row):
+    half_scale, half_shift = 0.5 * scale, 0.5 * shift
+    slope_scale = half_scale.astype(BF16)
     for s in range(2):
         halves = []
         for q in range(2):
-            total = None
+            sums = []
             for p in (2 * q, 2 * q + 1):
+                lanes = slice((p % 2) * 128, (p % 2 + 1) * 128)
+                acts = []
                 for r in range(2):
                     at = q * 4 * KW + (2 * s + r) * KW
-                    half = z[at : at + KP, (p % 2) * 128 : (p % 2 + 1) * 128] * (0.5 * scale) + 0.5 * shift
-                    act, slope = silu_parts(half)
-                    d1[d1_row + 2 * s + r, :, p * 128 : (p + 1) * 128] = (0.5 * scale) * slope
-                    act = rounded(act)
-                    total = act if total is None else total + act
-            halves.append(total * (0.25 * keeps[s]))
+                    act, slope = silu_parts((z[at : at + KW, lanes] * half_scale + half_shift).astype(BF16))
+                    d1[d1_row + 2 * s + r, :, p * 128 : (p + 1) * 128] = slope_scale * slope
+                    acts.append(act)
+                sums.append((acts[0] + acts[1]).astype(F32))
+            halves.append((sums[0] + sums[1])[:KP] * (0.25 * keeps[s]))
         put_line(x2, x2_row + s, [before(halves[1]), halves[0], halves[1], after(halves[0])])
 
 
 def own_kernel(
     grid_rows, grid_cols,
-    noise_index, inputs, one, two, w1t, rows_sc, cols_sc, noise,
+    noise_index, rows_sc, cols_sc, noise, inputs_in, one, two, w1t_in,
     x1_out, d1_out, x2_out,
-    x1, stage, d1, x2, mask, side, z0, z1, sems,
+    x1, stage, d1, x2, mask, side, inputs, w1t, z0, z1, sems,
 ):
     odd = odd_column()
     halos = [
         pltpu.make_async_copy(one, side.at[1 - odd], sems.at[0]),
         pltpu.make_async_copy(two, side.at[odd], sems.at[1]),
     ]
-    for copy in halos:
+    early = pltpu.make_async_copy(inputs_in.at[pl.ds(0, 12)], inputs.at[pl.ds(0, 12)], sems.at[5])
+    got_w1t = pltpu.make_async_copy(w1t_in, w1t, sems.at[6])
+    late = pltpu.make_async_copy(inputs_in.at[pl.ds(12, 36)], inputs.at[pl.ds(12, 36)], sems.at[7])
+    for copy in (*halos, early, got_w1t, late):
         copy.start()
     fill_mask(grid_rows // 4, grid_cols // 4, mask)
     scale, shift = modulation(noise, noise_index)
-    for copy in halos:
+    for copy in (*halos, early):
         copy.wait()
 
     def first(q):
@@ -346,8 +354,10 @@
 
     first(0)
     first(1)
+    got_w1t.wait()
     z0[...] = dot(0)
     first(2)
+    late.wait()
 
     def two_steps(i, _):
         t = 2 * i + 1
@@ -381,19 +391,21 @@
     shape = jax.ShapeDtypeStruct
     return pl.pallas_call(
         kernel,
-        out_shape=[shape((48, KW, 768), BF16), shape((44, KP, 512), F32), shape((22, KW, 512), BF16)],
-        in_specs=[smem_spec(), vmem_spec(), any_spec(), any_spec()] + [vmem_spec()] * 4,
+        out_shape=[shape((48, KW, 768), BF16), shape((44, KW, 512), BF16), shape((22, KW, 512), BF16)],
+        in_specs=[smem_spec()] + [vmem_spec()] * 3 + [any_spec()] * 4,
         out_specs=[any_spec()] * 3,
         scratch_shapes=[
             vm((48, KW, 768), BF16),
             vm((4, 160, 128), F32),
-            vm((44, KP, 512), F32),
+            vm((44, KW, 512), BF16),
             vm((22, KW, 512), BF16),
             vm((LOWS, KP, 128), F32),
             vm((2, ROWS + 4, 16, 128), BF16),
+            vm((ROWS, 8, 16, 128), BF16),
+            vm((1536, 256), BF16),
             vm((8 * KW, 256), F32),
             vm((8 * KW, 256), F32),
-            pltpu.SemaphoreType.DMA((5,)),
+            pltpu.SemaphoreType.DMA((8,)),
         ],
         compiler_params=pltpu.CompilerParams(vmem_limit_bytes=VMEM_LIMIT),
         cost_estimate=pl.CostEstimate(flops=4 * 10**9, bytes_accessed=30 * 10**6, transcendentals=0),
@@ -403,11 +415,11 @@
 
 def lines_kernel(
     grid_rows, grid_cols,
-    noise_index, cot, w1t, rows_sc, cols_sc, noise,
-    off, near, one, two, w2t_in, w2b_in, w3_in, w3b_in, x1_in, d1_in, x2_in,
-    coarse_out, g1_out, keep_msg, give_msg,
+    noise_index, rows_sc, cols_sc, noise,
+    cot_in, w1t_in, off, near, one, two, w2t_in, w2b_in, w3_in, w3b_in, x1_in, d1_in, x2_in,
+    coarse_out, g1_out, keep_out, give_out,
     rim, stage, x1, d1, x2, d2, x3, cp, side, side32, g3, xb2, g2, g1, coarse,
-    acc, acc3, gw, ms, mask, z0, z1, w2t, w2b, w3, w3b, sems,
+    acc, acc3, gw, msg, mask, z0, z1, cot, w1t, w2t, w2b, w3, w3b, sems,
 ):
     core = lax.axis_index("core")
     odd = odd_column()
@@ -422,15 +434,19 @@
         fetch(x1_in.at[pl.ds(0, 4)], x1.at[pl.ds(16, 4)], 2),
         fetch(x1_in.at[pl.ds(44, 4)], x1.at[pl.ds(60, 4)], 3),
     ]
+    got_w1t = fetch(w1t_in, w1t, 13)
     got_x2 = fetch(x2_in, x2.at[pl.ds(9, 22)], 4)
     units = pl.ds(ROWS + 1, 3)
     got_sides = [fetch(one.at[units], side.at[1 - odd], 5), fetch(two.at[units], side.at[odd], 6)]
+    got_cot = fetch(cot_in, cot, 14)
     got_w2t = fetch(w2t_in, w2t, 7)
     got_w3 = [fetch(w3_in, w3, 8), fetch(w3b_in, w3b, 9)]
     got_w2b = fetch(w2b_in, w2b, 10)
     got_d1 = fetch(d1_in, d1.at[pl.ds(18, 44)], 11)
     got_x1 = fetch(x1_in.at[pl.ds(4, 40)], x1.at[pl.ds(20, 40)], 12)
     fill_mask(grid_rows // 4, grid_cols // 4, mask)
+    gw[:, 0:8, :] = jnp.zeros((4, 8, 128), F32)
+    gw[:, 1160:1168, :] = jnp.zeros((4, 8, 128), F32)
     scale, shift = modulation(noise, noise_index)
     for copy in got_rims:
         copy.wait()
@@ -458,7 +474,7 @@
 
     first(0)
     first(1)
-    for copy in got_edges:
+    for copy in (*got_edges, got_w1t):
         copy.wait()
     z0[...] = dot(0)
     first(2)
@@ -504,7 +520,7 @@
     pipeline(6, lambda t: product(around(x2, 2 + 6 * t, 6, slice(0, 512)), w2t[...]), conv_two_post, z0, z1)
 
     cp[...] = jnp.zeros_like(cp)
-    for copy in got_sides:
+    for copy in (*got_sides, got_cot):
         copy.wait()
     for h in range(2):
         lanes = slice(h * 128, (h + 1) * 128)
@@ -577,7 +593,8 @@
             both = [(base + z[i * KW : i * KW + KP, q * 128 : (q + 1) * 128]) * keep for q in range(2)]
             for r in range(2):
                 row = 2 * m + r
-                planes = [both[p // 2] * d1[row, :, p * 128 : (p + 1) * 128] for p in range(4)]
+                slopes = [d1[row, :, p * 128 : (p + 1) * 128].astype(F32)[:KP] for p in range(4)]
+                planes = [both[p // 2] * slopes[p] for p in range(4)]
                 for n, line in enumerate([before(planes[3])] + planes + [after(planes[0])]):
                     g1[row - 12, :, n * 128 : (n + 1) * 128] = line[:KO].astype(BF16)
 
@@ -592,12 +609,7 @@
             for v in range(3):
                 left = (4 * u + v) * 128
                 term = acc[0:128, left : left + 128] + acc[128:256, left + 128 : left + 256]
-                gw[at, pl.ds((3 * u + v) * 128, 128), :] = term.T
-
-    def nines(t):
-        for owner in range(128):
-            at = owner * 40 + t * 9
-            ms[at : at + 9, :] = gw[t, owner * 9 : owner * 9 + 9, :]
+                gw[at, pl.ds(8 + (3 * u + v) * 128, 128), :] = term.T
 
     def one_chunk(t):
         grads = jnp.concatenate(
@@ -613,25 +625,26 @@
     acc[...] = one_chunk(0)
     for tap in range(9):
         turned = acc3[:, tap * 128 : (tap + 1) * 128].T
-        gw[2, pl.ds(tap * 128, 128), :] = turned[:, 0:128]
-        gw[3, pl.ds(tap * 128, 128), :] = turned[:, 128:256]
-    nines(1)
+        gw[2, pl.ds(8 + tap * 128, 128), :] = turned[:, 0:128]
+        gw[3, pl.ds(8 + tap * 128, 128), :] = turned[:, 128:256]
     acc[...] += one_chunk(1)
-    nines(2)
-    nines(3)
     acc[...] += one_chunk(2)
+    fold_weights(0)
+    line = lax.broadcasted_iota(jnp.int32, (8, 128), 0)
+    none = jnp.zeros((8, 128), F32)
     for owner in range(128):
-        ms[owner * 40 + 36 : owner * 40 + 40, :] = jnp.zeros((4, 128), F32)
-    fold_weights(0)
-    nines(0)
-
-    def msg_step(n, _):
-        rows = pl.ds(pl.multiple_of(n * 320, 320), 320)
-        keep_msg[rows, :] = ms[pl.ds(pl.multiple_of((2 * n + core) * 320, 320), 320), :].astype(BF16)
-        give_msg[rows, :] = ms[pl.ds(pl.multiple_of((2 * n + 1 - core) * 320, 320), 320), :].astype(BF16)
-        return 0
-
-    lax.fori_loop(0, 8, msg_step, 0)
+        at = 8 + 9 * owner
+        parts = [gw[0, at : at + 8, :]]
+        for t in range(1, 5):
+            rest = gw[t - 1, at + 9 - t : at + 17 - t, :]
+            start = gw[t, at - t : at + 8 - t, :] if t < 4 else none
+            parts.append(jnp.where(line < t, rest, start))
+        row, col = divmod(owner, 8)
+        msg[row % 2, (row // 2) * 8 + col] = jnp.concatenate(parts, axis=0).astype(BF16)
+    put_keep = fetch(msg.at[core], keep_out, 2)
+    put_give = fetch(msg.at[1 - core], give_out, 3)
+    put_keep.wait()
+    put_give.wait()
     put_coarse.wait()
     put_g1.wait()
 
@@ -646,16 +659,16 @@
         out_shape=[
             jax.ShapeDtypeStruct((12, KO, 256), BF16),
             jax.ShapeDtypeStruct((50, KO, 768), BF16),
-            jax.ShapeDtypeStruct((2560, 128), BF16),
-            jax.ShapeDtypeStruct((2560, 128), BF16),
+            jax.ShapeDtypeStruct((64, 40, 128), BF16),
+            jax.ShapeDtypeStruct((64, 40, 128), BF16),
         ],
-        in_specs=[smem_spec()] + [vmem_spec()] * 5 + [any_spec()] * 11,
-        out_specs=[any_spec(), any_spec(), vmem_spec(), vmem_spec()],
+        in_specs=[smem_spec()] + [vmem_spec()] * 3 + [any_spec()] * 13,
+        out_specs=[any_spec()] * 4,
         scratch_shapes=[
             vm((2, HALO + 1, 10, 16, 128), BF16),
             vm((4, 160, 128), F32),
             vm((PAD_ROWS, KW, 768), BF16),
-            vm((PAD_ROWS, KP, 512), F32),
+            vm((PAD_ROWS, KW, 512), BF16),
             vm((PAIRS, KW, 512), BF16),
             vm((PAIRS, KP, 256), F32),
             vm((LOWS, KW, 384), BF16),
@@ -669,16 +682,18 @@
             vm((16, KO, 256), BF16),
             vm((256, 1536), F32),
             vm((256, 1152), F32),
-            vm((4, 1152, 128), F32),
-            vm((5120, 128), F32),
+            vm((4, 1168, 128), F32),
+            vm((2, 64, 40, 128), BF16),
             vm((LOWS, KP, 128), F32),
             vm((8 * KW, 256), F32),
             vm((8 * KW, 256), F32),
+            vm((12, KO, 256), BF16),
+            vm((1536, 256), BF16),
             vm((1536, 256), BF16),
             vm((256, 1536), BF16),
             vm((1152, 256), BF16),
             vm((128, 2304), BF16),
-            pltpu.SemaphoreType.DMA((13,)),
+            pltpu.SemaphoreType.DMA((15,)),
         ],
         compiler_params=pltpu.CompilerParams(vmem_limit_bytes=VMEM_LIMIT),
         name="encoder_levels",
@@ -724,11 +739,14 @@
 
 
 def add(keep, other):
+    block = pl.BlockSpec((16, 40, 128), lambda i: (i, 0, 0))
     return pl.pallas_call(
         add_kernel,
+        grid=(4,),
         out_shape=jax.ShapeDtypeStruct(keep.shape, BF16),
-        in_specs=[vmem_spec()] * 2,
-        out_specs=vmem_spec(),
+        in_specs=[block] * 2,
+        out_specs=block,
+        compiler_params=pltpu.CompilerParams(vmem_limit_bytes=VMEM_LIMIT),
         name="add_core_terms",
     )(keep, other)
 
@@ -750,19 +768,19 @@
     grid = (lax.axis_size(ROW_AXES) * ROWS, lax.axis_size("tx") * 4 * KO)
     inputs = inputs.reshape(ROWS, 8, 16, 128)
     one, two, cots = sides(inputs, cotangent)
+    two = swapped(two, "tx", True)
     one = swapped(one, "tx", False)
-    two = swapped(two, "tx", True)
     w1t, w1b, w2t, w2b, w3b, rows_sc, cols_sc = prep(*grid, anchor, weight_one, weight_two, weight_three, frequency)
     off, near = rims(inputs, cots, one, two, rows_sc)
     off = swapped(off, ROW_AXES, True)
     near = lax.ppermute(near, "core", [(0, 1), (1, 0)])
-    x1, d1, x2 = own_rows(*grid, noise_index, inputs, one, two, w1t, rows_sc, cols_sc, noise_table)
+    x1, d1, x2 = own_rows(*grid, noise_index, rows_sc, cols_sc, noise_table, inputs, one, two, w1t)
     coarse, g1, keep_msg, give_msg = levels(
-        *grid, noise_index, cotangent, w1t, rows_sc, cols_sc, noise_table,
+        *grid, noise_index, rows_sc, cols_sc, noise_table, cotangent, w1t,
         off, near, one, two, w2t, w2b, weight_three, w3b, x1, d1, x2,
     )
     other = lax.ppermute(give_msg, "core", [(0, 1), (1, 0)])
-    msg = add(keep_msg, other).reshape(64, 40, 128)
+    msg = add(keep_msg, other)
     got = lax.all_to_all(msg, ("chip", "tx"), 0, 0, tiled=True)
     grad_inputs = input_grad(g1, w1b)
     return (coarse, grad_inputs, *collect(got))

time: 86.7 us -> 87.4 us (level)
    pallas_call x1, Pallas kernels: 2.27 us -> 3.43 us  [add(): pl.pallas_call(add_kernel, grid=(4,), out_shape=jax.ShapeDtypeStruct(keep...]
  transfers between devices with their start and end apart: 6 -> 6, of which waited for: 3 -> 3; matrix products, arithmetic and copies ran while one was open for 0% -> 0% of each run, Pallas kernels for 23% -> 22%
where the time goes in v3:
time: 87.4 us; the launch traced here: 86.9 us
  Pallas kernels  47.7 us (55%)
  starting transfers between devices  22.1 us (25%)
  waiting for transfers between devices  11.8 us (14%)
  local copies, waits for them, and re-layouts  3.28 us (4%)
  between operations  1.39 us (2%)
    pallas_call x1, Pallas kernels, levels(): pl.pallas_call(kernel, out_shape=[jax.ShapeDtypeStruct((12, KO, 256), BF1...  19.7 us
    all_to_all x1, starting transfers between devices, body(): got = lax.all_to_all(msg, ('chip', 'tx'), 0, 0, tiled=True)  15.7 us
    pallas_call x1, Pallas kernels, own_rows(): pl.pallas_call(kernel, out_shape=[shape((48, KW, 768), BF16), shape((44,...  8.89 us
    all_to_all x1, waiting for transfers between devices, body(): got = lax.all_to_all(msg, ('chip', 'tx'), 0, 0, tiled=True)  8.11 us
    pallas_call x1, Pallas kernels, input_grad(): pl.pallas_call(input_kernel, grid=(6,), out_shape=jax.ShapeDtypeStruct((R...  6.93 us
    pallas_call x1, Pallas kernels, prep(): pl.pallas_call(kernel, out_shape=[shape((1536, 256), BF16), shape((256, 1...  3.46 us
    pallas_call x1, Pallas kernels, add(): pl.pallas_call(add_kernel, grid=(4,), out_shape=jax.ShapeDtypeStruct(keep...  3.43 us
    ppermute x1, starting transfers between devices, body(): near = lax.ppermute(near, 'core', [(0, 1), (1, 0)])  3.22 us
  transfers between devices with their start and end apart: 6, of which 3 were waited for; matrix products, arithmetic and copies ran while one was open for 0% of the time, Pallas kernels for 22%

profile of v3, /device:TPU:0, one launch (start us, length us, event | category | flops | bytes accessed | tf_op | source)
XLA Modules:
  0.0 86.9 jit_solution(1745641219468719986)
XLA Ops:
  0.6 2.8 %pack_columns.1 = (bf16[52,16,128]{2,1,0:T(8,128)(2,1)}, bf16[52,16,128]{2,1,0:T(8,128)(2,1)}, bf16[2,8,16,128]{3,2,1,0:T(8,128)(2,1)}) custom-call(bf16[48,8,16,128]{3,2,1,0:T(8,128)(2,1)} %bitcast.1, bf16[12,32,256]{2,1,0:T(8,128)(2,1)} %refs_4_.3), custom_call_target="tpu_custom_call" | custom-call | tf_op jit(solution)/shard_map/pack_columns/pallas_call | solution.py:71
  3.4 1.7 %collective-permute-start = (bf16[52,16,128]{2,1,0:T(8,128)(2,1)}, bf16[52,16,128]{2,1,0:T(8,128)(2,1)S(1)}, u32[]{:S(2)}, u32[]{:S(2)}) collective-permute-start(bf16[52,16,128]{2,1,0:T(8,128)(2,1)} %get-tuple-element.28), channel_id=1, source_target_pairs={{0,1},{1,0},{2,3},{3,2},{4,5},{5,4},{6,7},{7,6},{8,9},{9,8},{10,11... | collective-permute-start | bytes 638984 | tf_op jit(solution)/shard_map/ppermute | solution.py:764
  5.0 0.7 collective-permute-start.1
  5.7 3.5 %weight_forms.1 = (bf16[1536,256]{1,0:T(8,128)(2,1)}, bf16[256,1536]{1,0:T(8,128)(2,1)}, bf16[1536,256]{1,0:T(8,128)(2,1)}, bf16[256,1536]{1,0:T(8,128)(2,1)}, b...) custom-call(s32[2]{0:T(128)} %refs_0_.3, bf16[1152,128]{1,0:T(8,128)(2,1)} %refs_1_.1, ...), custom_call_target="tpu_custom_call" | custom-call | tf_op jit(solution)/shard_map/weight_forms/pallas_call | solution.py:163
  9.2 1.3 %collective-permute-done.one.refs_5_.refs_8_ = bf16[52,16,128]{2,1,0:T(8,128)(2,1)S(1)} collective-permute-done((bf16[52,16,128]{2,1,0:T(8,128)(2,1)}, bf16[52,16,128]{2,1,0:T(8,128)(2,1)S(1)}, u32[]{:S(2)}, u32[]{:S(2)}) %collective-permute-start) | collective-permute-done | bytes 213024 | tf_op jit(solution)/shard_map/ppermute | solution.py:764
  10.5 0.0 copy-start
  10.5 0.0 collective-permute-done.1.two.refs_6_.refs_9_
  10.5 0.0 copy-start.1
  10.5 0.7 copy-done
  11.2 0.1 copy-done.1
  11.3 2.5 %pack_rows.1 = (bf16[17,10,16,128]{3,2,1,0:T(8,128)(2,1)}, bf16[17,10,16,128]{3,2,1,0:T(8,128)(2,1)}) custom-call(bf16[48,8,16,128]{3,2,1,0:T(8,128)(2,1)} %bitcast.2, bf16[2,8,16,128]{3,2,1,0:T(8,128)(2,1)} %get-tuple-element.27.cots, bf16[52,16,128]{2,1,0:T(8,128)(2,1)} %copy-done, bf16[52,16,128]{2,1,0:T(8,128)(2,1)} %copy-done.1, ...), custom_call_target="tpu_custom_call" | custom-call | tf_op jit(solution)/shard_map/pack_rows/pallas_call | solution.py:104
  13.8 0.7 collective-permute-start.2
  14.5 3.2 %collective-permute-start.3 = (bf16[17,10,16,128]{3,2,1,0:T(8,128)(2,1)}, bf16[17,10,16,128]{3,2,1,0:T(8,128)(2,1)S(1)}, u32[]{:S(2)}, u32[]{:S(2)}) collective-permute-start(bf16[17,10,16,128]{3,2,1,0:T(8,128)(2,1)} %get-tuple-element.31), channel_id=1, source_target_pairs={{0,8},{8,0},{1,9},{9,1},{2,10},{10,2},{3,11},{11,3},{4,12},{12,4},... | collective-permute-start | bytes 2088968 | tf_op jit(solution)/shard_map/ppermute | solution.py:776
  18.4 8.9 %own_rows.1 = (bf16[48,48,768]{2,1,0:T(8,128)(2,1)}, bf16[44,48,512]{2,1,0:T(8,128)(2,1)}, bf16[22,48,512]{2,1,0:T(8,128)(2,1)}) custom-call(s32[1]{0:T(128)S(6)} %copy.14.refs_0_, f32[2,80,128]{2,1,0:T(8,128)} %get-tuple-element.24._.refs_1_, f32[2,4,40,128]{3,2,1,0:T(8,128)} %get-tuple-element.25.refs_2_, f32[64,256]{1,0:T(8,128)} %refs_3_.5, ...), custom_call_target="tpu_custom_call" | custom-call | flops 4000000000 | bytes 30000000 | tf_op jit(solution)/shard_map/own_rows/pallas_call | solution.py:392
  27.3 0.0 collective-permute-done.2.refs_6_
  27.3 0.0 copy-start.2
  27.3 0.0 collective-permute-done.3.refs_7_
  27.3 0.0 copy-start.3
  27.3 0.8 copy-done.2
  28.1 0.2 copy-done.3
  28.4 19.7 %encoder_levels.1 = (bf16[12,32,256]{2,1,0:T(8,128)(2,1)}, bf16[50,32,768]{2,1,0:T(8,128)(2,1)}, bf16[64,40,128]{2,1,0:T(8,128)(2,1)}, bf16[64,40,128]{2,1,0:T(8,128)(2,1)}) custom-call(s32[1]{0:T(128)S(6)} %copy.14.refs_0_, f32[2,80,128]{2,1,0:T(8,128)} %get-tuple-element.24._.refs_1_, f32[2,4,40,128]{3,2,1,0:T(8,128)} %get-tuple-element.25.refs_2_, ...), custom_call_target="tpu_custom_call" | custom-call | tf_op jit(solution)/shard_map/encoder_levels/pallas_call | solution.py:657
  48.1 0.1 collective-permute-start.4
  48.2 2.3 %collective-permute-done.4.other = bf16[64,40,128]{2,1,0:T(8,128)(2,1)S(1)} collective-permute-done((bf16[64,40,128]{2,1,0:T(8,128)(2,1)}, bf16[64,40,128]{2,1,0:T(8,128)(2,1)S(1)}, u32[]{:S(2)}, u32[]{:S(2)}) %collective-permute-start.4) | collective-permute-done | bytes 655392 | tf_op jit(solution)/shard_map/ppermute | solution.py:782
  50.5 0.0 copy-start.4
  50.5 0.8 copy-done.4
  51.3 3.4 %add_core_terms.1 = bf16[64,40,128]{2,1,0:T(8,128)(2,1)} custom-call(bf16[64,40,128]{2,1,0:T(8,128)(2,1)} %get-tuple-element.41.keep, bf16[64,40,128]{2,1,0:T(8,128)(2,1)} %copy-done.4), custom_call_target="tpu_custom_call" | custom-call | tf_op jit(solution)/shard_map/add_core_terms/pallas_call | solution.py:743
  54.7 15.7 %all-to-all-start = ((bf16[64,40,128]{2,1,0:T(8,128)(2,1)}), bf16[64,40,128]{2,1,0:T(8,128)(2,1)S(1)}, u32[]{:S(2)}, u32[]{:S(2)}) async-start(bf16[64,40,128]{2,1,0:T(8,128)(2,1)} %add_core_terms.1), calls=%async_computation | async-start | bytes 1310720 | tf_op jit(solution)/shard_map/all_to_all | solution.py:784
  70.5 6.9 %input_grad.1 = bf16[48,128,128]{2,1,0:T(8,128)(2,1)} custom-call(bf16[50,32,768]{2,1,0:T(8,128)(2,1)} %get-tuple-element.39.g1.g1_next, bf16[50,32,768]{2,1,0:T(8,128)(2,1)} %get-tuple-element.39.g1.g1_next, bf16[256,1536]{1,0:T(8,128)(2,1)} %get-tuple-element.40.w1b), custom_call_target="tpu_custom_call" | custom-call | flops 1811939328 | bytes 8388608 | tf_op jit(solution)/shard_map/input_grad/pallas_call | solution.py:720
  77.4 8.1 %all-to-all-done = bf16[64,40,128]{2,1,0:T(8,128)(2,1)S(1)} async-done(((bf16[64,40,128]{2,1,0:T(8,128)(2,1)}), bf16[64,40,128]{2,1,0:T(8,128)(2,1)S(1)}, u32[]{:S(2)}, u32[]{:S(2)}) %all-to-all-start) | async-done | bytes 655392 | tf_op jit(solution)/shard_map/all_to_all | solution.py:784
  85.5 0.1 convert_reduce_fusion
  85.6 0.6 fusion
  86.3 0.6 pad_maximum_fusion
Async XLA Ops:
  3.4 7.1 %collective-permute-start = (bf16[52,16,128]{2,1,0:T(8,128)(2,1)}, bf16[52,16,128]{2,1,0:T(8,128)(2,1)S(1)}, u32[]{:S(2)}, u32[]{:S(2)}) collective-permute-start(bf16[52,16,128]{2,1,0:T(8,128)(2,1)} %get-tuple-element.28), channel_id=1, source_target_pairs={{0,1},{1,0},{2,3},{3,2},{4,5},{5,4},{6,7},{7,6},{8,9},{9,8},{10,11... | collective-permute-start | bytes 638984 | tf_op jit(solution)/shard_map/ppermute | solution.py:764
  5.0 5.5 %collective-permute-start.1 = (bf16[52,16,128]{2,1,0:T(8,128)(2,1)}, bf16[52,16,128]{2,1,0:T(8,128)(2,1)S(1)}, u32[]{:S(2)}, u32[]{:S(2)}) collective-permute-start(bf16[52,16,128]{2,1,0:T(8,128)(2,1)} %get-tuple-element.29), channel_id=1, source_target_pairs={{1,2},{2,1},{3,4},{4,3},{5,6},{6,5},{9,10},{10,9},{11,12},{12,11},... | collective-permute-start | bytes 638984 | tf_op jit(solution)/shard_map/ppermute | solution.py:764
  10.5 0.7 copy-start
  10.5 0.8 copy-start.1
  13.8 13.5 %collective-permute-start.2 = (bf16[17,10,16,128]{3,2,1,0:T(8,128)(2,1)}, bf16[17,10,16,128]{3,2,1,0:T(8,128)(2,1)S(1)}, u32[]{:S(2)}, u32[]{:S(2)}) collective-permute-start(bf16[17,10,16,128]{3,2,1,0:T(8,128)(2,1)} %get-tuple-element.30), channel_id=1, source_target_pairs={{8,16},{16,8},{24,32},{32,24},{40,48},{48,40},{56,64},{64,56},{72,... | collective-permute-start | bytes 2088968 | tf_op jit(solution)/shard_map/ppermute | solution.py:764
  14.5 12.8 %collective-permute-start.3 = (bf16[17,10,16,128]{3,2,1,0:T(8,128)(2,1)}, bf16[17,10,16,128]{3,2,1,0:T(8,128)(2,1)S(1)}, u32[]{:S(2)}, u32[]{:S(2)}) collective-permute-start(bf16[17,10,16,128]{3,2,1,0:T(8,128)(2,1)} %get-tuple-element.31), channel_id=1, source_target_pairs={{0,8},{8,0},{1,9},{9,1},{2,10},{10,2},{3,11},{11,3},{4,12},{12,4},... | collective-permute-start | bytes 2088968 | tf_op jit(solution)/shard_map/ppermute | solution.py:776
  27.3 0.9 copy-start.2
  27.3 1.1 %copy-start.3 = (bf16[17,10,16,128]{3,2,1,0:T(8,128)(2,1)}, bf16[17,10,16,128]{3,2,1,0:T(8,128)(2,1)S(1)}, u32[]{:S(2)}) copy-start(bf16[17,10,16,128]{3,2,1,0:T(8,128)(2,1)S(1)} %collective-permute-done.3.refs_7_) | copy-start | bytes 2088964
  48.1 2.4 %collective-permute-start.4 = (bf16[64,40,128]{2,1,0:T(8,128)(2,1)}, bf16[64,40,128]{2,1,0:T(8,128)(2,1)S(1)}, u32[]{:S(2)}, u32[]{:S(2)}) collective-permute-start(bf16[64,40,128]{2,1,0:T(8,128)(2,1)} %get-tuple-element.42), channel_id=1, source_target_pairs={{0,8},{8,0},{1,9},{9,1},{2,10},{10,2},{3,11},{11,3},{4,12},{12,4},... | collective-permute-start | bytes 1966088 | tf_op jit(solution)/shard_map/ppermute | solution.py:782
  50.5 0.8 copy-start.4
  54.7 30.8 %all-to-all-start = ((bf16[64,40,128]{2,1,0:T(8,128)(2,1)}), bf16[64,40,128]{2,1,0:T(8,128)(2,1)S(1)}, u32[]{:S(2)}, u32[]{:S(2)}) async-start(bf16[64,40,128]{2,1,0:T(8,128)(2,1)} %add_core_terms.1), calls=%async_computation | async-start | bytes 1310720 | tf_op jit(solution)/shard_map/all_to_all | solution.py:784

commit v4 on v3

--- a/solution.py
+++ b/solution.py
@@ -16,7 +16,7 @@
 PAD_ROWS = ROWS + 2 * HALO
 PAIRS = PAD_ROWS // 2
 LOWS = PAIRS // 2
-VMEM_LIMIT = 60 * 1024 * 1024
+MIB = 1024 * 1024
 
 
 def any_spec():
@@ -74,7 +74,7 @@
         in_specs=[any_spec(), vmem_spec()],
         out_specs=[vmem_spec()] * 3,
         scratch_shapes=[pltpu.VMEM((48, 128), F32), pltpu.SemaphoreType.DMA((2,))],
-        compiler_params=pltpu.CompilerParams(vmem_limit_bytes=VMEM_LIMIT),
+        compiler_params=pltpu.CompilerParams(vmem_limit_bytes=8 * MIB),
         name="pack_columns",
     )(inputs, cot)
 
@@ -107,7 +107,7 @@
         in_specs=[any_spec()] * len(args),
         out_specs=[vmem_spec()] * 2,
         scratch_shapes=[pltpu.SemaphoreType.DMA((12,))],
-        compiler_params=pltpu.CompilerParams(vmem_limit_bytes=VMEM_LIMIT),
+        compiler_params=pltpu.CompilerParams(vmem_limit_bytes=8 * MIB),
         name="pack_rows",
     )(*args)
 
@@ -173,7 +173,7 @@
         ],
         in_specs=[smem_spec()] + [vmem_spec()] * 4,
         out_specs=[vmem_spec()] * 7,
-        compiler_params=pltpu.CompilerParams(vmem_limit_bytes=VMEM_LIMIT),
+        compiler_params=pltpu.CompilerParams(vmem_limit_bytes=12 * MIB),
         name="weight_forms",
     )(anchor, w1, w2, w3, frequency)
 
@@ -340,8 +340,6 @@
             return flat(inputs[row]), side[1, 1 + row], side[0, 1 + row]
 
         first_lines(load, HALO + 4 * q, 4 * q, (rows_sc, cols_sc), stage, x1)
-        part = pl.ds(4 * q, 4)
-        pltpu.make_async_copy(x1.at[part], x1_out.at[part], sems.at[2]).start()
 
     def dot(t):
         return conv_one_dot(x1, 4 * t + 2, w1t)
@@ -349,38 +347,29 @@
     def post(t, z):
         keeps = [mask[(9 + 2 * t) // 2], mask[(10 + 2 * t) // 2]]
         conv_one_post(z, scale, shift, keeps, d1, 4 * t, x2, 2 * t)
-        part = pl.ds(4 * t, 4)
-        pltpu.make_async_copy(d1.at[part], d1_out.at[part], sems.at[3]).start()
 
     first(0)
     first(1)
     got_w1t.wait()
-    z0[...] = dot(0)
-    first(2)
     late.wait()
-
-    def two_steps(i, _):
-        t = 2 * i + 1
-        z1[...] = dot(t)
-        first(t + 2)
-        post(t - 1, z0)
-        z0[...] = dot(t + 1)
-        first(t + 3)
-        post(t, z1)
-        return 0
-
-    lax.fori_loop(0, 4, two_steps, 0)
-    z1[...] = dot(9)
-    first(11)
-    post(8, z0)
-    z0[...] = dot(10)
-    post(9, z1)
+    z = (z0, z1)
+    for t in range(11):
+        z[t % 2][...] = dot(t)
+        if t + 2 < 12:
+            first(t + 2)
+        if t > 0:
+            post(t - 1, z[(t - 1) % 2])
+        if t == 9:
+            put_x1 = pltpu.make_async_copy(x1, x1_out, sems.at[2])
+            put_x1.start()
     post(10, z0)
-    last = pltpu.make_async_copy(x2, x2_out, sems.at[4])
-    last.start()
-    pltpu.make_async_copy(x1, x1_out, sems.at[2]).wait()
-    pltpu.make_async_copy(d1, d1_out, sems.at[3]).wait()
-    last.wait()
+    put_d1 = pltpu.make_async_copy(d1, d1_out, sems.at[3])
+    put_x2 = pltpu.make_async_copy(x2, x2_out, sems.at[4])
+    put_d1.start()
+    put_x2.start()
+    put_x1.wait()
+    put_d1.wait()
+    put_x2.wait()
 
 
 def own_rows(grid_rows, grid_cols, *args):
@@ -407,7 +396,7 @@
             vm((8 * KW, 256), F32),
             pltpu.SemaphoreType.DMA((8,)),
         ],
-        compiler_params=pltpu.CompilerParams(vmem_limit_bytes=VMEM_LIMIT),
+        compiler_params=pltpu.CompilerParams(vmem_limit_bytes=18 * MIB),
         cost_estimate=pl.CostEstimate(flops=4 * 10**9, bytes_accessed=30 * 10**6, transcendentals=0),
         name="own_rows",
     )(*args)
@@ -452,8 +441,7 @@
         copy.wait()
 
     def first(n):
-        below = n // 4
-        start = 4 * (n % 4)
+        below, start = n // 4, 4 * (n % 4)
         base = start + (HALO + ROWS) * below
 
         def load(i):
@@ -463,7 +451,7 @@
         first_lines(load, base, base, (rows_sc, cols_sc), stage, x1)
 
     def mid_of(t):
-        return jnp.where(t < 4, 1 + 2 * t, 23 + 2 * t)
+        return 1 + 2 * t if t < 4 else 23 + 2 * t
 
     def dot(t):
         return conv_one_dot(x1, 2 * mid_of(t), w1t)
@@ -476,27 +464,13 @@
     first(1)
     for copy in (*got_edges, got_w1t):
         copy.wait()
-    z0[...] = dot(0)
-    first(2)
-
-    def two_steps(i, _):
-        t = 2 * i + 1
-        z1[...] = dot(t)
-        first(t + 2)
-        post(t - 1, z0)
-        z0[...] = dot(t + 1)
-        first(t + 3)
-        post(t, z1)
-        return 0
-
-    lax.fori_loop(0, 2, two_steps, 0)
-    z1[...] = dot(5)
-    first(7)
-    post(4, z0)
-    z0[...] = dot(6)
-    post(5, z1)
-    z1[...] = dot(7)
-    post(6, z0)
+    z = (z0, z1)
+    for t in range(8):
+        z[t % 2][...] = dot(t)
+        if t + 2 < 8:
+            first(t + 2)
+        if t > 0:
+            post(t - 1, z[(t - 1) % 2])
     post(7, z1)
     got_x2.wait()
     got_w2t.wait()
@@ -695,7 +669,7 @@
             vm((128, 2304), BF16),
             pltpu.SemaphoreType.DMA((15,)),
         ],
-        compiler_params=pltpu.CompilerParams(vmem_limit_bytes=VMEM_LIMIT),
+        compiler_params=pltpu.CompilerParams(vmem_limit_bytes=46 * MIB),
         name="encoder_levels",
     )(*args)
 
@@ -728,27 +702,10 @@
         ],
         out_specs=pl.BlockSpec((8, 128, 128), lambda i: (i, 0, 0)),
         scratch_shapes=[pltpu.VMEM((8, 128, 128), F32)],
-        compiler_params=pltpu.CompilerParams(vmem_limit_bytes=VMEM_LIMIT),
+        compiler_params=pltpu.CompilerParams(vmem_limit_bytes=16 * MIB),
         cost_estimate=pl.CostEstimate(flops=2 * 6144 * 1152 * 128, bytes_accessed=8 * 1024 * 1024, transcendentals=0),
         name="input_grad",
     )(g1, g1, w1b)
-
-
-def add_kernel(keep, other, out):
-    out[...] = (keep[...].astype(F32) + other[...].astype(F32)).astype(BF16)
-
-
-def add(keep, other):
-    block = pl.BlockSpec((16, 40, 128), lambda i: (i, 0, 0))
-    return pl.pallas_call(
-        add_kernel,
-        grid=(4,),
-        out_shape=jax.ShapeDtypeStruct(keep.shape, BF16),
-        in_specs=[block] * 2,
-        out_specs=block,
-        compiler_params=pltpu.CompilerParams(vmem_limit_bytes=VMEM_LIMIT),
-        name="add_core_terms",
-    )(keep, other)
 
 
 def collect(got):
@@ -780,7 +737,7 @@
         off, near, one, two, w2t, w2b, weight_three, w3b, x1, d1, x2,
     )
     other = lax.ppermute(give_msg, "core", [(0, 1), (1, 0)])
-    msg = add(keep_msg, other)
+    msg = (keep_msg.astype(F32) + other.astype(F32)).astype(BF16)
     got = lax.all_to_all(msg, ("chip", "tx"), 0, 0, tiled=True)
     grad_inputs = input_grad(g1, w1b)
     return (coarse, grad_inputs, *collect(got))

time: 87.4 us -> 79.2 us (0.906)
  Pallas kernels: 47.7 us -> 31.1 us
  local copies, waits for them, and re-layouts: 3.28 us -> 9.07 us
  other arithmetic: 0.73 us -> 2.84 us
    unnamed x10 -> x28, local copies, waits for them, and re-layouts: 2.67 us -> 8.46 us
    pallas_call x1 -> x0, Pallas kernels: 3.43 us -> none  [add(): pl.pallas_call(add_kernel, grid=(4,), out_shape=jax.ShapeDtypeStruct(keep...]
    pallas_call x1, Pallas kernels: 2.75 us -> 0.11 us  [sides(): pl.pallas_call(side_kernel, out_shape=[jax.ShapeDtypeStruct((ROWS + 4, 16...]
    pallas_call x1, Pallas kernels: 19.7 us -> 17.2 us  [levels(): pl.pallas_call(kernel, out_shape=[jax.ShapeDtypeStruct((12, KO, 256), BF1...]
    pallas_call x1, Pallas kernels: 6.93 us -> 4.64 us  [input_grad(): pl.pallas_call(input_kernel, grid=(6,), out_shape=jax.ShapeDtypeStruct((R...]
    pallas_call x1, Pallas kernels: 2.51 us -> 0.33 us  [rims(): pl.pallas_call(rim_kernel, out_shape=[jax.ShapeDtypeStruct((HALO + 1, 10,...]
    all_to_all x1, waiting for transfers between devices: 8.11 us -> 10.3 us  [body(): got = lax.all_to_all(msg, ('chip', 'tx'), 0, 0, tiled=True)]
    pallas_call x1, Pallas kernels: 3.46 us -> 1.46 us  [prep(): pl.pallas_call(kernel, out_shape=[shape((1536, 256), BF16), shape((256, 1...]
  transfers between devices with their start and end apart: 6 -> 6, of which waited for: 3 -> 3; matrix products, arithmetic and copies ran while one was open for 0% -> 0% of each run, Pallas kernels for 22% -> 17%
where the time goes in v4:
time: 79.2 us; the launch traced here: 78.7 us
  Pallas kernels  31.1 us (39%)
  starting transfers between devices  21.8 us (28%)
  waiting for transfers between devices  12.5 us (16%)
  local copies, waits for them, and re-layouts  9.07 us (11%)
  other arithmetic  2.84 us (4%)
  between operations  1.46 us (2%)
    pallas_call x1, Pallas kernels, levels(): pl.pallas_call(kernel, out_shape=[jax.ShapeDtypeStruct((12, KO, 256), BF1...  17.2 us
    all_to_all x1, starting transfers between devices, body(): got = lax.all_to_all(msg, ('chip', 'tx'), 0, 0, tiled=True)  15.5 us
    all_to_all x1, waiting for transfers between devices, body(): got = lax.all_to_all(msg, ('chip', 'tx'), 0, 0, tiled=True)  10.3 us
    unnamed x28, local copies, waits for them, and re-layouts  8.46 us
    pallas_call x1, Pallas kernels, own_rows(): pl.pallas_call(kernel, out_shape=[shape((48, KW, 768), BF16), shape((44,...  7.34 us
    pallas_call x1, Pallas kernels, input_grad(): pl.pallas_call(input_kernel, grid=(6,), out_shape=jax.ShapeDtypeStruct((R...  4.64 us
    ppermute x1, starting transfers between devices, body(): near = lax.ppermute(near, 'core', [(0, 1), (1, 0)])  3.22 us
    ppermute x3, starting transfers between devices, swapped(): return lax.ppermute(block, axis, pairs)  3.02 us
  transfers between devices with their start and end apart: 6, of which 3 were waited for; matrix products, arithmetic and copies ran while one was open for 0% of the time, Pallas kernels for 17%

profile of v4, /device:TPU:0, one launch (start us, length us, event | category | flops | bytes accessed | tf_op | source)
XLA Modules:
  0.0 78.7 jit_solution(6004013153616530302)
XLA Ops:
  0.7 1.4 %copy-done.1 = bf16[48,128,128]{2,1,0:T(8,128)(2,1)S(1)} copy-done((bf16[48,128,128]{2,1,0:T(8,128)(2,1)S(1)}, bf16[48,128,128]{2,1,0:T(8,128)(2,1)}, u32[]{:S(2)}) %copy-start.1) | copy-done | bytes 1572888
  2.1 0.9 %copy-done.7 = bf16[12,32,256]{2,1,0:T(8,128)(2,1)S(1)} copy-done((bf16[12,32,256]{2,1,0:T(8,128)(2,1)S(1)}, bf16[12,32,256]{2,1,0:T(8,128)(2,1)}, u32[]{:S(2)}) %copy-start.7) | copy-done | bytes 196632
  3.0 0.1 pack_columns.1
  3.1 1.7 %collective-permute-start = (bf16[52,16,128]{2,1,0:T(8,128)(2,1)S(1)}, bf16[52,16,128]{2,1,0:T(8,128)(2,1)S(1)}, u32[]{:S(2)}, u32[]{:S(2)}) collective-permute-start(bf16[52,16,128]{2,1,0:T(8,128)(2,1)S(1)} %get-tuple-element.28), channel_id=1, source_target_pairs={{0,1},{1,0},{2,3},{3,2},{4,5},{5,4},{6,7},{7,6},{8,9},{9,8},{10,11... | collective-permute-start | bytes 638984 | tf_op jit(solution)/shard_map/ppermute | solution.py:721
  4.8 0.7 collective-permute-start.1
  5.5 0.0 copy-start.4
  5.5 1.1 %copy-done.4 = bf16[1152,256]{1,0:T(8,128)(2,1)S(1)} copy-done((bf16[1152,256]{1,0:T(8,128)(2,1)S(1)}, bf16[1152,256]{1,0:T(8,128)(2,1)}, u32[]{:S(2)}) %copy-start.4) | copy-done | bytes 589848
  6.5 1.0 %copy-done.9 = bf16[1152,128]{1,0:T(8,128)(2,1)S(1)} copy-done((bf16[1152,128]{1,0:T(8,128)(2,1)S(1)}, bf16[1152,128]{1,0:T(8,128)(2,1)}, u32[]{:S(2)}) %copy-start.9) | copy-done | bytes 294936
  7.5 1.0 %copy-done.10 = bf16[1152,128]{1,0:T(8,128)(2,1)S(1)} copy-done((bf16[1152,128]{1,0:T(8,128)(2,1)S(1)}, bf16[1152,128]{1,0:T(8,128)(2,1)}, u32[]{:S(2)}) %copy-start.10) | copy-done | bytes 294936
  8.5 1.5 %weight_forms.1 = (bf16[1536,256]{1,0:T(8,128)(2,1)S(1)}, bf16[256,1536]{1,0:T(8,128)(2,1)S(1)}, bf16[1536,256]{1,0:T(8,128)(2,1)S(1)}, bf16[256,1536]{1,0:T(8,1...) custom-call(s32[2]{0:T(128)S(1)} %copy-done.13, ...), custom_call_target="tpu_custom_call" | custom-call | tf_op jit(solution)/shard_map/weight_forms/pallas_call | solution.py:163
  9.9 0.1 collective-permute-done.one.refs_5_.refs_8_
  10.0 0.0 collective-permute-done.1.two.refs_6_.refs_9_
  10.0 0.3 pack_rows.1
  10.4 0.7 collective-permute-start.2
  11.1 3.2 %collective-permute-start.3 = (bf16[17,10,16,128]{3,2,1,0:T(8,128)(2,1)S(1)}, bf16[17,10,16,128]{3,2,1,0:T(8,128)(2,1)S(1)}, u32[]{:S(2)}, u32[]{:S(2)}) collective-permute-start(bf16[17,10,16,128]{3,2,1,0:T(8,128)(2,1)S(1)} %get-tuple-element.31), channel_id=1, source_target_pairs={{0,8},{8,0},{1,9},{9,1},{2,10},{10,2},{3,11},{11,3},{4,12},{12,4},... | collective-permute-start | bytes 2088968 | tf_op jit(solution)/shard_map/ppermute | solution.py:733
  15.0 0.0 copy-start.5
  15.0 0.0 copy-start.8
  15.0 7.3 %own_rows.1 = (bf16[48,48,768]{2,1,0:T(8,128)(2,1)S(1)}, bf16[44,48,512]{2,1,0:T(8,128)(2,1)S(1)}, bf16[22,48,512]{2,1,0:T(8,128)(2,1)S(1)}) custom-call(s32[1]{0:T(128)S(6)} %copy.14.refs_0_, f32[2,80,128]{2,1,0:T(8,128)S(1)} %get-tuple-element.24._.refs_1_, f32[2,4,40,128]{3,2,1,0:T(8,128)S(1)} %get-tuple-element.25.refs_2_, f32[64,256]{1,0:T(8,128)S(1)} %copy-done.11, ...), custom_call_target="tpu_custom_call" | custom-call | flops 4000000000 | bytes 30000000 | tf_op jit(solution)/shard_map/own_rows/pallas_call | solution.py:381
  22.4 1.7 %copy-done.3 = bf16[48,48,768]{2,1,0:T(8,128)(2,1)} copy-done((bf16[48,48,768]{2,1,0:T(8,128)(2,1)}, bf16[48,48,768]{2,1,0:T(8,128)(2,1)S(1)}, u32[]{:S(2)}) %copy-start.3) | copy-done | bytes 3538968
  24.1 1.4 %copy-done.6 = bf16[44,48,512]{2,1,0:T(8,128)(2,1)} copy-done((bf16[44,48,512]{2,1,0:T(8,128)(2,1)}, bf16[44,48,512]{2,1,0:T(8,128)(2,1)S(1)}, u32[]{:S(2)}) %copy-start.6) | copy-done | bytes 2162712
  25.5 0.0 collective-permute-done.2.refs_6_
  25.5 0.0 collective-permute-done.3.refs_7_
  25.5 17.2 %encoder_levels.1 = (bf16[12,32,256]{2,1,0:T(8,128)(2,1)}, bf16[50,32,768]{2,1,0:T(8,128)(2,1)}, bf16[64,40,128]{2,1,0:T(8,128)(2,1)S(1)}, bf16[64,40,128]{2,1,0:T(8,128)(2,1)S(1)}) custom-call(s32[1]{0:T(128)S(6)} %copy.14.refs_0_, f32[2,80,128]{2,1,0:T(8,128)S(1)} %get-tuple-element.24._.refs_1_, f32[2,4,40,128]{3,2,1,0:T(8,128)S(1)} %get-tuple-element.25.refs_2_, ...), custom_call_target="tpu_custom_call" | custom-call | tf_op jit(solution)/shard_map/encoder_levels/pallas_call | solution.py:631
  42.7 0.1 collective-permute-start.4
  42.8 2.1 %collective-permute-done.4 = bf16[64,40,128]{2,1,0:T(8,128)(2,1)S(1)} collective-permute-done((bf16[64,40,128]{2,1,0:T(8,128)(2,1)S(1)}, bf16[64,40,128]{2,1,0:T(8,128)(2,1)S(1)}, u32[]{:S(2)}, u32[]{:S(2)}) %collective-permute-start.4) | collective-permute-done | bytes 655392 | tf_op jit(solution)/shard_map/ppermute | solution.py:739
  44.9 1.0 %add_convert_fusion = bf16[64,40,128]{2,1,0:T(8,128)(2,1)} fusion(bf16[64,40,128]{2,1,0:T(8,128)(2,1)S(1)} %collective-permute-done.4, bf16[64,40,128]{2,1,0:T(8,128)(2,1)S(1)} %get-tuple-element.41), kind=kLoop, calls=%fused_computation.1 | loop fusion | flops 1310720 | bytes 1966080 | tf_op jit(solution)/shard_map/convert_element_type | solution.py:740
  45.9 15.5 %all-to-all-start = ((bf16[64,40,128]{2,1,0:T(8,128)(2,1)}), bf16[64,40,128]{2,1,0:T(8,128)(2,1)}, u32[]{:S(2)}, u32[]{:S(2)}) async-start(bf16[64,40,128]{2,1,0:T(8,128)(2,1)} %add_convert_fusion), calls=%async_computation | async-start | bytes 1310720 | tf_op jit(solution)/shard_map/all_to_all | solution.py:741
  61.4 4.6 %input_grad.1 = bf16[48,128,128]{2,1,0:T(8,128)(2,1)} custom-call(bf16[50,32,768]{2,1,0:T(8,128)(2,1)S(1)} %copy-done, bf16[50,32,768]{2,1,0:T(8,128)(2,1)S(1)} %copy-done, bf16[256,1536]{1,0:T(8,128)(2,1)S(1)} %get-tuple-element.40.w1b), custom_call_target="tpu_custom_call" | custom-call | flops 1811939328 | bytes 8388608 | tf_op jit(solution)/shard_map/input_grad/pallas_call | solution.py:694
  66.0 10.3 %all-to-all-done = bf16[64,40,128]{2,1,0:T(8,128)(2,1)} async-done(((bf16[64,40,128]{2,1,0:T(8,128)(2,1)}), bf16[64,40,128]{2,1,0:T(8,128)(2,1)}, u32[]{:S(2)}, u32[]{:S(2)}) %all-to-all-start) | async-done | bytes 655392 | tf_op jit(solution)/shard_map/all_to_all | solution.py:741
  76.3 1.2 %convert_reduce_fusion = f32[40,128]{1,0:T(8,128)S(1)} fusion(bf16[64,40,128]{2,1,0:T(8,128)(2,1)} %all-to-all-done), kind=kLoop, calls=%fused_computation | loop fusion | flops 650240 | bytes 675840 | tf_op jit(solution)/shard_map/reduce_sum | solution.py:712
  77.5 0.6 fusion
  78.1 0.6 pad_maximum_fusion
  (18 shorter events, 0.0 us)
Async XLA Ops:
  0.6 4.8 %copy-start.13 = (s32[2]{0:T(128)S(1)}, s32[2]{0:T(128)}, u32[]{:S(2)}) copy-start(s32[2]{0:T(128)} %refs_0_.3) | copy-start | bytes 28
  0.6 4.8 %copy-start.12 = (f32[2,128]{1,0:T(2,128)S(1)}, f32[2,128]{1,0:T(2,128)}, u32[]{:S(2)}) copy-start(f32[2,128]{1,0:T(2,128)} %refs_4_.2) | copy-start | bytes 3076
  0.7 1.4 %copy-start.1 = (bf16[48,128,128]{2,1,0:T(8,128)(2,1)S(1)}, bf16[48,128,128]{2,1,0:T(8,128)(2,1)}, u32[]{:S(2)}) copy-start(bf16[48,128,128]{2,1,0:T(8,128)(2,1)} %param.9) | copy-start | bytes 4718596
  2.1 0.9 %copy-start.7 = (bf16[12,32,256]{2,1,0:T(8,128)(2,1)S(1)}, bf16[12,32,256]{2,1,0:T(8,128)(2,1)}, u32[]{:S(2)}) copy-start(bf16[12,32,256]{2,1,0:T(8,128)(2,1)} %refs_4_.3) | copy-start | bytes 589828
  3.0 7.0 %copy-start.2 = (bf16[48,128,128]{2,1,0:T(8,128)(2,1)S(1)}, bf16[48,128,128]{2,1,0:T(8,128)(2,1)}, u32[]{:S(2)}) copy-start(bf16[48,128,128]{2,1,0:T(8,128)(2,1)} %param.9) | copy-start | bytes 4718596
  3.1 6.9 %collective-permute-start = (bf16[52,16,128]{2,1,0:T(8,128)(2,1)S(1)}, bf16[52,16,128]{2,1,0:T(8,128)(2,1)S(1)}, u32[]{:S(2)}, u32[]{:S(2)}) collective-permute-start(bf16[52,16,128]{2,1,0:T(8,128)(2,1)S(1)} %get-tuple-element.28), channel_id=1, source_target_pairs={{0,1},{1,0},{2,3},{3,2},{4,5},{5,4},{6,7},{7,6},{8,9},{9,8},{10,11... | collective-permute-start | bytes 638984 | tf_op jit(solution)/shard_map/ppermute | solution.py:721
  4.8 5.3 %collective-permute-start.1 = (bf16[52,16,128]{2,1,0:T(8,128)(2,1)S(1)}, bf16[52,16,128]{2,1,0:T(8,128)(2,1)S(1)}, u32[]{:S(2)}, u32[]{:S(2)}) collective-permute-start(bf16[52,16,128]{2,1,0:T(8,128)(2,1)S(1)} %get-tuple-element.29), channel_id=1, source_target_pairs={{1,2},{2,1},{3,4},{4,3},{5,6},{6,5},{9,10},{10,9},{11,12},{12,11},... | collective-permute-start | bytes 638984 | tf_op jit(solution)/shard_map/ppermute | solution.py:721
  5.5 1.1 %copy-start.4 = (bf16[1152,256]{1,0:T(8,128)(2,1)S(1)}, bf16[1152,256]{1,0:T(8,128)(2,1)}, u32[]{:S(2)}) copy-start(bf16[1152,256]{1,0:T(8,128)(2,1)} %refs_12_.1) | copy-start | bytes 1769476
  6.5 1.0 %copy-start.9 = (bf16[1152,128]{1,0:T(8,128)(2,1)S(1)}, bf16[1152,128]{1,0:T(8,128)(2,1)}, u32[]{:S(2)}) copy-start(bf16[1152,128]{1,0:T(8,128)(2,1)} %refs_1_.1) | copy-start | bytes 884740
  7.5 1.0 %copy-start.10 = (bf16[1152,128]{1,0:T(8,128)(2,1)S(1)}, bf16[1152,128]{1,0:T(8,128)(2,1)}, u32[]{:S(2)}) copy-start(bf16[1152,128]{1,0:T(8,128)(2,1)} %refs_2_.1) | copy-start | bytes 884740
  8.5 6.5 %copy-start.11 = (f32[64,256]{1,0:T(8,128)S(1)}, f32[64,256]{1,0:T(8,128)}, u32[]{:S(2)}) copy-start(f32[64,256]{1,0:T(8,128)} %refs_3_.5) | copy-start | bytes 196612
  10.4 15.1 %collective-permute-start.2 = (bf16[17,10,16,128]{3,2,1,0:T(8,128)(2,1)S(1)}, bf16[17,10,16,128]{3,2,1,0:T(8,128)(2,1)S(1)}, u32[]{:S(2)}, u32[]{:S(2)}) collective-permute-start(bf16[17,10,16,128]{3,2,1,0:T(8,128)(2,1)S(1)} %get-tuple-element.30), channel_id=1, source_target_pairs={{8,16},{16,8},{24,32},{32,24},{40,48},{48,40},{56,64},{64,56},{72,... | collective-permute-start | bytes 2088968 | tf_op jit(solution)/shard_map/ppermute | solution.py:721
  11.1 14.4 %collective-permute-start.3 = (bf16[17,10,16,128]{3,2,1,0:T(8,128)(2,1)S(1)}, bf16[17,10,16,128]{3,2,1,0:T(8,128)(2,1)S(1)}, u32[]{:S(2)}, u32[]{:S(2)}) collective-permute-start(bf16[17,10,16,128]{3,2,1,0:T(8,128)(2,1)S(1)} %get-tuple-element.31), channel_id=1, source_target_pairs={{0,8},{8,0},{1,9},{9,1},{2,10},{10,2},{3,11},{11,3},{4,12},{12,4},... | collective-permute-start | bytes 2088968 | tf_op jit(solution)/shard_map/ppermute | solution.py:733
  15.0 10.5 %copy-start.5 = (bf16[1152,256]{1,0:T(8,128)(2,1)S(1)}, bf16[1152,256]{1,0:T(8,128)(2,1)}, u32[]{:S(2)}) copy-start(bf16[1152,256]{1,0:T(8,128)(2,1)} %refs_12_.1) | copy-start | bytes 1769476
  15.0 10.5 %copy-start.8 = (bf16[12,32,256]{2,1,0:T(8,128)(2,1)S(1)}, bf16[12,32,256]{2,1,0:T(8,128)(2,1)}, u32[]{:S(2)}) copy-start(bf16[12,32,256]{2,1,0:T(8,128)(2,1)} %refs_4_.3) | copy-start | bytes 589828
  22.4 1.8 %copy-start.3 = (bf16[48,48,768]{2,1,0:T(8,128)(2,1)}, bf16[48,48,768]{2,1,0:T(8,128)(2,1)S(1)}, u32[]{:S(2)}) copy-start(bf16[48,48,768]{2,1,0:T(8,128)(2,1)S(1)} %get-tuple-element.35.refs_14_) | copy-start | bytes 10616836
  24.1 1.4 %copy-start.6 = (bf16[44,48,512]{2,1,0:T(8,128)(2,1)}, bf16[44,48,512]{2,1,0:T(8,128)(2,1)S(1)}, u32[]{:S(2)}) copy-start(bf16[44,48,512]{2,1,0:T(8,128)(2,1)S(1)} %get-tuple-element.36.refs_15_) | copy-start | bytes 6488068
  42.7 2.2 %collective-permute-start.4 = (bf16[64,40,128]{2,1,0:T(8,128)(2,1)S(1)}, bf16[64,40,128]{2,1,0:T(8,128)(2,1)S(1)}, u32[]{:S(2)}, u32[]{:S(2)}) collective-permute-start(bf16[64,40,128]{2,1,0:T(8,128)(2,1)S(1)} %get-tuple-element.42), channel_id=1, source_target_pairs={{0,8},{8,0},{1,9},{9,1},{2,10},{10,2},{3,11},{11,3},{4,12},{12,4},... | collective-permute-start | bytes 1966088 | tf_op jit(solution)/shard_map/ppermute | solution.py:739
  44.9 16.5 %copy-start = (bf16[50,32,768]{2,1,0:T(8,128)(2,1)S(1)}, bf16[50,32,768]{2,1,0:T(8,128)(2,1)}, u32[]{:S(2)}) copy-start(bf16[50,32,768]{2,1,0:T(8,128)(2,1)} %get-tuple-element.39.g1.g1_next) | copy-start | bytes 7372804
  45.9 30.4 %all-to-all-start = ((bf16[64,40,128]{2,1,0:T(8,128)(2,1)}), bf16[64,40,128]{2,1,0:T(8,128)(2,1)}, u32[]{:S(2)}, u32[]{:S(2)}) async-start(bf16[64,40,128]{2,1,0:T(8,128)(2,1)} %add_convert_fusion), calls=%async_computation | async-start | bytes 1310720 | tf_op jit(solution)/shard_map/all_to_all | solution.py:741

commit v5 on v4

--- a/solution.py
+++ b/solution.py
@@ -264,27 +264,13 @@
 
 
 def pipeline(steps, dot, post, z0, z1):
-    def put(z, t):
-        total = dot(t)
-        z[0 : total.shape[0], :] = total
-
-    put(z0, 0)
-
-    def two(i, _):
-        put(z1, 2 * i + 1)
-        post(2 * i, z0)
-        put(z0, 2 * i + 2)
-        post(2 * i + 1, z1)
-        return 0
-
-    if steps > 2:
-        lax.fori_loop(0, (steps - 1) // 2, two, 0)
-    if steps % 2 == 0:
-        put(z1, steps - 1)
-        post(steps - 2, z0)
-        post(steps - 1, z1)
-    else:
-        post(steps - 1, z0)
+    z = (z0, z1)
+    for t in range(steps + 1):
+        if t < steps:
+            total = dot(t)
+            z[t % 2][0 : total.shape[0], 0 : total.shape[1]] = total
+        if t > 0:
+            post(t - 1, z[(t - 1) % 2])
 
 
 def conv_one_dot(x1, row, w1t):
@@ -466,7 +452,7 @@
         copy.wait()
     z = (z0, z1)
     for t in range(8):
-        z[t % 2][...] = dot(t)
+        z[t % 2][0 : 8 * KW, :] = dot(t)
         if t + 2 < 8:
             first(t + 2)
         if t > 0:
@@ -476,8 +462,8 @@
     got_w2t.wait()
 
     def conv_two_post(t, z):
-        for s in range(3):
-            low = 1 + 3 * t + s
+        for s in range(6):
+            low = 1 + 6 * t + s
             total = None
             for q in range(2):
                 lanes = slice(q * 128, (q + 1) * 128)
@@ -491,7 +477,7 @@
             line = total * (0.25 * mask[low])
             put_line(x3, low, [before(line), line, after(line)])
 
-    pipeline(6, lambda t: product(around(x2, 2 + 6 * t, 6, slice(0, 512)), w2t[...]), conv_two_post, z0, z1)
+    pipeline(3, lambda t: product(around(x2, 2 + 12 * t, 12, slice(0, 512)), w2t[...]), conv_two_post, z0, z1)
 
     cp[...] = jnp.zeros_like(cp)
     for copy in (*got_sides, got_cot):
@@ -522,20 +508,20 @@
     g3[18] = jnp.zeros((KW, 768), BF16)
 
     def conv_three_post(t, z):
-        for i in range(4):
-            row = 2 + 4 * t + i
+        for i in range(8):
+            row = 2 + 8 * t + i
             act, slope = silu_parts(0.5 * z[i * KW : i * KW + KP, :])
             keep = 0.5 * mask[row]
             line = cp[row - 2] * slope * jnp.concatenate([keep, keep], axis=1)
             put_line(g3, row, [before(line), line, after(line)])
             coarse[row - 2] = act[:KO].astype(BF16)
 
-    pipeline(4, lambda t: product(around(x3, 2 + 4 * t, 4, slice(0, 384)), w3[...]), conv_three_post, z0, z1)
+    pipeline(2, lambda t: product(around(x3, 2 + 8 * t, 8, slice(0, 384)), w3[...]), conv_three_post, z0, z1)
     put_coarse = fetch(coarse.at[pl.ds(2, 12)], coarse_out, 0)
 
     def back_three_post(t, z):
-        for i in range(4):
-            low = 2 + 4 * t + i
+        for i in range(8):
+            low = 2 + 8 * t + i
             line = 0.25 * z[i * KW : i * KW + KP, 0:128]
             xb2[low] = line
             line = line * mask[low]
@@ -545,10 +531,9 @@
                 put_line(g2, row, [before(one), zero, one, after(zero)])
 
     def back_three_dot(t):
-        total = product_turned(around(g3, 2 + 4 * t, 4, slice(0, 768)), w3b[...])
-        return jnp.concatenate([total, total], axis=1)
-
-    pipeline(4, back_three_dot, back_three_post, z0, z1)
+        return product_turned(around(g3, 2 + 8 * t, 8, slice(0, 768)), w3b[...])
+
+    pipeline(2, back_three_dot, back_three_post, z0, z1)
     acc3[...] = weight_terms(
         g3[4:16, 0:KO, 256:512].reshape(12 * KO, 256), around(x3, 4, 12, slice(0, 384), KO)
     )
@@ -559,8 +544,8 @@
     got_d1.wait()
 
     def back_two_post(t, z):
-        for i in range(4):
-            m = 6 + 4 * t + i
+        for i in range(7):
+            m = 6 + 7 * t + i
             low = m // 2
             keep = 0.25 * mask[low]
             base = xb2[low]
@@ -573,7 +558,7 @@
                     g1[row - 12, :, n * 128 : (n + 1) * 128] = line[:KO].astype(BF16)
 
     pipeline(
-        7, lambda t: product_turned(around(g2, 6 + 4 * t, 4, slice(0, 512)), w2b[...]), back_two_post, z0, z1
+        4, lambda t: product_turned(around(g2, 6 + 7 * t, 7, slice(0, 512)), w2b[...]), back_two_post, z0, z1
     )
     put_g1 = fetch(g1.at[pl.ds(3, 50)], g1_out, 1)
     got_x1.wait()
@@ -614,7 +599,7 @@
             start = gw[t, at - t : at + 8 - t, :] if t < 4 else none
             parts.append(jnp.where(line < t, rest, start))
         row, col = divmod(owner, 8)
-        msg[row % 2, (row // 2) * 8 + col] = jnp.concatenate(parts, axis=0).astype(BF16)
+        msg[row % 2, col * 8 + row // 2] = jnp.concatenate(parts, axis=0).astype(BF16)
     put_keep = fetch(msg.at[core], keep_out, 2)
     put_give = fetch(msg.at[1 - core], give_out, 3)
     put_keep.wait()
@@ -659,8 +644,8 @@
             vm((4, 1168, 128), F32),
             vm((2, 64, 40, 128), BF16),
             vm((LOWS, KP, 128), F32),
-            vm((8 * KW, 256), F32),
-            vm((8 * KW, 256), F32),
+            vm((12 * KW, 256), F32),
+            vm((12 * KW, 256), F32),
             vm((12, KO, 256), BF16),
             vm((1536, 256), BF16),
             vm((1536, 256), BF16),
@@ -669,7 +654,7 @@
             vm((128, 2304), BF16),
             pltpu.SemaphoreType.DMA((15,)),
         ],
-        compiler_params=pltpu.CompilerParams(vmem_limit_bytes=46 * MIB),
+        compiler_params=pltpu.CompilerParams(vmem_limit_bytes=38 * MIB),
         name="encoder_levels",
     )(*args)
 
@@ -738,8 +723,11 @@
     )
     other = lax.ppermute(give_msg, "core", [(0, 1), (1, 0)])
     msg = (keep_msg.astype(F32) + other.astype(F32)).astype(BF16)
-    got = lax.all_to_all(msg, ("chip", "tx"), 0, 0, tiled=True)
+    got = lax.all_to_all(msg, "tx", 0, 0, tiled=True)
     grad_inputs = input_grad(g1, w1b)
+    got, grad_inputs = lax.optimization_barrier((got, grad_inputs))
+    msg = got.reshape(8, 8, 40, 128).astype(F32).sum(axis=0).astype(BF16)
+    got = lax.all_to_all(msg, "chip", 0, 0, tiled=True)
     return (coarse, grad_inputs, *collect(got))
 
 

time: 79.2 us -> 83.2 us (1.051)
  blocking collectives: 0 us -> 16.6 us
  starting transfers between devices: 21.8 us -> 15.5 us
  waiting for transfers between devices: 12.5 us -> 9.32 us
  local copies, waits for them, and re-layouts: 9.07 us -> 5.96 us
    all_to_all x0 -> x1, blocking collectives: none -> 16.6 us  [body(): got = lax.all_to_all(msg, 'chip', 0, 0, tiled=True)]
    all_to_all x1, starting transfers between devices: 15.5 us -> 8.58 us  [body(): got = lax.all_to_all(msg, 'tx', 0, 0, tiled=True)]
    unnamed x28 -> x22, local copies, waits for them, and re-layouts: 8.46 us -> 5.35 us
    all_to_all x1, waiting for transfers between devices: 10.3 us -> 7.48 us  [body(): got = lax.all_to_all(msg, 'tx', 0, 0, tiled=True)]
    reduce_sum x1, other arithmetic: 1.21 us -> 0.02 us  [collect(): sums = got.astype(F32).sum(axis=0)]
    reduce_sum x0 -> x1, other arithmetic: none -> 1.18 us  [body(): msg = got.reshape(8, 8, 40, 128).astype(F32).sum(axis=0).astype(BF16)]
  transfers between devices with their start and end apart: 6 -> 6, of which waited for: 3 -> 3; matrix products, arithmetic and copies ran while one was open for 0% -> 0% of each run, Pallas kernels for 17% -> 16%
where the time goes in v5:
time: 83.2 us; the launch traced here: 82.8 us
  Pallas kernels  31.1 us (37%)
  blocking collectives  16.6 us (20%)
  starting transfers between devices  15.5 us (19%)
  waiting for transfers between devices  9.32 us (11%)
  local copies, waits for them, and re-layouts  5.96 us (7%)
  other arithmetic  2.83 us (3%)
  between operations  1.46 us (2%)
    pallas_call x1, Pallas kernels, levels(): pl.pallas_call(kernel, out_shape=[jax.ShapeDtypeStruct((12, KO, 256), BF1...  17.2 us
    all_to_all x1, blocking collectives, body(): got = lax.all_to_all(msg, 'chip', 0, 0, tiled=True)  16.6 us
    all_to_all x1, starting transfers between devices, body(): got = lax.all_to_all(msg, 'tx', 0, 0, tiled=True)  8.58 us
    all_to_all x1, waiting for transfers between devices, body(): got = lax.all_to_all(msg, 'tx', 0, 0, tiled=True)  7.48 us
    pallas_call x1, Pallas kernels, own_rows(): pl.pallas_call(kernel, out_shape=[shape((48, KW, 768), BF16), shape((44,...  7.34 us
    unnamed x22, local copies, waits for them, and re-layouts  5.35 us
    pallas_call x1, Pallas kernels, input_grad(): pl.pallas_call(input_kernel, grid=(6,), out_shape=jax.ShapeDtypeStruct((R...  4.63 us
    ppermute x1, starting transfers between devices, body(): near = lax.ppermute(near, 'core', [(0, 1), (1, 0)])  3.22 us
  transfers between devices with their start and end apart: 6, of which 3 were waited for; matrix products, arithmetic and copies ran while one was open for 0% of the time, Pallas kernels for 16%

profile of v5, /device:TPU:0, one launch (start us, length us, event | category | flops | bytes accessed | tf_op | source)
XLA Modules:
  0.0 82.8 jit_solution(2023456035170410764)
XLA Ops:
  0.6 0.0 copy-start.10
  0.7 1.4 %copy-done = bf16[48,128,128]{2,1,0:T(8,128)(2,1)S(1)} copy-done((bf16[48,128,128]{2,1,0:T(8,128)(2,1)S(1)}, bf16[48,128,128]{2,1,0:T(8,128)(2,1)}, u32[]{:S(2)}) %copy-start) | copy-done | bytes 1572888
  2.1 0.9 %copy-done.4 = bf16[12,32,256]{2,1,0:T(8,128)(2,1)S(1)} copy-done((bf16[12,32,256]{2,1,0:T(8,128)(2,1)S(1)}, bf16[12,32,256]{2,1,0:T(8,128)(2,1)}, u32[]{:S(2)}) %copy-start.4) | copy-done | bytes 196632
  3.0 0.1 pack_columns.1
  3.1 1.7 %collective-permute-start = (bf16[52,16,128]{2,1,0:T(8,128)(2,1)S(1)}, bf16[52,16,128]{2,1,0:T(8,128)(2,1)S(1)}, u32[]{:S(2)}, u32[]{:S(2)}) collective-permute-start(bf16[52,16,128]{2,1,0:T(8,128)(2,1)S(1)} %get-tuple-element.30), channel_id=1, source_target_pairs={{0,1},{1,0},{2,3},{3,2},{4,5},{5,4},{6,7},{7,6},{8,9},{9,8},{10,11... | collective-permute-start | bytes 638984 | tf_op jit(solution)/shard_map/ppermute | solution.py:706
  4.8 0.7 collective-permute-start.1
  5.5 0.0 copy-start.2
  5.5 1.1 %copy-done.2 = bf16[1152,256]{1,0:T(8,128)(2,1)S(1)} copy-done((bf16[1152,256]{1,0:T(8,128)(2,1)S(1)}, bf16[1152,256]{1,0:T(8,128)(2,1)}, u32[]{:S(2)}) %copy-start.2) | copy-done | bytes 589848
  6.5 1.0 %copy-done.6 = bf16[1152,128]{1,0:T(8,128)(2,1)S(1)} copy-done((bf16[1152,128]{1,0:T(8,128)(2,1)S(1)}, bf16[1152,128]{1,0:T(8,128)(2,1)}, u32[]{:S(2)}) %copy-start.6) | copy-done | bytes 294936
  7.5 1.0 %copy-done.7 = bf16[1152,128]{1,0:T(8,128)(2,1)S(1)} copy-done((bf16[1152,128]{1,0:T(8,128)(2,1)S(1)}, bf16[1152,128]{1,0:T(8,128)(2,1)}, u32[]{:S(2)}) %copy-start.7) | copy-done | bytes 294936
  8.5 1.5 %weight_forms.1 = (bf16[1536,256]{1,0:T(8,128)(2,1)S(1)}, bf16[256,1536]{1,0:T(8,128)(2,1)S(1)}, bf16[1536,256]{1,0:T(8,128)(2,1)S(1)}, bf16[256,1536]{1,0:T(8,1...) custom-call(s32[2]{0:T(128)S(1)} %copy-done.10, ...), custom_call_target="tpu_custom_call" | custom-call | tf_op jit(solution)/shard_map/weight_forms/pallas_call | solution.py:163
  9.9 0.1 collective-permute-done.one.refs_5_.refs_8_
  10.0 0.0 collective-permute-done.1.two.refs_6_.refs_9_
  10.0 0.3 pack_rows.1
  10.4 0.7 collective-permute-start.2
  11.1 3.2 %collective-permute-start.3 = (bf16[17,10,16,128]{3,2,1,0:T(8,128)(2,1)S(1)}, bf16[17,10,16,128]{3,2,1,0:T(8,128)(2,1)S(1)}, u32[]{:S(2)}, u32[]{:S(2)}) collective-permute-start(bf16[17,10,16,128]{3,2,1,0:T(8,128)(2,1)S(1)} %get-tuple-element.33), channel_id=1, source_target_pairs={{0,8},{8,0},{1,9},{9,1},{2,10},{10,2},{3,11},{11,3},{4,12},{12,4},... | collective-permute-start | bytes 2088968 | tf_op jit(solution)/shard_map/ppermute | solution.py:718
  15.0 0.0 copy-start.3
  15.0 0.0 copy-start.5
  15.0 7.3 %own_rows.1 = (bf16[48,48,768]{2,1,0:T(8,128)(2,1)S(1)}, bf16[44,48,512]{2,1,0:T(8,128)(2,1)S(1)}, bf16[22,48,512]{2,1,0:T(8,128)(2,1)S(1)}) custom-call(s32[1]{0:T(128)S(6)} %copy.14.refs_0_, f32[2,80,128]{2,1,0:T(8,128)S(1)} %get-tuple-element.26._.refs_1_, f32[2,4,40,128]{3,2,1,0:T(8,128)S(1)} %get-tuple-element.27.refs_2_, f32[64,256]{1,0:T(8,128)S(1)} %copy-done.8, ...), custom_call_target="tpu_custom_call" | custom-call | flops 4000000000 | bytes 30000000 | tf_op jit(solution)/shard_map/own_rows/pallas_call | solution.py:367
  22.4 0.0 collective-permute-done.2.refs_6_
  22.4 0.0 collective-permute-done.3.refs_7_
  22.4 17.2 %encoder_levels.1 = (bf16[12,32,256]{2,1,0:T(8,128)(2,1)}, bf16[50,32,768]{2,1,0:T(8,128)(2,1)S(1)}, bf16[64,40,128]{2,1,0:T(8,128)(2,1)S(1)}, bf16[64,40,128]{2,1,0:T(8,128)(2,1)S(1)}) custom-call(s32[1]{0:T(128)S(6)} %copy.14.refs_0_, f32[2,80,128]{2,1,0:T(8,128)S(1)} %get-tuple-element.26._.refs_1_, f32[2,4,40,128]{3,2,1,0:T(8,128)S(1)} %get-tuple-element.27.refs_2_, ...), custom_call_target="tpu_custom_call" | custom-call | tf_op jit(solution)/shard_map/encoder_levels/pallas_call | solution.py:616
  39.6 0.6 collective-permute-start.4
  40.3 1.7 %collective-permute-done.4 = bf16[64,40,128]{2,1,0:T(8,128)(2,1)S(1)} collective-permute-done((bf16[64,40,128]{2,1,0:T(8,128)(2,1)S(1)}, bf16[64,40,128]{2,1,0:T(8,128)(2,1)S(1)}, u32[]{:S(2)}, u32[]{:S(2)}) %collective-permute-start.4) | collective-permute-done | bytes 655392 | tf_op jit(solution)/shard_map/ppermute | solution.py:724
  42.0 1.0 %add_convert_fusion = bf16[64,40,128]{2,1,0:T(8,128)(2,1)} fusion(bf16[64,40,128]{2,1,0:T(8,128)(2,1)S(1)} %collective-permute-done.4, bf16[64,40,128]{2,1,0:T(8,128)(2,1)S(1)} %get-tuple-element.41), kind=kLoop, calls=%fused_computation | loop fusion | flops 1310720 | bytes 1966080 | tf_op jit(solution)/shard_map/convert_element_type | solution.py:725
  43.0 8.6 %all-to-all-start = ((bf16[64,40,128]{2,1,0:T(8,128)(2,1)}), bf16[64,40,128]{2,1,0:T(8,128)(2,1)}, u32[]{:S(2)}, u32[]{:S(2)}) async-start(bf16[64,40,128]{2,1,0:T(8,128)(2,1)} %add_convert_fusion), calls=%async_computation | async-start | bytes 1310720 | tf_op jit(solution)/shard_map/all_to_all | solution.py:726
  51.6 4.6 %input_grad.1 = bf16[48,128,128]{2,1,0:T(8,128)(2,1)} custom-call(bf16[50,32,768]{2,1,0:T(8,128)(2,1)S(1)} %get-tuple-element.43.g1.g1_next, bf16[50,32,768]{2,1,0:T(8,128)(2,1)S(1)} %get-tuple-element.43.g1.g1_next, bf16[256,1536]{1,0:T(8,128)(2,1)S(1)} %get-tuple-element.44.w1b), custom_call_target="tpu_custom_call" | custom-call | flops 1811939328 | bytes 8388608 | tf_op jit(solution)/shard_map/input_grad/pallas_call | solution.py:679
  56.2 7.5 %all-to-all-done = bf16[64,40,128]{2,1,0:T(8,128)(2,1)} async-done(((bf16[64,40,128]{2,1,0:T(8,128)(2,1)}), bf16[64,40,128]{2,1,0:T(8,128)(2,1)}, u32[]{:S(2)}, u32[]{:S(2)}) %all-to-all-start) | async-done | bytes 655392 | tf_op jit(solution)/shard_map/all_to_all | solution.py:726
  63.7 1.2 %reduce_sum.21 = bf16[8,40,128]{2,1,0:T(8,128)(2,1)S(1)} reduce(bf16[8,8,40,128]{3,2,1,0:T(8,128)(2,1)} %bitcast.1, bf16[]{:T(256)} %constant.2.clone.1), dimensions={0}, to_apply=%region_0.0 | reduce | flops 286720 | bytes 737282 | tf_op jit(solution)/shard_map/reduce_sum | solution.py:729
  64.9 16.6 %all_to_all.10 = bf16[8,40,128]{2,1,0:T(8,128)(2,1)S(1)} all-to-all(bf16[8,40,128]{2,1,0:T(8,128)(2,1)S(1)} %reduce_sum.21), channel_id=1, replica_groups=mesh['chip'=8,'core'=2,'tx'=8] {'chip'}, dimensions={0} | all-to-all | bytes 163840 | tf_op jit(solution)/shard_map/all_to_all | solution.py:730
  81.5 0.6 fusion
  82.2 0.6 pad_maximum_fusion
  (14 shorter events, 0.0 us)
Async XLA Ops:
  0.6 4.8 %copy-start.10 = (s32[2]{0:T(128)S(1)}, s32[2]{0:T(128)}, u32[]{:S(2)}) copy-start(s32[2]{0:T(128)} %refs_0_.3) | copy-start | bytes 28
  0.6 4.8 %copy-start.9 = (f32[2,128]{1,0:T(2,128)S(1)}, f32[2,128]{1,0:T(2,128)}, u32[]{:S(2)}) copy-start(f32[2,128]{1,0:T(2,128)} %refs_4_.2) | copy-start | bytes 3076
  0.7 1.4 %copy-start = (bf16[48,128,128]{2,1,0:T(8,128)(2,1)S(1)}, bf16[48,128,128]{2,1,0:T(8,128)(2,1)}, u32[]{:S(2)}) copy-start(bf16[48,128,128]{2,1,0:T(8,128)(2,1)} %param.9) | copy-start | bytes 4718596
  2.1 0.9 %copy-start.4 = (bf16[12,32,256]{2,1,0:T(8,128)(2,1)S(1)}, bf16[12,32,256]{2,1,0:T(8,128)(2,1)}, u32[]{:S(2)}) copy-start(bf16[12,32,256]{2,1,0:T(8,128)(2,1)} %refs_4_.3) | copy-start | bytes 589828
  3.0 7.0 %copy-start.1 = (bf16[48,128,128]{2,1,0:T(8,128)(2,1)S(1)}, bf16[48,128,128]{2,1,0:T(8,128)(2,1)}, u32[]{:S(2)}) copy-start(bf16[48,128,128]{2,1,0:T(8,128)(2,1)} %param.9) | copy-start | bytes 4718596
  3.1 6.9 %collective-permute-start = (bf16[52,16,128]{2,1,0:T(8,128)(2,1)S(1)}, bf16[52,16,128]{2,1,0:T(8,128)(2,1)S(1)}, u32[]{:S(2)}, u32[]{:S(2)}) collective-permute-start(bf16[52,16,128]{2,1,0:T(8,128)(2,1)S(1)} %get-tuple-element.30), channel_id=1, source_target_pairs={{0,1},{1,0},{2,3},{3,2},{4,5},{5,4},{6,7},{7,6},{8,9},{9,8},{10,11... | collective-permute-start | bytes 638984 | tf_op jit(solution)/shard_map/ppermute | solution.py:706
  4.8 5.3 %collective-permute-start.1 = (bf16[52,16,128]{2,1,0:T(8,128)(2,1)S(1)}, bf16[52,16,128]{2,1,0:T(8,128)(2,1)S(1)}, u32[]{:S(2)}, u32[]{:S(2)}) collective-permute-start(bf16[52,16,128]{2,1,0:T(8,128)(2,1)S(1)} %get-tuple-element.31), channel_id=1, source_target_pairs={{1,2},{2,1},{3,4},{4,3},{5,6},{6,5},{9,10},{10,9},{11,12},{12,11},... | collective-permute-start | bytes 638984 | tf_op jit(solution)/shard_map/ppermute | solution.py:706
  5.5 1.1 %copy-start.2 = (bf16[1152,256]{1,0:T(8,128)(2,1)S(1)}, bf16[1152,256]{1,0:T(8,128)(2,1)}, u32[]{:S(2)}) copy-start(bf16[1152,256]{1,0:T(8,128)(2,1)} %refs_12_.1) | copy-start | bytes 1769476
  6.5 1.0 %copy-start.6 = (bf16[1152,128]{1,0:T(8,128)(2,1)S(1)}, bf16[1152,128]{1,0:T(8,128)(2,1)}, u32[]{:S(2)}) copy-start(bf16[1152,128]{1,0:T(8,128)(2,1)} %refs_1_.1) | copy-start | bytes 884740
  7.5 1.0 %copy-start.7 = (bf16[1152,128]{1,0:T(8,128)(2,1)S(1)}, bf16[1152,128]{1,0:T(8,128)(2,1)}, u32[]{:S(2)}) copy-start(bf16[1152,128]{1,0:T(8,128)(2,1)} %refs_2_.1) | copy-start | bytes 884740
  8.5 6.5 %copy-start.8 = (f32[64,256]{1,0:T(8,128)S(1)}, f32[64,256]{1,0:T(8,128)}, u32[]{:S(2)}) copy-start(f32[64,256]{1,0:T(8,128)} %refs_3_.5) | copy-start | bytes 196612
  10.4 12.0 %collective-permute-start.2 = (bf16[17,10,16,128]{3,2,1,0:T(8,128)(2,1)S(1)}, bf16[17,10,16,128]{3,2,1,0:T(8,128)(2,1)S(1)}, u32[]{:S(2)}, u32[]{:S(2)}) collective-permute-start(bf16[17,10,16,128]{3,2,1,0:T(8,128)(2,1)S(1)} %get-tuple-element.32), channel_id=1, source_target_pairs={{8,16},{16,8},{24,32},{32,24},{40,48},{48,40},{56,64},{64,56},{72,... | collective-permute-start | bytes 2088968 | tf_op jit(solution)/shard_map/ppermute | solution.py:706
  11.1 11.3 %collective-permute-start.3 = (bf16[17,10,16,128]{3,2,1,0:T(8,128)(2,1)S(1)}, bf16[17,10,16,128]{3,2,1,0:T(8,128)(2,1)S(1)}, u32[]{:S(2)}, u32[]{:S(2)}) collective-permute-start(bf16[17,10,16,128]{3,2,1,0:T(8,128)(2,1)S(1)} %get-tuple-element.33), channel_id=1, source_target_pairs={{0,8},{8,0},{1,9},{9,1},{2,10},{10,2},{3,11},{11,3},{4,12},{12,4},... | collective-permute-start | bytes 2088968 | tf_op jit(solution)/shard_map/ppermute | solution.py:718
  15.0 7.4 %copy-start.3 = (bf16[1152,256]{1,0:T(8,128)(2,1)S(1)}, bf16[1152,256]{1,0:T(8,128)(2,1)}, u32[]{:S(2)}) copy-start(bf16[1152,256]{1,0:T(8,128)(2,1)} %refs_12_.1) | copy-start | bytes 1769476
  15.0 7.4 %copy-start.5 = (bf16[12,32,256]{2,1,0:T(8,128)(2,1)S(1)}, bf16[12,32,256]{2,1,0:T(8,128)(2,1)}, u32[]{:S(2)}) copy-start(bf16[12,32,256]{2,1,0:T(8,128)(2,1)} %refs_4_.3) | copy-start | bytes 589828
  39.6 2.4 %collective-permute-start.4 = (bf16[64,40,128]{2,1,0:T(8,128)(2,1)S(1)}, bf16[64,40,128]{2,1,0:T(8,128)(2,1)S(1)}, u32[]{:S(2)}, u32[]{:S(2)}) collective-permute-start(bf16[64,40,128]{2,1,0:T(8,128)(2,1)S(1)} %get-tuple-element.42), channel_id=1, source_target_pairs={{0,8},{8,0},{1,9},{9,1},{2,10},{10,2},{3,11},{11,3},{4,12},{12,4},... | collective-permute-start | bytes 1966088 | tf_op jit(solution)/shard_map/ppermute | solution.py:724
  43.0 20.7 %all-to-all-start = ((bf16[64,40,128]{2,1,0:T(8,128)(2,1)}), bf16[64,40,128]{2,1,0:T(8,128)(2,1)}, u32[]{:S(2)}, u32[]{:S(2)}) async-start(bf16[64,40,128]{2,1,0:T(8,128)(2,1)} %add_convert_fusion), calls=%async_computation | async-start | bytes 1310720 | tf_op jit(solution)/shard_map/all_to_all | solution.py:726

commit v6 on v5

--- a/solution.py
+++ b/solution.py
@@ -42,7 +42,7 @@
     return lax.rem(lax.axis_index("tx"), 2)
 
 
-def side_kernel(inputs, cot, one, two, cots, side32, sems):
+def side_kernel(inputs, cot, one, two, side32, sems):
     odd = odd_column()
     copies = [
         pltpu.make_async_copy(inputs.at[:, 7 - 7 * odd], one.at[pl.ds(1, ROWS)], sems.at[0]),
@@ -59,10 +59,6 @@
         side = side32[...].astype(BF16).reshape(3, 16, 128)
         target[pl.ds(0, 1)] = side[0:1]
         target[pl.ds(1 + ROWS, 3)] = side
-    for at, start in ((0, 10), (1, 0)):
-        for r in range(2):
-            for h in range(2):
-                cots[at, pl.ds((r * 2 + h) * 2, 2)] = cot[start + r, :, h * 128 : (h + 1) * 128].reshape(2, 16, 128)
     for copy in copies:
         copy.wait()
 
@@ -70,16 +66,40 @@
 def sides(inputs, cot):
     return pl.pallas_call(
         side_kernel,
-        out_shape=[jax.ShapeDtypeStruct((ROWS + 4, 16, 128), BF16)] * 2 + [jax.ShapeDtypeStruct((2, 8, 16, 128), BF16)],
+        out_shape=[jax.ShapeDtypeStruct((ROWS + 4, 16, 128), BF16)] * 2,
         in_specs=[any_spec(), vmem_spec()],
-        out_specs=[vmem_spec()] * 3,
+        out_specs=[vmem_spec()] * 2,
         scratch_shapes=[pltpu.VMEM((48, 128), F32), pltpu.SemaphoreType.DMA((2,))],
         compiler_params=pltpu.CompilerParams(vmem_limit_bytes=8 * MIB),
         name="pack_columns",
     )(inputs, cot)
 
 
-def rim_kernel(inputs, cots, one, two, _, off, near, sems):
+def edge_kernel(inputs, cot, _, off, cots, sem):
+    core = lax.axis_index("core")
+    copy = pltpu.make_async_copy(inputs.at[pl.ds((ROWS - HALO) * core, HALO)], off.at[pl.ds(0, HALO)], sem)
+    copy.start()
+    for r in range(2):
+        for h in range(2):
+            lanes, units = slice(h * 128, (h + 1) * 128), pl.ds((r * 2 + h) * 2, 2)
+            off[HALO, units] = cot[10 * core + r, :, lanes].reshape(2, 16, 128)
+            cots[units] = cot[10 - 10 * core + r, :, lanes].reshape(2, 16, 128)
+    copy.wait()
+
+
+def edges(*args):
+    return pl.pallas_call(
+        edge_kernel,
+        out_shape=[jax.ShapeDtypeStruct((HALO + 1, 8, 16, 128), BF16), jax.ShapeDtypeStruct((8, 16, 128), BF16)],
+        in_specs=[any_spec(), vmem_spec(), any_spec()],
+        out_specs=[vmem_spec()] * 2,
+        scratch_shapes=[pltpu.SemaphoreType.DMA],
+        compiler_params=pltpu.CompilerParams(vmem_limit_bytes=8 * MIB),
+        name="pack_off_rows",
+    )(*args)
+
+
+def rim_kernel(inputs, cots, one, two, _, near, corner, sems):
     core = lax.axis_index("core")
     copies = []
 
@@ -89,12 +109,11 @@
         copies.append(copy)
 
     body = pl.ds(0, HALO)
-    for target, low in ((off, core), (near, 1 - core)):
-        row = (ROWS - HALO) * low
-        fetch(inputs.at[pl.ds(row, HALO)], target.at[body, pl.ds(0, 8)])
-        fetch(cots.at[1 - low], target.at[HALO, pl.ds(0, 8)])
-        for unit, side in ((8, one), (9, two)):
-            fetch(side.at[pl.ds(1 + row, HALO)], target.at[body, unit])
+    fetch(inputs.at[pl.ds((ROWS - HALO) * (1 - core), HALO)], near.at[body, pl.ds(0, 8)])
+    fetch(cots, near.at[HALO, pl.ds(0, 8)])
+    for target, low, first in ((near, 1 - core, 8), (corner, core, 0)):
+        for unit, side in ((first, one), (first + 1, two)):
+            fetch(side.at[pl.ds(1 + (ROWS - HALO) * low, HALO)], target.at[body, unit])
             fetch(side.at[(3 + ROWS) * low], target.at[HALO, unit])
     for copy in copies:
         copy.wait()
@@ -103,10 +122,10 @@
 def rims(*args):
     return pl.pallas_call(
         rim_kernel,
-        out_shape=[jax.ShapeDtypeStruct((HALO + 1, 10, 16, 128), BF16)] * 2,
+        out_shape=[jax.ShapeDtypeStruct((HALO + 1, units, 16, 128), BF16) for units in (10, 2)],
         in_specs=[any_spec()] * len(args),
         out_specs=[vmem_spec()] * 2,
-        scratch_shapes=[pltpu.SemaphoreType.DMA((12,))],
+        scratch_shapes=[pltpu.SemaphoreType.DMA((10,))],
         compiler_params=pltpu.CompilerParams(vmem_limit_bytes=8 * MIB),
         name="pack_rows",
     )(*args)
@@ -301,23 +320,20 @@
 
 def own_kernel(
     grid_rows, grid_cols,
-    noise_index, rows_sc, cols_sc, noise, inputs_in, one, two, w1t_in,
+    noise_index, rows_sc, cols_sc, noise, inputs, w1t, one, two,
     x1_out, d1_out, x2_out,
-    x1, stage, d1, x2, mask, side, inputs, w1t, z0, z1, sems,
+    x1, stage, d1, x2, mask, side, z0, z1, sems,
 ):
     odd = odd_column()
     halos = [
         pltpu.make_async_copy(one, side.at[1 - odd], sems.at[0]),
         pltpu.make_async_copy(two, side.at[odd], sems.at[1]),
     ]
-    early = pltpu.make_async_copy(inputs_in.at[pl.ds(0, 12)], inputs.at[pl.ds(0, 12)], sems.at[5])
-    got_w1t = pltpu.make_async_copy(w1t_in, w1t, sems.at[6])
-    late = pltpu.make_async_copy(inputs_in.at[pl.ds(12, 36)], inputs.at[pl.ds(12, 36)], sems.at[7])
-    for copy in (*halos, early, got_w1t, late):
+    for copy in halos:
         copy.start()
     fill_mask(grid_rows // 4, grid_cols // 4, mask)
     scale, shift = modulation(noise, noise_index)
-    for copy in (*halos, early):
+    for copy in halos:
         copy.wait()
 
     def first(q):
@@ -336,8 +352,6 @@
 
     first(0)
     first(1)
-    got_w1t.wait()
-    late.wait()
     z = (z0, z1)
     for t in range(11):
         z[t % 2][...] = dot(t)
@@ -367,7 +381,7 @@
     return pl.pallas_call(
         kernel,
         out_shape=[shape((48, KW, 768), BF16), shape((44, KW, 512), BF16), shape((22, KW, 512), BF16)],
-        in_specs=[smem_spec()] + [vmem_spec()] * 3 + [any_spec()] * 4,
+        in_specs=[smem_spec()] + [vmem_spec()] * 5 + [any_spec()] * 2,
         out_specs=[any_spec()] * 3,
         scratch_shapes=[
             vm((48, KW, 768), BF16),
@@ -376,11 +390,9 @@
             vm((22, KW, 512), BF16),
             vm((LOWS, KP, 128), F32),
             vm((2, ROWS + 4, 16, 128), BF16),
-            vm((ROWS, 8, 16, 128), BF16),
-            vm((1536, 256), BF16),
             vm((8 * KW, 256), F32),
             vm((8 * KW, 256), F32),
-            pltpu.SemaphoreType.DMA((8,)),
+            pltpu.SemaphoreType.DMA((5,)),
         ],
         compiler_params=pltpu.CompilerParams(vmem_limit_bytes=18 * MIB),
         cost_estimate=pl.CostEstimate(flops=4 * 10**9, bytes_accessed=30 * 10**6, transcendentals=0),
@@ -391,10 +403,10 @@
 def lines_kernel(
     grid_rows, grid_cols,
     noise_index, rows_sc, cols_sc, noise,
-    cot_in, w1t_in, off, near, one, two, w2t_in, w2b_in, w3_in, w3b_in, x1_in, d1_in, x2_in,
+    cot, w1t, w2t, w2b, w3, w3b, off, corner, near, one, two, x1_in, d1_in, x2_in,
     coarse_out, g1_out, keep_out, give_out,
     rim, stage, x1, d1, x2, d2, x3, cp, side, side32, g3, xb2, g2, g1, coarse,
-    acc, acc3, gw, msg, mask, z0, z1, cot, w1t, w2t, w2b, w3, w3b, sems,
+    acc, acc3, gw, msg, mask, z0, z1, sems,
 ):
     core = lax.axis_index("core")
     odd = odd_column()
@@ -404,21 +416,20 @@
         copy.start()
         return copy
 
-    got_rims = [fetch(off, rim.at[core], 0), fetch(near, rim.at[1 - core], 1)]
+    got_rims = [
+        fetch(off, rim.at[core, :, pl.ds(0, 8)], 0),
+        fetch(corner, rim.at[core, :, pl.ds(8, 2)], 7),
+        fetch(near, rim.at[1 - core], 1),
+    ]
     got_edges = [
         fetch(x1_in.at[pl.ds(0, 4)], x1.at[pl.ds(16, 4)], 2),
         fetch(x1_in.at[pl.ds(44, 4)], x1.at[pl.ds(60, 4)], 3),
     ]
-    got_w1t = fetch(w1t_in, w1t, 13)
     got_x2 = fetch(x2_in, x2.at[pl.ds(9, 22)], 4)
     units = pl.ds(ROWS + 1, 3)
     got_sides = [fetch(one.at[units], side.at[1 - odd], 5), fetch(two.at[units], side.at[odd], 6)]
-    got_cot = fetch(cot_in, cot, 14)
-    got_w2t = fetch(w2t_in, w2t, 7)
-    got_w3 = [fetch(w3_in, w3, 8), fetch(w3b_in, w3b, 9)]
-    got_w2b = fetch(w2b_in, w2b, 10)
-    got_d1 = fetch(d1_in, d1.at[pl.ds(18, 44)], 11)
-    got_x1 = fetch(x1_in.at[pl.ds(4, 40)], x1.at[pl.ds(20, 40)], 12)
+    got_d1 = fetch(d1_in, d1.at[pl.ds(18, 44)], 8)
+    got_x1 = fetch(x1_in.at[pl.ds(4, 40)], x1.at[pl.ds(20, 40)], 9)
     fill_mask(grid_rows // 4, grid_cols // 4, mask)
     gw[:, 0:8, :] = jnp.zeros((4, 8, 128), F32)
     gw[:, 1160:1168, :] = jnp.zeros((4, 8, 128), F32)
@@ -448,7 +459,7 @@
 
     first(0)
     first(1)
-    for copy in (*got_edges, got_w1t):
+    for copy in got_edges:
         copy.wait()
     z = (z0, z1)
     for t in range(8):
@@ -459,7 +470,6 @@
             post(t - 1, z[(t - 1) % 2])
     post(7, z1)
     got_x2.wait()
-    got_w2t.wait()
 
     def conv_two_post(t, z):
         for s in range(6):
@@ -480,7 +490,7 @@
     pipeline(3, lambda t: product(around(x2, 2 + 12 * t, 12, slice(0, 512)), w2t[...]), conv_two_post, z0, z1)
 
     cp[...] = jnp.zeros_like(cp)
-    for copy in (*got_sides, got_cot):
+    for copy in got_sides:
         copy.wait()
     for h in range(2):
         lanes = slice(h * 128, (h + 1) * 128)
@@ -502,8 +512,6 @@
                 for r in range(2):
                     start = skip + r * 4 + h * 2
                     cp[row + r, at : at + 2, h * 128 : (h + 1) * 128] = side32[start : start + 2]
-    for copy in got_w3:
-        copy.wait()
     g3[1] = jnp.zeros((KW, 768), BF16)
     g3[18] = jnp.zeros((KW, 768), BF16)
 
@@ -540,7 +548,6 @@
     acc[...] = weight_terms(
         g2[8:32, 0:KO, 128:384].reshape(24 * KO, 256), around(x2, 8, 24, slice(0, 512), KO)
     )
-    got_w2b.wait()
     got_d1.wait()
 
     def back_two_post(t, z):
@@ -599,7 +606,7 @@
             start = gw[t, at - t : at + 8 - t, :] if t < 4 else none
             parts.append(jnp.where(line < t, rest, start))
         row, col = divmod(owner, 8)
-        msg[row % 2, col * 8 + row // 2] = jnp.concatenate(parts, axis=0).astype(BF16)
+        msg[row % 2, (row // 2) * 8 + col] = jnp.concatenate(parts, axis=0).astype(BF16)
     put_keep = fetch(msg.at[core], keep_out, 2)
     put_give = fetch(msg.at[1 - core], give_out, 3)
     put_keep.wait()
@@ -621,7 +628,7 @@
             jax.ShapeDtypeStruct((64, 40, 128), BF16),
             jax.ShapeDtypeStruct((64, 40, 128), BF16),
         ],
-        in_specs=[smem_spec()] + [vmem_spec()] * 3 + [any_spec()] * 13,
+        in_specs=[smem_spec()] + [vmem_spec()] * 9 + [any_spec()] * 8,
         out_specs=[any_spec()] * 4,
         scratch_shapes=[
             vm((2, HALO + 1, 10, 16, 128), BF16),
@@ -646,15 +653,9 @@
             vm((LOWS, KP, 128), F32),
             vm((12 * KW, 256), F32),
             vm((12 * KW, 256), F32),
-            vm((12, KO, 256), BF16),
-            vm((1536, 256), BF16),
-            vm((1536, 256), BF16),
-            vm((256, 1536), BF16),
-            vm((1152, 256), BF16),
-            vm((128, 2304), BF16),
-            pltpu.SemaphoreType.DMA((15,)),
+            pltpu.SemaphoreType.DMA((10,)),
         ],
-        compiler_params=pltpu.CompilerParams(vmem_limit_bytes=38 * MIB),
+        compiler_params=pltpu.CompilerParams(vmem_limit_bytes=36 * MIB),
         name="encoder_levels",
     )(*args)
 
@@ -709,25 +710,25 @@
 def body(inputs, weight_one, weight_two, weight_three, noise_table, frequency, anchor, noise_index, cotangent):
     grid = (lax.axis_size(ROW_AXES) * ROWS, lax.axis_size("tx") * 4 * KO)
     inputs = inputs.reshape(ROWS, 8, 16, 128)
-    one, two, cots = sides(inputs, cotangent)
+    one, two = sides(inputs, cotangent)
+    off, cots = edges(inputs, cotangent, two)
     two = swapped(two, "tx", True)
     one = swapped(one, "tx", False)
+    off = swapped(off, ROW_AXES, True)
     w1t, w1b, w2t, w2b, w3b, rows_sc, cols_sc = prep(*grid, anchor, weight_one, weight_two, weight_three, frequency)
-    off, near = rims(inputs, cots, one, two, rows_sc)
-    off = swapped(off, ROW_AXES, True)
+    near, corner = rims(inputs, cots, one, two, rows_sc)
     near = lax.ppermute(near, "core", [(0, 1), (1, 0)])
-    x1, d1, x2 = own_rows(*grid, noise_index, rows_sc, cols_sc, noise_table, inputs, one, two, w1t)
+    corner, off = lax.optimization_barrier((corner, off))
+    corner = swapped(corner, ROW_AXES, True)
+    x1, d1, x2 = own_rows(*grid, noise_index, rows_sc, cols_sc, noise_table, inputs, w1t, one, two)
     coarse, g1, keep_msg, give_msg = levels(
-        *grid, noise_index, rows_sc, cols_sc, noise_table, cotangent, w1t,
-        off, near, one, two, w2t, w2b, weight_three, w3b, x1, d1, x2,
+        *grid, noise_index, rows_sc, cols_sc, noise_table,
+        cotangent, w1t, w2t, w2b, weight_three, w3b, off, corner, near, one, two, x1, d1, x2,
     )
     other = lax.ppermute(give_msg, "core", [(0, 1), (1, 0)])
     msg = (keep_msg.astype(F32) + other.astype(F32)).astype(BF16)
-    got = lax.all_to_all(msg, "tx", 0, 0, tiled=True)
+    got = lax.all_to_all(msg, ("chip", "tx"), 0, 0, tiled=True)
     grad_inputs = input_grad(g1, w1b)
-    got, grad_inputs = lax.optimization_barrier((got, grad_inputs))
-    msg = got.reshape(8, 8, 40, 128).astype(F32).sum(axis=0).astype(BF16)
-    got = lax.all_to_all(msg, "chip", 0, 0, tiled=True)
     return (coarse, grad_inputs, *collect(got))
 
 

time: 83.2 us -> 79.9 us (0.960)
  blocking collectives: 16.6 us -> 0 us
  starting transfers between devices: 15.5 us -> 28.2 us
  waiting for transfers between devices: 9.32 us -> 14.5 us
  local copies, waits for them, and re-layouts: 5.96 us -> 2.98 us
  Pallas kernels: 31.1 us -> 29.6 us
    all_to_all x1 -> x0, blocking collectives: 16.6 us -> none  [body(): got = lax.all_to_all(msg, 'chip', 0, 0, tiled=True)]
    all_to_all x1, starting transfers between devices: 8.58 us -> 17.7 us  [body(): got = lax.all_to_all(msg, ('chip', 'tx'), 0, 0, tiled=True)]
    ppermute x1, starting transfers between devices: 0.63 us -> 4.62 us  [body(): other = lax.ppermute(give_msg, 'core', [(0, 1), (1, 0)])]
    all_to_all x1, waiting for transfers between devices: 7.48 us -> 10.5 us  [body(): got = lax.all_to_all(msg, ('chip', 'tx'), 0, 0, tiled=True)]
    unnamed x22 -> x20, local copies, waits for them, and re-layouts: 5.35 us -> 2.37 us
    ppermute x3 -> x4, waiting for transfers between devices: 0.11 us -> 2.29 us  [swapped(): return lax.ppermute(block, axis, pairs)]
    ppermute x1, starting transfers between devices: 3.22 us -> 1.98 us  [body(): near = lax.ppermute(near, 'core', [(0, 1), (1, 0)])]
    reduce_sum x1, other arithmetic: 0.02 us -> 1.21 us  [collect(): sums = got.astype(F32).sum(axis=0)]
  transfers between devices with their start and end apart: 6 -> 7, of which waited for: 3 -> 3; matrix products, arithmetic and copies ran while one was open for 0% -> 0% of each run, Pallas kernels for 16% -> 16%
where the time goes in v6:
time: 79.9 us; the launch traced here: 79.6 us
  Pallas kernels  29.6 us (37%)
  starting transfers between devices  28.2 us (35%)
  waiting for transfers between devices  14.5 us (18%)
  local copies, waits for them, and re-layouts  2.98 us (4%)
  other arithmetic  2.83 us (4%)
  between operations  1.49 us (2%)
    all_to_all x1, starting transfers between devices, body(): got = lax.all_to_all(msg, ('chip', 'tx'), 0, 0, tiled=True)  17.7 us
    pallas_call x1, Pallas kernels, levels(): pl.pallas_call(kernel, out_shape=[jax.ShapeDtypeStruct((12, KO, 256), BF1...  16.3 us
    all_to_all x1, waiting for transfers between devices, body(): got = lax.all_to_all(msg, ('chip', 'tx'), 0, 0, tiled=True)  10.5 us
    pallas_call x1, Pallas kernels, own_rows(): pl.pallas_call(kernel, out_shape=[shape((48, KW, 768), BF16), shape((44,...  6.79 us
    pallas_call x1, Pallas kernels, input_grad(): pl.pallas_call(input_kernel, grid=(6,), out_shape=jax.ShapeDtypeStruct((R...  4.64 us
    ppermute x1, starting transfers between devices, body(): other = lax.ppermute(give_msg, 'core', [(0, 1), (1, 0)])  4.62 us
    ppermute x4, starting transfers between devices, swapped(): return lax.ppermute(block, axis, pairs)  3.81 us
    unnamed x20, local copies, waits for them, and re-layouts  2.37 us
  transfers between devices with their start and end apart: 7, of which 3 were waited for; matrix products, arithmetic and copies ran while one was open for 0% of the time, Pallas kernels for 16%

profile of v6, /device:TPU:0, one launch (start us, length us, event | category | flops | bytes accessed | tf_op | source)
XLA Modules:
  0.0 79.6 jit_solution(16050693458217394724)
XLA Ops:
  0.6 0.0 copy-start
  0.6 1.4 %copy-done = bf16[48,128,128]{2,1,0:T(8,128)(2,1)S(1)} copy-done((bf16[48,128,128]{2,1,0:T(8,128)(2,1)S(1)}, bf16[48,128,128]{2,1,0:T(8,128)(2,1)}, u32[]{:S(2)}) %copy-start) | copy-done | bytes 1572888
  2.0 0.9 %copy-done.3 = bf16[12,32,256]{2,1,0:T(8,128)(2,1)S(1)} copy-done((bf16[12,32,256]{2,1,0:T(8,128)(2,1)S(1)}, bf16[12,32,256]{2,1,0:T(8,128)(2,1)}, u32[]{:S(2)}) %copy-start.3) | copy-done | bytes 196632
  3.0 0.0 copy-start.9
  3.0 0.1 pack_columns.1
  3.1 0.0 copy-start.1
  3.1 0.1 pack_off_rows.1
  3.2 0.8 %collective-permute-start.2 = (bf16[17,8,16,128]{3,2,1,0:T(8,128)(2,1)S(1)}, bf16[17,8,16,128]{3,2,1,0:T(8,128)(2,1)S(1)}, u32[]{:S(2)}, u32[]{:S(2)}) collective-permute-start(bf16[17,8,16,128]{3,2,1,0:T(8,128)(2,1)S(1)} %get-tuple-element.37), channel_id=1, source_target_pairs={{8,16},{16,8},{24,32},{32,24},{40,48},{48,40},{56,64},{64,56},{72,... | collective-permute-start | bytes 1671176 | tf_op jit(solution)/shard_map/ppermute | solution.py:707
  4.1 0.0 copy-start.7
  4.1 1.7 %collective-permute-start = (bf16[52,16,128]{2,1,0:T(8,128)(2,1)S(1)}, bf16[52,16,128]{2,1,0:T(8,128)(2,1)S(1)}, u32[]{:S(2)}, u32[]{:S(2)}) collective-permute-start(bf16[52,16,128]{2,1,0:T(8,128)(2,1)S(1)} %get-tuple-element.35), channel_id=1, source_target_pairs={{0,1},{1,0},{2,3},{3,2},{4,5},{5,4},{6,7},{7,6},{8,9},{9,8},{10,11... | collective-permute-start | bytes 638984 | tf_op jit(solution)/shard_map/ppermute | solution.py:707
  5.7 0.7 collective-permute-start.1
  6.4 1.5 %weight_forms.1 = (bf16[1536,256]{1,0:T(8,128)(2,1)S(1)}, bf16[256,1536]{1,0:T(8,128)(2,1)S(1)}, bf16[1536,256]{1,0:T(8,128)(2,1)S(1)}, bf16[256,1536]{1,0:T(8,1...) custom-call(s32[2]{0:T(128)S(1)} %copy-done.9, ...), custom_call_target="tpu_custom_call" | custom-call | tf_op jit(solution)/shard_map/weight_forms/pallas_call | solution.py:182
  7.9 2.3 %collective-permute-done.one.refs_6_.refs_13_ = bf16[52,16,128]{2,1,0:T(8,128)(2,1)S(1)} collective-permute-done((bf16[52,16,128]{2,1,0:T(8,128)(2,1)S(1)}, bf16[52,16,128]{2,1,0:T(8,128)(2,1)S(1)}, u32[]{:S(2)}, u32[]{:S(2)}) %collective-permute-start) | collective-permute-done | bytes 213024 | tf_op jit(solution)/shard_map/ppermute | solution.py:707
  10.2 0.0 collective-permute-done.1.two.refs_7_.refs_14_
  10.2 0.2 pack_rows.1
  10.4 2.0 %collective-permute-start.4 = (bf16[17,10,16,128]{3,2,1,0:T(8,128)(2,1)S(1)}, bf16[17,10,16,128]{3,2,1,0:T(8,128)(2,1)S(1)}, u32[]{:S(2)}, u32[]{:S(2)}) collective-permute-start(bf16[17,10,16,128]{3,2,1,0:T(8,128)(2,1)S(1)} %get-tuple-element.40), channel_id=1, source_target_pairs={{0,8},{8,0},{1,9},{9,1},{2,10},{10,2},{3,11},{11,3},{4,12},{12,4},... | collective-permute-start | bytes 2088968 | tf_op jit(solution)/shard_map/ppermute | solution.py:720
  13.1 0.0 collective-permute-done.2.refs_10_
  13.1 0.7 collective-permute-start.3
  13.8 0.0 copy-start.4
  13.8 6.8 %own_rows.1 = (bf16[48,48,768]{2,1,0:T(8,128)(2,1)S(1)}, bf16[44,48,512]{2,1,0:T(8,128)(2,1)S(1)}, bf16[22,48,512]{2,1,0:T(8,128)(2,1)S(1)}) custom-call(s32[1]{0:T(128)S(6)} %copy.14.refs_0_, f32[2,80,128]{2,1,0:T(8,128)S(1)} %get-tuple-element.27._.refs_1_, f32[2,4,40,128]{3,2,1,0:T(8,128)S(1)} %get-tuple-element.28.refs_2_, f32[64,256]{1,0:T(8,128)S(1)} %copy-done.7, ...), custom_call_target="tpu_custom_call" | custom-call | flops 4000000000 | bytes 30000000 | tf_op jit(solution)/shard_map/own_rows/pallas_call | solution.py:381
  20.6 0.0 collective-permute-done.3.refs_11_
  20.6 0.0 collective-permute-done.4.refs_12_
  20.6 16.3 %encoder_levels.1 = (bf16[12,32,256]{2,1,0:T(8,128)(2,1)}, bf16[50,32,768]{2,1,0:T(8,128)(2,1)S(1)}, bf16[64,40,128]{2,1,0:T(8,128)(2,1)S(1)}, bf16[64,40,128]{2,1,0:T(8,128)(2,1)S(1)}) custom-call(s32[1]{0:T(128)S(6)} %copy.14.refs_0_, f32[2,80,128]{2,1,0:T(8,128)S(1)} %get-tuple-element.27._.refs_1_, f32[2,4,40,128]{3,2,1,0:T(8,128)S(1)} %get-tuple-element.28.refs_2_, ...), custom_call_target="tpu_custom_call" | custom-call | tf_op jit(solution)/shard_map/encoder_levels/pallas_call | solution.py:623
  36.9 4.6 %collective-permute-start.5 = (bf16[64,40,128]{2,1,0:T(8,128)(2,1)S(1)}, bf16[64,40,128]{2,1,0:T(8,128)(2,1)S(1)}, u32[]{:S(2)}, u32[]{:S(2)}) collective-permute-start(bf16[64,40,128]{2,1,0:T(8,128)(2,1)S(1)} %get-tuple-element.48), channel_id=1, source_target_pairs={{0,8},{8,0},{1,9},{9,1},{2,10},{10,2},{3,11},{11,3},{4,12},{12,4},... | collective-permute-start | bytes 1966088 | tf_op jit(solution)/shard_map/ppermute | solution.py:728
  41.5 1.7 %collective-permute-done.5 = bf16[64,40,128]{2,1,0:T(8,128)(2,1)S(1)} collective-permute-done((bf16[64,40,128]{2,1,0:T(8,128)(2,1)S(1)}, bf16[64,40,128]{2,1,0:T(8,128)(2,1)S(1)}, u32[]{:S(2)}, u32[]{:S(2)}) %collective-permute-start.5) | collective-permute-done | bytes 655392 | tf_op jit(solution)/shard_map/ppermute | solution.py:728
  43.2 1.0 %add_convert_fusion = bf16[64,40,128]{2,1,0:T(8,128)(2,1)} fusion(bf16[64,40,128]{2,1,0:T(8,128)(2,1)S(1)} %collective-permute-done.5, bf16[64,40,128]{2,1,0:T(8,128)(2,1)S(1)} %get-tuple-element.47), kind=kLoop, calls=%fused_computation.1 | loop fusion | flops 1310720 | bytes 1966080 | tf_op jit(solution)/shard_map/convert_element_type | solution.py:729
  44.2 17.7 %all-to-all-start = ((bf16[64,40,128]{2,1,0:T(8,128)(2,1)}), bf16[64,40,128]{2,1,0:T(8,128)(2,1)}, u32[]{:S(2)}, u32[]{:S(2)}) async-start(bf16[64,40,128]{2,1,0:T(8,128)(2,1)} %add_convert_fusion), calls=%async_computation | async-start | bytes 1310720 | tf_op jit(solution)/shard_map/all_to_all | solution.py:730
  62.0 4.6 %input_grad.1 = bf16[48,128,128]{2,1,0:T(8,128)(2,1)} custom-call(bf16[50,32,768]{2,1,0:T(8,128)(2,1)S(1)} %get-tuple-element.45.g1.g1_next, bf16[50,32,768]{2,1,0:T(8,128)(2,1)S(1)} %get-tuple-element.45.g1.g1_next, bf16[256,1536]{1,0:T(8,128)(2,1)S(1)} %get-tuple-element.46.w1b), custom_call_target="tpu_custom_call" | custom-call | flops 1811939328 | bytes 8388608 | tf_op jit(solution)/shard_map/input_grad/pallas_call | solution.py:680
  66.6 10.5 %all-to-all-done = bf16[64,40,128]{2,1,0:T(8,128)(2,1)} async-done(((bf16[64,40,128]{2,1,0:T(8,128)(2,1)}), bf16[64,40,128]{2,1,0:T(8,128)(2,1)}, u32[]{:S(2)}, u32[]{:S(2)}) %all-to-all-start) | async-done | bytes 655392 | tf_op jit(solution)/shard_map/all_to_all | solution.py:730
  77.1 1.2 %convert_reduce_fusion = f32[40,128]{1,0:T(8,128)S(1)} fusion(bf16[64,40,128]{2,1,0:T(8,128)(2,1)} %all-to-all-done), kind=kLoop, calls=%fused_computation | loop fusion | flops 650240 | bytes 675840 | tf_op jit(solution)/shard_map/reduce_sum | solution.py:698
  78.3 0.6 fusion
  79.0 0.6 pad_maximum_fusion
  (13 shorter events, 0.0 us)
Async XLA Ops:
  0.6 1.4 %copy-start = (bf16[48,128,128]{2,1,0:T(8,128)(2,1)S(1)}, bf16[48,128,128]{2,1,0:T(8,128)(2,1)}, u32[]{:S(2)}) copy-start(bf16[48,128,128]{2,1,0:T(8,128)(2,1)} %param.9) | copy-start | bytes 4718596
  2.0 0.9 %copy-start.3 = (bf16[12,32,256]{2,1,0:T(8,128)(2,1)S(1)}, bf16[12,32,256]{2,1,0:T(8,128)(2,1)}, u32[]{:S(2)}) copy-start(bf16[12,32,256]{2,1,0:T(8,128)(2,1)} %refs_4_.3) | copy-start | bytes 589828
  3.0 3.4 %copy-start.2 = (bf16[1152,256]{1,0:T(8,128)(2,1)S(1)}, bf16[1152,256]{1,0:T(8,128)(2,1)}, u32[]{:S(2)}) copy-start(bf16[1152,256]{1,0:T(8,128)(2,1)} %refs_8_.1) | copy-start | bytes 1769476
  3.0 3.4 %copy-start.5 = (bf16[1152,128]{1,0:T(8,128)(2,1)S(1)}, bf16[1152,128]{1,0:T(8,128)(2,1)}, u32[]{:S(2)}) copy-start(bf16[1152,128]{1,0:T(8,128)(2,1)} %refs_1_.1) | copy-start | bytes 884740
  3.0 3.4 %copy-start.6 = (bf16[1152,128]{1,0:T(8,128)(2,1)S(1)}, bf16[1152,128]{1,0:T(8,128)(2,1)}, u32[]{:S(2)}) copy-start(bf16[1152,128]{1,0:T(8,128)(2,1)} %refs_2_.1) | copy-start | bytes 884740
  3.0 3.4 %copy-start.8 = (f32[2,128]{1,0:T(2,128)S(1)}, f32[2,128]{1,0:T(2,128)}, u32[]{:S(2)}) copy-start(f32[2,128]{1,0:T(2,128)} %refs_4_.2) | copy-start | bytes 3076
  3.0 3.4 %copy-start.9 = (s32[2]{0:T(128)S(1)}, s32[2]{0:T(128)}, u32[]{:S(2)}) copy-start(s32[2]{0:T(128)} %refs_0_.3) | copy-start | bytes 28
  3.1 7.1 %copy-start.1 = (bf16[48,128,128]{2,1,0:T(8,128)(2,1)S(1)}, bf16[48,128,128]{2,1,0:T(8,128)(2,1)}, u32[]{:S(2)}) copy-start(bf16[48,128,128]{2,1,0:T(8,128)(2,1)} %param.9) | copy-start | bytes 4718596
  3.2 9.9 %collective-permute-start.2 = (bf16[17,8,16,128]{3,2,1,0:T(8,128)(2,1)S(1)}, bf16[17,8,16,128]{3,2,1,0:T(8,128)(2,1)S(1)}, u32[]{:S(2)}, u32[]{:S(2)}) collective-permute-start(bf16[17,8,16,128]{3,2,1,0:T(8,128)(2,1)S(1)} %get-tuple-element.37), channel_id=1, source_target_pairs={{8,16},{16,8},{24,32},{32,24},{40,48},{48,40},{56,64},{64,56},{72,... | collective-permute-start | bytes 1671176 | tf_op jit(solution)/shard_map/ppermute | solution.py:707
  4.1 9.7 %copy-start.7 = (f32[64,256]{1,0:T(8,128)S(1)}, f32[64,256]{1,0:T(8,128)}, u32[]{:S(2)}) copy-start(f32[64,256]{1,0:T(8,128)} %refs_3_.5) | copy-start | bytes 196612
  4.1 6.1 %collective-permute-start = (bf16[52,16,128]{2,1,0:T(8,128)(2,1)S(1)}, bf16[52,16,128]{2,1,0:T(8,128)(2,1)S(1)}, u32[]{:S(2)}, u32[]{:S(2)}) collective-permute-start(bf16[52,16,128]{2,1,0:T(8,128)(2,1)S(1)} %get-tuple-element.35), channel_id=1, source_target_pairs={{0,1},{1,0},{2,3},{3,2},{4,5},{5,4},{6,7},{7,6},{8,9},{9,8},{10,11... | collective-permute-start | bytes 638984 | tf_op jit(solution)/shard_map/ppermute | solution.py:707
  5.7 4.5 %collective-permute-start.1 = (bf16[52,16,128]{2,1,0:T(8,128)(2,1)S(1)}, bf16[52,16,128]{2,1,0:T(8,128)(2,1)S(1)}, u32[]{:S(2)}, u32[]{:S(2)}) collective-permute-start(bf16[52,16,128]{2,1,0:T(8,128)(2,1)S(1)} %get-tuple-element.33._), channel_id=1, source_target_pairs={{1,2},{2,1},{3,4},{4,3},{5,6},{6,5},{9,10},{10,9},{11,12},{12,11},... | collective-permute-start | bytes 638984 | tf_op jit(solution)/shard_map/ppermute | solution.py:707
  10.4 10.2 %collective-permute-start.4 = (bf16[17,10,16,128]{3,2,1,0:T(8,128)(2,1)S(1)}, bf16[17,10,16,128]{3,2,1,0:T(8,128)(2,1)S(1)}, u32[]{:S(2)}, u32[]{:S(2)}) collective-permute-start(bf16[17,10,16,128]{3,2,1,0:T(8,128)(2,1)S(1)} %get-tuple-element.40), channel_id=1, source_target_pairs={{0,8},{8,0},{1,9},{9,1},{2,10},{10,2},{3,11},{11,3},{4,12},{12,4},... | collective-permute-start | bytes 2088968 | tf_op jit(solution)/shard_map/ppermute | solution.py:720
  13.1 7.5 %collective-permute-start.3 = (bf16[17,2,16,128]{3,2,1,0:T(8,128)(2,1)S(1)}, bf16[17,2,16,128]{3,2,1,0:T(8,128)(2,1)S(1)}, u32[]{:S(2)}, u32[]{:S(2)}) collective-permute-start(bf16[17,2,16,128]{3,2,1,0:T(8,128)(2,1)S(1)} %get-tuple-element.39), channel_id=1, source_target_pairs={{8,16},{16,8},{24,32},{32,24},{40,48},{48,40},{56,64},{64,56},{72,... | collective-permute-start | bytes 417800 | tf_op jit(solution)/shard_map/ppermute | solution.py:707
  13.8 6.8 %copy-start.4 = (bf16[12,32,256]{2,1,0:T(8,128)(2,1)S(1)}, bf16[12,32,256]{2,1,0:T(8,128)(2,1)}, u32[]{:S(2)}) copy-start(bf16[12,32,256]{2,1,0:T(8,128)(2,1)} %refs_4_.3) | copy-start | bytes 589828
  36.9 6.3 %collective-permute-start.5 = (bf16[64,40,128]{2,1,0:T(8,128)(2,1)S(1)}, bf16[64,40,128]{2,1,0:T(8,128)(2,1)S(1)}, u32[]{:S(2)}, u32[]{:S(2)}) collective-permute-start(bf16[64,40,128]{2,1,0:T(8,128)(2,1)S(1)} %get-tuple-element.48), channel_id=1, source_target_pairs={{0,8},{8,0},{1,9},{9,1},{2,10},{10,2},{3,11},{11,3},{4,12},{12,4},... | collective-permute-start | bytes 1966088 | tf_op jit(solution)/shard_map/ppermute | solution.py:728
  44.2 32.9 %all-to-all-start = ((bf16[64,40,128]{2,1,0:T(8,128)(2,1)}), bf16[64,40,128]{2,1,0:T(8,128)(2,1)}, u32[]{:S(2)}, u32[]{:S(2)}) async-start(bf16[64,40,128]{2,1,0:T(8,128)(2,1)} %add_convert_fusion), calls=%async_computation | async-start | bytes 1310720 | tf_op jit(solution)/shard_map/all_to_all | solution.py:730

commit v7 on v5

--- a/solution.py
+++ b/solution.py
@@ -299,25 +299,37 @@
         put_line(x2, x2_row + s, [before(halves[1]), halves[0], halves[1], after(halves[0])])
 
 
+def conv_two_post(z, at, keep, x2, d2, row, x3, low):
+    total = None
+    for q in range(2):
+        lanes = slice(q * 128, (q + 1) * 128)
+        for r in range(2):
+            start = at + r * KW
+            act, slope = silu_parts(0.5 * z[start : start + KP, lanes])
+            d2[row + r, :, lanes] = 0.5 * slope
+            down = x2[row + r, :, (q + 1) * 128 : (q + 2) * 128].astype(F32)[:KP]
+            act = rounded(down + act)
+            total = act if total is None else total + act
+    line = total * (0.25 * keep)
+    put_line(x3, low, [before(line), line, after(line)])
+
+
 def own_kernel(
     grid_rows, grid_cols,
-    noise_index, rows_sc, cols_sc, noise, inputs_in, one, two, w1t_in,
-    x1_out, d1_out, x2_out,
-    x1, stage, d1, x2, mask, side, inputs, w1t, z0, z1, sems,
+    noise_index, rows_sc, cols_sc, noise, inputs, w1t, w2t, one, two,
+    x1_out, d1_out, x2_out, x3_out, d2_out,
+    x1, stage, d1, x2, mask, side, z0, z1, x3, d2, sems,
 ):
     odd = odd_column()
     halos = [
         pltpu.make_async_copy(one, side.at[1 - odd], sems.at[0]),
         pltpu.make_async_copy(two, side.at[odd], sems.at[1]),
     ]
-    early = pltpu.make_async_copy(inputs_in.at[pl.ds(0, 12)], inputs.at[pl.ds(0, 12)], sems.at[5])
-    got_w1t = pltpu.make_async_copy(w1t_in, w1t, sems.at[6])
-    late = pltpu.make_async_copy(inputs_in.at[pl.ds(12, 36)], inputs.at[pl.ds(12, 36)], sems.at[7])
-    for copy in (*halos, early, got_w1t, late):
+    for copy in halos:
         copy.start()
     fill_mask(grid_rows // 4, grid_cols // 4, mask)
     scale, shift = modulation(noise, noise_index)
-    for copy in (*halos, early):
+    for copy in halos:
         copy.wait()
 
     def first(q):
@@ -336,11 +348,9 @@
 
     first(0)
     first(1)
-    got_w1t.wait()
-    late.wait()
     z = (z0, z1)
     for t in range(11):
-        z[t % 2][...] = dot(t)
+        z[t % 2][0 : 8 * KW, :] = dot(t)
         if t + 2 < 12:
             first(t + 2)
         if t > 0:
@@ -353,6 +363,23 @@
     put_x2 = pltpu.make_async_copy(x2, x2_out, sems.at[4])
     put_d1.start()
     put_x2.start()
+
+    def conv_two_dot(t):
+        return product(around(x2, 1 + 10 * t, 10, slice(0, 512)), w2t[...])
+
+    def conv_two_steps(t, z):
+        for n in range(5):
+            low = 5 * t + n
+            conv_two_post(z, 2 * n * KW, mask[5 + low], x2_own, d2, 2 * low, x3, low)
+
+    x2_own = x2.at[pl.ds(1, 20)]
+    pipeline(2, conv_two_dot, conv_two_steps, z0, z1)
+    put_x3 = pltpu.make_async_copy(x3, x3_out, sems.at[5])
+    put_d2 = pltpu.make_async_copy(d2, d2_out, sems.at[6])
+    put_x3.start()
+    put_d2.start()
+    put_x3.wait()
+    put_d2.wait()
     put_x1.wait()
     put_d1.wait()
     put_x2.wait()
@@ -366,9 +393,15 @@
     shape = jax.ShapeDtypeStruct
     return pl.pallas_call(
         kernel,
-        out_shape=[shape((48, KW, 768), BF16), shape((44, KW, 512), BF16), shape((22, KW, 512), BF16)],
-        in_specs=[smem_spec()] + [vmem_spec()] * 3 + [any_spec()] * 4,
-        out_specs=[any_spec()] * 3,
+        out_shape=[
+            shape((48, KW, 768), BF16),
+            shape((44, KW, 512), BF16),
+            shape((22, KW, 512), BF16),
+            shape((10, KW, 384), BF16),
+            shape((20, KP, 256), F32),
+        ],
+        in_specs=[smem_spec()] + [vmem_spec()] * 6 + [any_spec()] * 2,
+        out_specs=[any_spec()] * 5,
         scratch_shapes=[
             vm((48, KW, 768), BF16),
             vm((4, 160, 128), F32),
@@ -376,13 +409,13 @@
             vm((22, KW, 512), BF16),
             vm((LOWS, KP, 128), F32),
             vm((2, ROWS + 4, 16, 128), BF16),
-            vm((ROWS, 8, 16, 128), BF16),
-            vm((1536, 256), BF16),
-            vm((8 * KW, 256), F32),
-            vm((8 * KW, 256), F32),
-            pltpu.SemaphoreType.DMA((8,)),
+            vm((10 * KW, 256), F32),
+            vm((10 * KW, 256), F32),
+            vm((10, KW, 384), BF16),
+            vm((20, KP, 256), F32),
+            pltpu.SemaphoreType.DMA((7,)),
         ],
-        compiler_params=pltpu.CompilerParams(vmem_limit_bytes=18 * MIB),
+        compiler_params=pltpu.CompilerParams(vmem_limit_bytes=20 * MIB),
         cost_estimate=pl.CostEstimate(flops=4 * 10**9, bytes_accessed=30 * 10**6, transcendentals=0),
         name="own_rows",
     )(*args)
@@ -391,10 +424,10 @@
 def lines_kernel(
     grid_rows, grid_cols,
     noise_index, rows_sc, cols_sc, noise,
-    cot_in, w1t_in, off, near, one, two, w2t_in, w2b_in, w3_in, w3b_in, x1_in, d1_in, x2_in,
+    cot, w1t, w2t, w2b, w3, w3b, off, near, one, two, x1_in, d1_in, x2_in, x3_in, d2_in,
     coarse_out, g1_out, keep_out, give_out,
     rim, stage, x1, d1, x2, d2, x3, cp, side, side32, g3, xb2, g2, g1, coarse,
-    acc, acc3, gw, msg, mask, z0, z1, cot, w1t, w2t, w2b, w3, w3b, sems,
+    acc, acc3, gw, msg, mask, z0, z1, sems,
 ):
     core = lax.axis_index("core")
     odd = odd_column()
@@ -409,16 +442,12 @@
         fetch(x1_in.at[pl.ds(0, 4)], x1.at[pl.ds(16, 4)], 2),
         fetch(x1_in.at[pl.ds(44, 4)], x1.at[pl.ds(60, 4)], 3),
     ]
-    got_w1t = fetch(w1t_in, w1t, 13)
     got_x2 = fetch(x2_in, x2.at[pl.ds(9, 22)], 4)
     units = pl.ds(ROWS + 1, 3)
     got_sides = [fetch(one.at[units], side.at[1 - odd], 5), fetch(two.at[units], side.at[odd], 6)]
-    got_cot = fetch(cot_in, cot, 14)
-    got_w2t = fetch(w2t_in, w2t, 7)
-    got_w3 = [fetch(w3_in, w3, 8), fetch(w3b_in, w3b, 9)]
-    got_w2b = fetch(w2b_in, w2b, 10)
-    got_d1 = fetch(d1_in, d1.at[pl.ds(18, 44)], 11)
-    got_x1 = fetch(x1_in.at[pl.ds(4, 40)], x1.at[pl.ds(20, 40)], 12)
+    got_low = [fetch(x3_in, x3.at[pl.ds(5, 10)], 7), fetch(d2_in, d2.at[pl.ds(10, 20)], 10)]
+    got_d1 = fetch(d1_in, d1.at[pl.ds(18, 44)], 8)
+    got_x1 = fetch(x1_in.at[pl.ds(4, 40)], x1.at[pl.ds(20, 40)], 9)
     fill_mask(grid_rows // 4, grid_cols // 4, mask)
     gw[:, 0:8, :] = jnp.zeros((4, 8, 128), F32)
     gw[:, 1160:1168, :] = jnp.zeros((4, 8, 128), F32)
@@ -448,7 +477,7 @@
 
     first(0)
     first(1)
-    for copy in (*got_edges, got_w1t):
+    for copy in got_edges:
         copy.wait()
     z = (z0, z1)
     for t in range(8):
@@ -459,28 +488,21 @@
             post(t - 1, z[(t - 1) % 2])
     post(7, z1)
     got_x2.wait()
-    got_w2t.wait()
-
-    def conv_two_post(t, z):
-        for s in range(6):
-            low = 1 + 6 * t + s
-            total = None
-            for q in range(2):
-                lanes = slice(q * 128, (q + 1) * 128)
-                for r in range(2):
-                    row, at = 2 * low + r, (2 * s + r) * KW
-                    act, slope = silu_parts(0.5 * z[at : at + KP, lanes])
-                    d2[row, :, lanes] = 0.5 * slope
-                    down = x2[row, :, (q + 1) * 128 : (q + 2) * 128].astype(F32)[:KP]
-                    act = rounded(down + act)
-                    total = act if total is None else total + act
-            line = total * (0.25 * mask[low])
-            put_line(x3, low, [before(line), line, after(line)])
-
-    pipeline(3, lambda t: product(around(x2, 2 + 12 * t, 12, slice(0, 512)), w2t[...]), conv_two_post, z0, z1)
+
+    def conv_two_dot(t):
+        return product(around(x2, 2 + 28 * t, 8, slice(0, 512)), w2t[...])
+
+    def conv_two_steps(t, z):
+        for n in range(4):
+            low = 1 + 14 * t + n
+            conv_two_post(z, 2 * n * KW, mask[low], x2, d2, 2 * low, x3, low)
+
+    pipeline(2, conv_two_dot, conv_two_steps, z0, z1)
+    for copy in got_low:
+        copy.wait()
 
     cp[...] = jnp.zeros_like(cp)
-    for copy in (*got_sides, got_cot):
+    for copy in got_sides:
         copy.wait()
     for h in range(2):
         lanes = slice(h * 128, (h + 1) * 128)
@@ -502,8 +524,6 @@
                 for r in range(2):
                     start = skip + r * 4 + h * 2
                     cp[row + r, at : at + 2, h * 128 : (h + 1) * 128] = side32[start : start + 2]
-    for copy in got_w3:
-        copy.wait()
     g3[1] = jnp.zeros((KW, 768), BF16)
     g3[18] = jnp.zeros((KW, 768), BF16)
 
@@ -540,7 +560,6 @@
     acc[...] = weight_terms(
         g2[8:32, 0:KO, 128:384].reshape(24 * KO, 256), around(x2, 8, 24, slice(0, 512), KO)
     )
-    got_w2b.wait()
     got_d1.wait()
 
     def back_two_post(t, z):
@@ -599,7 +618,7 @@
             start = gw[t, at - t : at + 8 - t, :] if t < 4 else none
             parts.append(jnp.where(line < t, rest, start))
         row, col = divmod(owner, 8)
-        msg[row % 2, col * 8 + row // 2] = jnp.concatenate(parts, axis=0).astype(BF16)
+        msg[row % 2, (row // 2) * 8 + col] = jnp.concatenate(parts, axis=0).astype(BF16)
     put_keep = fetch(msg.at[core], keep_out, 2)
     put_give = fetch(msg.at[1 - core], give_out, 3)
     put_keep.wait()
@@ -621,7 +640,7 @@
             jax.ShapeDtypeStruct((64, 40, 128), BF16),
             jax.ShapeDtypeStruct((64, 40, 128), BF16),
         ],
-        in_specs=[smem_spec()] + [vmem_spec()] * 3 + [any_spec()] * 13,
+        in_specs=[smem_spec()] + [vmem_spec()] * 9 + [any_spec()] * 9,
         out_specs=[any_spec()] * 4,
         scratch_shapes=[
             vm((2, HALO + 1, 10, 16, 128), BF16),
@@ -644,17 +663,11 @@
             vm((4, 1168, 128), F32),
             vm((2, 64, 40, 128), BF16),
             vm((LOWS, KP, 128), F32),
-            vm((12 * KW, 256), F32),
-            vm((12 * KW, 256), F32),
-            vm((12, KO, 256), BF16),
-            vm((1536, 256), BF16),
-            vm((1536, 256), BF16),
-            vm((256, 1536), BF16),
-            vm((1152, 256), BF16),
-            vm((128, 2304), BF16),
-            pltpu.SemaphoreType.DMA((15,)),
+            vm((8 * KW, 256), F32),
+            vm((8 * KW, 256), F32),
+            pltpu.SemaphoreType.DMA((11,)),
         ],
-        compiler_params=pltpu.CompilerParams(vmem_limit_bytes=38 * MIB),
+        compiler_params=pltpu.CompilerParams(vmem_limit_bytes=36 * MIB),
         name="encoder_levels",
     )(*args)
 
@@ -693,9 +706,40 @@
     )(g1, g1, w1b)
 
 
+def collect_kernel(got, one, two, three, held, total, sems):
+    copies = []
+    for n in range(4):
+        part = pl.ds(16 * n, 16)
+        copies.append(pltpu.make_async_copy(got.at[part], held.at[part], sems.at[n]))
+        copies[n].start()
+    sums = None
+    for n, copy in enumerate(copies):
+        copy.wait()
+        for i in range(16):
+            term = held[16 * n + i].astype(F32)
+            sums = term if sums is None else sums + term
+    total[...] = sums
+    one[...] = total[0:9, :]
+    two[...] = total[9:18, :]
+    three[:, 0:128] = total[18:27, :]
+    three[:, 128:256] = total[27:36, :]
+
+
 def collect(got):
-    sums = got.astype(F32).sum(axis=0)
-    return sums[0:9], sums[9:18], jnp.concatenate([sums[18:27], sums[27:36]], axis=1)
+    shape = jax.ShapeDtypeStruct
+    return pl.pallas_call(
+        collect_kernel,
+        out_shape=[shape((9, 128), F32), shape((9, 128), F32), shape((9, 256), F32)],
+        in_specs=[any_spec()],
+        out_specs=[vmem_spec()] * 3,
+        scratch_shapes=[
+            pltpu.VMEM((64, 40, 128), BF16),
+            pltpu.VMEM((40, 128), F32),
+            pltpu.SemaphoreType.DMA((4,)),
+        ],
+        compiler_params=pltpu.CompilerParams(vmem_limit_bytes=8 * MIB),
+        name="collect_weights",
+    )(got)
 
 
 def swapped(block, axis, odd_first):
@@ -716,18 +760,17 @@
     off, near = rims(inputs, cots, one, two, rows_sc)
     off = swapped(off, ROW_AXES, True)
     near = lax.ppermute(near, "core", [(0, 1), (1, 0)])
-    x1, d1, x2 = own_rows(*grid, noise_index, rows_sc, cols_sc, noise_table, inputs, one, two, w1t)
+    x1, d1, x2, x3, d2 = own_rows(
+        *grid, noise_index, rows_sc, cols_sc, noise_table, inputs, w1t, w2t, one, two
+    )
     coarse, g1, keep_msg, give_msg = levels(
-        *grid, noise_index, rows_sc, cols_sc, noise_table, cotangent, w1t,
-        off, near, one, two, w2t, w2b, weight_three, w3b, x1, d1, x2,
+        *grid, noise_index, rows_sc, cols_sc, noise_table,
+        cotangent, w1t, w2t, w2b, weight_three, w3b, off, near, one, two, x1, d1, x2, x3, d2,
     )
     other = lax.ppermute(give_msg, "core", [(0, 1), (1, 0)])
     msg = (keep_msg.astype(F32) + other.astype(F32)).astype(BF16)
-    got = lax.all_to_all(msg, "tx", 0, 0, tiled=True)
+    got = lax.all_to_all(msg, ("chip", "tx"), 0, 0, tiled=True)
     grad_inputs = input_grad(g1, w1b)
-    got, grad_inputs = lax.optimization_barrier((got, grad_inputs))
-    msg = got.reshape(8, 8, 40, 128).astype(F32).sum(axis=0).astype(BF16)
-    got = lax.all_to_all(msg, "chip", 0, 0, tiled=True)
     return (coarse, grad_inputs, *collect(got))
 
 

time: 83.2 us -> 75.2 us (0.904)
  blocking collectives: 16.6 us -> 0 us
  starting transfers between devices: 15.5 us -> 22.3 us
  waiting for transfers between devices: 9.32 us -> 11.5 us
  other arithmetic: 2.83 us -> 1.03 us
    all_to_all x1 -> x0, blocking collectives: 16.6 us -> none  [body(): got = lax.all_to_all(msg, 'chip', 0, 0, tiled=True)]
    all_to_all x1, starting transfers between devices: 8.58 us -> 16 us  [body(): got = lax.all_to_all(msg, ('chip', 'tx'), 0, 0, tiled=True)]
    pallas_call x1, Pallas kernels: 17.2 us -> 15.3 us  [levels(): pl.pallas_call(kernel, out_shape=[jax.ShapeDtypeStruct((12, KO, 256), BF1...]
    all_to_all x1, waiting for transfers between devices: 7.48 us -> 9.29 us  [body(): got = lax.all_to_all(msg, ('chip', 'tx'), 0, 0, tiled=True)]
    pallas_call x0 -> x1, Pallas kernels: none -> 1.57 us  [collect(): pl.pallas_call(collect_kernel, out_shape=[shape((9, 128), F32), shape((9,...]
    reduce_sum x2 -> x0, other arithmetic: 1.2 us -> none  [the longest x1 1.18 us: body(): msg = got.reshape(8, 8, 40, 128).astype(F32).sum(axis=0).astype(BF16)]
    unnamed x22 -> x26, local copies, waits for them, and re-layouts: 5.35 us -> 6.48 us
    pallas_call x1, Pallas kernels: 7.34 us -> 8.45 us  [own_rows(): pl.pallas_call(kernel, out_shape=[shape((48, KW, 768), BF16), shape((44,...]
  transfers between devices with their start and end apart: 6 -> 6, of which waited for: 3 -> 3; matrix products, arithmetic and copies ran while one was open for 0% -> 0% of each run, Pallas kernels for 16% -> 19%
where the time goes in v7:
time: 75.2 us; the launch traced here: 74.8 us
  Pallas kernels  31.8 us (42%)
  starting transfers between devices  22.3 us (30%)
  waiting for transfers between devices  11.5 us (15%)
  local copies, waits for them, and re-layouts  6.48 us (9%)
  between operations  1.64 us (2%)
  other arithmetic  1.03 us (1%)
    all_to_all x1, starting transfers between devices, body(): got = lax.all_to_all(msg, ('chip', 'tx'), 0, 0, tiled=True)  16 us
    pallas_call x1, Pallas kernels, levels(): pl.pallas_call(kernel, out_shape=[jax.ShapeDtypeStruct((12, KO, 256), BF1...  15.3 us
    all_to_all x1, waiting for transfers between devices, body(): got = lax.all_to_all(msg, ('chip', 'tx'), 0, 0, tiled=True)  9.29 us
    pallas_call x1, Pallas kernels, own_rows(): pl.pallas_call(kernel, out_shape=[shape((48, KW, 768), BF16), shape((44,...  8.45 us
    unnamed x26, local copies, waits for them, and re-layouts  6.48 us
    pallas_call x1, Pallas kernels, input_grad(): pl.pallas_call(input_kernel, grid=(6,), out_shape=jax.ShapeDtypeStruct((R...  4.61 us
    ppermute x1, starting transfers between devices, body(): near = lax.ppermute(near, 'core', [(0, 1), (1, 0)])  3.22 us
    ppermute x3, starting transfers between devices, swapped(): return lax.ppermute(block, axis, pairs)  3.02 us
  transfers between devices with their start and end apart: 6, of which 3 were waited for; matrix products, arithmetic and copies ran while one was open for 0% of the time, Pallas kernels for 19%

profile of v7, /device:TPU:0, one launch (start us, length us, event | category | flops | bytes accessed | tf_op | source)
XLA Modules:
  0.0 74.8 jit_solution(4878358907040844109)
XLA Ops:
  0.7 1.4 %copy-done = bf16[48,128,128]{2,1,0:T(8,128)(2,1)S(1)} copy-done((bf16[48,128,128]{2,1,0:T(8,128)(2,1)S(1)}, bf16[48,128,128]{2,1,0:T(8,128)(2,1)}, u32[]{:S(2)}) %copy-start) | copy-done | bytes 1572888
  2.1 0.9 %copy-done.6 = bf16[12,32,256]{2,1,0:T(8,128)(2,1)S(1)} copy-done((bf16[12,32,256]{2,1,0:T(8,128)(2,1)S(1)}, bf16[12,32,256]{2,1,0:T(8,128)(2,1)}, u32[]{:S(2)}) %copy-start.6) | copy-done | bytes 196632
  3.0 0.1 pack_columns.1
  3.1 1.7 %collective-permute-start = (bf16[52,16,128]{2,1,0:T(8,128)(2,1)S(1)}, bf16[52,16,128]{2,1,0:T(8,128)(2,1)S(1)}, u32[]{:S(2)}, u32[]{:S(2)}) collective-permute-start(bf16[52,16,128]{2,1,0:T(8,128)(2,1)S(1)} %get-tuple-element.36), channel_id=1, source_target_pairs={{0,1},{1,0},{2,3},{3,2},{4,5},{5,4},{6,7},{7,6},{8,9},{9,8},{10,11... | collective-permute-start | bytes 638984 | tf_op jit(solution)/shard_map/ppermute | solution.py:750
  4.8 0.7 collective-permute-start.1
  5.5 0.0 copy-start.2
  5.5 1.1 %copy-done.2 = bf16[1152,256]{1,0:T(8,128)(2,1)S(1)} copy-done((bf16[1152,256]{1,0:T(8,128)(2,1)S(1)}, bf16[1152,256]{1,0:T(8,128)(2,1)}, u32[]{:S(2)}) %copy-start.2) | copy-done | bytes 589848
  6.5 1.0 %copy-done.8 = bf16[1152,128]{1,0:T(8,128)(2,1)S(1)} copy-done((bf16[1152,128]{1,0:T(8,128)(2,1)S(1)}, bf16[1152,128]{1,0:T(8,128)(2,1)}, u32[]{:S(2)}) %copy-start.8) | copy-done | bytes 294936
  7.5 1.0 %copy-done.9 = bf16[1152,128]{1,0:T(8,128)(2,1)S(1)} copy-done((bf16[1152,128]{1,0:T(8,128)(2,1)S(1)}, bf16[1152,128]{1,0:T(8,128)(2,1)}, u32[]{:S(2)}) %copy-start.9) | copy-done | bytes 294936
  8.5 1.5 %weight_forms.1 = (bf16[1536,256]{1,0:T(8,128)(2,1)S(1)}, bf16[256,1536]{1,0:T(8,128)(2,1)S(1)}, bf16[1536,256]{1,0:T(8,128)(2,1)S(1)}, bf16[256,1536]{1,0:T(8,1...) custom-call(s32[2]{0:T(128)S(1)} %copy-done.12, ...), custom_call_target="tpu_custom_call" | custom-call | tf_op jit(solution)/shard_map/weight_forms/pallas_call | solution.py:163
  9.9 0.0 copy-start.4
  9.9 0.1 collective-permute-done.one.refs_7_.refs_12_
  10.0 0.0 collective-permute-done.1.two.refs_8_.refs_13_
  10.0 0.3 pack_rows.1
  10.4 0.7 collective-permute-start.2
  11.1 3.2 %collective-permute-start.3 = (bf16[17,10,16,128]{3,2,1,0:T(8,128)(2,1)S(1)}, bf16[17,10,16,128]{3,2,1,0:T(8,128)(2,1)S(1)}, u32[]{:S(2)}, u32[]{:S(2)}) collective-permute-start(bf16[17,10,16,128]{3,2,1,0:T(8,128)(2,1)S(1)} %get-tuple-element.39), channel_id=1, source_target_pairs={{0,8},{8,0},{1,9},{9,1},{2,10},{10,2},{3,11},{11,3},{4,12},{12,4},... | collective-permute-start | bytes 2088968 | tf_op jit(solution)/shard_map/ppermute | solution.py:762
  15.0 0.0 copy-done.4
  15.0 0.0 copy-start.3
  15.0 0.0 copy-start.7
  15.0 8.4 %own_rows.1 = (bf16[48,48,768]{2,1,0:T(8,128)(2,1)S(1)}, bf16[44,48,512]{2,1,0:T(8,128)(2,1)S(1)}, bf16[22,48,512]{2,1,0:T(8,128)(2,1)S(1)}, bf16[10,48,384]{2,1,0:T(8,128)(2,1)S(1)}, f32[20,40,256]{2,1,0:T(8,128)S(1)}) custom-call(s32[1]{0:T(128)S(6)} %copy.14.refs_0_, f32[2,80,128]{2,1,0:T(8,128)S(1)} %get-tuple-element.29._.refs_1_, ...), custom_call_target="tpu_custom_call" | custom-call | flops 4000000000 | bytes 30000000 | tf_op jit(solution)/shard_map/own_rows/pallas_call | solution.py:394
  23.5 0.0 collective-permute-done.2.refs_10_
  23.5 0.0 collective-permute-done.3.refs_11_
  23.5 15.3 %encoder_levels.1 = (bf16[12,32,256]{2,1,0:T(8,128)(2,1)}, bf16[50,32,768]{2,1,0:T(8,128)(2,1)S(1)}, bf16[64,40,128]{2,1,0:T(8,128)(2,1)S(1)}, bf16[64,40,128]{2,1,0:T(8,128)(2,1)S(1)}) custom-call(s32[1]{0:T(128)S(6)} %copy.14.refs_0_, f32[2,80,128]{2,1,0:T(8,128)S(1)} %get-tuple-element.29._.refs_1_, f32[2,4,40,128]{3,2,1,0:T(8,128)S(1)} %get-tuple-element.30.refs_2_, ...), custom_call_target="tpu_custom_call" | custom-call | tf_op jit(solution)/shard_map/encoder_levels/pallas_call | solution.py:635
  38.8 0.1 collective-permute-start.4
  38.9 2.1 %collective-permute-done.4 = bf16[64,40,128]{2,1,0:T(8,128)(2,1)S(1)} collective-permute-done((bf16[64,40,128]{2,1,0:T(8,128)(2,1)S(1)}, bf16[64,40,128]{2,1,0:T(8,128)(2,1)S(1)}, u32[]{:S(2)}, u32[]{:S(2)}) %collective-permute-start.4) | collective-permute-done | bytes 655392 | tf_op jit(solution)/shard_map/ppermute | solution.py:770
  41.0 1.0 %add_convert_fusion = bf16[64,40,128]{2,1,0:T(8,128)(2,1)} fusion(bf16[64,40,128]{2,1,0:T(8,128)(2,1)S(1)} %collective-permute-done.4, bf16[64,40,128]{2,1,0:T(8,128)(2,1)S(1)} %get-tuple-element.48), kind=kLoop, calls=%fused_computation | loop fusion | flops 1310720 | bytes 1966080 | tf_op jit(solution)/shard_map/convert_element_type | solution.py:771
  42.0 16.0 %all-to-all-start = ((bf16[64,40,128]{2,1,0:T(8,128)(2,1)}), bf16[64,40,128]{2,1,0:T(8,128)(2,1)S(1)}, u32[]{:S(2)}, u32[]{:S(2)}) async-start(bf16[64,40,128]{2,1,0:T(8,128)(2,1)} %add_convert_fusion), calls=%async_computation | async-start | bytes 1310720 | tf_op jit(solution)/shard_map/all_to_all | solution.py:772
  58.0 0.0 copy-start.5
  58.0 1.1 %copy-done.5 = bf16[256,1536]{1,0:T(8,128)(2,1)S(1)} copy-done((bf16[256,1536]{1,0:T(8,128)(2,1)S(1)}, bf16[256,1536]{1,0:T(8,128)(2,1)}, u32[]{:S(2)}) %copy-start.5) | copy-done | bytes 786456
  59.1 4.6 %input_grad.1 = bf16[48,128,128]{2,1,0:T(8,128)(2,1)} custom-call(bf16[50,32,768]{2,1,0:T(8,128)(2,1)S(1)} %get-tuple-element.46.g1.g1_next, bf16[50,32,768]{2,1,0:T(8,128)(2,1)S(1)} %get-tuple-element.46.g1.g1_next, bf16[256,1536]{1,0:T(8,128)(2,1)S(1)} %copy-done.5), custom_call_target="tpu_custom_call" | custom-call | flops 1811939328 | bytes 8388608 | tf_op jit(solution)/shard_map/input_grad/pallas_call | solution.py:692
  63.7 9.3 %all-to-all-done.got = bf16[64,40,128]{2,1,0:T(8,128)(2,1)S(1)} async-done(((bf16[64,40,128]{2,1,0:T(8,128)(2,1)}), bf16[64,40,128]{2,1,0:T(8,128)(2,1)S(1)}, u32[]{:S(2)}, u32[]{:S(2)}) %all-to-all-start) | async-done | bytes 655392 | tf_op jit(solution)/shard_map/all_to_all | solution.py:772
  73.0 1.6 %collect_weights.1 = (f32[9,128]{1,0:T(8,128)}, f32[9,128]{1,0:T(8,128)}, f32[9,256]{1,0:T(8,128)}) custom-call(bf16[64,40,128]{2,1,0:T(8,128)(2,1)S(1)} %all-to-all-done.got), custom_call_target="tpu_custom_call" | custom-call | tf_op jit(solution)/shard_map/collect_weights/pallas_call | solution.py:730
  (14 shorter events, 0.0 us)
Async XLA Ops:
  0.6 4.8 %copy-start.12 = (s32[2]{0:T(128)S(1)}, s32[2]{0:T(128)}, u32[]{:S(2)}) copy-start(s32[2]{0:T(128)} %refs_0_.3) | copy-start | bytes 28
  0.6 4.8 %copy-start.11 = (f32[2,128]{1,0:T(2,128)S(1)}, f32[2,128]{1,0:T(2,128)}, u32[]{:S(2)}) copy-start(f32[2,128]{1,0:T(2,128)} %refs_4_.2) | copy-start | bytes 3076
  0.7 1.4 %copy-start = (bf16[48,128,128]{2,1,0:T(8,128)(2,1)S(1)}, bf16[48,128,128]{2,1,0:T(8,128)(2,1)}, u32[]{:S(2)}) copy-start(bf16[48,128,128]{2,1,0:T(8,128)(2,1)} %param.9) | copy-start | bytes 4718596
  2.1 0.9 %copy-start.6 = (bf16[12,32,256]{2,1,0:T(8,128)(2,1)S(1)}, bf16[12,32,256]{2,1,0:T(8,128)(2,1)}, u32[]{:S(2)}) copy-start(bf16[12,32,256]{2,1,0:T(8,128)(2,1)} %refs_4_.3) | copy-start | bytes 589828
  3.0 7.0 %copy-start.1 = (bf16[48,128,128]{2,1,0:T(8,128)(2,1)S(1)}, bf16[48,128,128]{2,1,0:T(8,128)(2,1)}, u32[]{:S(2)}) copy-start(bf16[48,128,128]{2,1,0:T(8,128)(2,1)} %param.9) | copy-start | bytes 4718596
  3.1 6.9 %collective-permute-start = (bf16[52,16,128]{2,1,0:T(8,128)(2,1)S(1)}, bf16[52,16,128]{2,1,0:T(8,128)(2,1)S(1)}, u32[]{:S(2)}, u32[]{:S(2)}) collective-permute-start(bf16[52,16,128]{2,1,0:T(8,128)(2,1)S(1)} %get-tuple-element.36), channel_id=1, source_target_pairs={{0,1},{1,0},{2,3},{3,2},{4,5},{5,4},{6,7},{7,6},{8,9},{9,8},{10,11... | collective-permute-start | bytes 638984 | tf_op jit(solution)/shard_map/ppermute | solution.py:750
  4.8 5.3 %collective-permute-start.1 = (bf16[52,16,128]{2,1,0:T(8,128)(2,1)S(1)}, bf16[52,16,128]{2,1,0:T(8,128)(2,1)S(1)}, u32[]{:S(2)}, u32[]{:S(2)}) collective-permute-start(bf16[52,16,128]{2,1,0:T(8,128)(2,1)S(1)} %get-tuple-element.37), channel_id=1, source_target_pairs={{1,2},{2,1},{3,4},{4,3},{5,6},{6,5},{9,10},{10,9},{11,12},{12,11},... | collective-permute-start | bytes 638984 | tf_op jit(solution)/shard_map/ppermute | solution.py:750
  5.5 1.1 %copy-start.2 = (bf16[1152,256]{1,0:T(8,128)(2,1)S(1)}, bf16[1152,256]{1,0:T(8,128)(2,1)}, u32[]{:S(2)}) copy-start(bf16[1152,256]{1,0:T(8,128)(2,1)} %refs_8_.1) | copy-start | bytes 1769476
  6.5 1.0 %copy-start.8 = (bf16[1152,128]{1,0:T(8,128)(2,1)S(1)}, bf16[1152,128]{1,0:T(8,128)(2,1)}, u32[]{:S(2)}) copy-start(bf16[1152,128]{1,0:T(8,128)(2,1)} %refs_1_.1) | copy-start | bytes 884740
  7.5 1.0 %copy-start.9 = (bf16[1152,128]{1,0:T(8,128)(2,1)S(1)}, bf16[1152,128]{1,0:T(8,128)(2,1)}, u32[]{:S(2)}) copy-start(bf16[1152,128]{1,0:T(8,128)(2,1)} %refs_2_.1) | copy-start | bytes 884740
  8.5 6.5 %copy-start.10 = (f32[64,256]{1,0:T(8,128)S(1)}, f32[64,256]{1,0:T(8,128)}, u32[]{:S(2)}) copy-start(f32[64,256]{1,0:T(8,128)} %refs_3_.5) | copy-start | bytes 196612
  9.9 5.0 %copy-start.4 = (bf16[256,1536]{1,0:T(8,128)(2,1)}, bf16[256,1536]{1,0:T(8,128)(2,1)S(1)}, u32[]{:S(2)}) copy-start(bf16[256,1536]{1,0:T(8,128)(2,1)S(1)} %get-tuple-element.47.w1b) | copy-start | bytes 2359300
  10.4 13.1 %collective-permute-start.2 = (bf16[17,10,16,128]{3,2,1,0:T(8,128)(2,1)S(1)}, bf16[17,10,16,128]{3,2,1,0:T(8,128)(2,1)S(1)}, u32[]{:S(2)}, u32[]{:S(2)}) collective-permute-start(bf16[17,10,16,128]{3,2,1,0:T(8,128)(2,1)S(1)} %get-tuple-element.38), channel_id=1, source_target_pairs={{8,16},{16,8},{24,32},{32,24},{40,48},{48,40},{56,64},{64,56},{72,... | collective-permute-start | bytes 2088968 | tf_op jit(solution)/shard_map/ppermute | solution.py:750
  11.1 12.4 %collective-permute-start.3 = (bf16[17,10,16,128]{3,2,1,0:T(8,128)(2,1)S(1)}, bf16[17,10,16,128]{3,2,1,0:T(8,128)(2,1)S(1)}, u32[]{:S(2)}, u32[]{:S(2)}) collective-permute-start(bf16[17,10,16,128]{3,2,1,0:T(8,128)(2,1)S(1)} %get-tuple-element.39), channel_id=1, source_target_pairs={{0,8},{8,0},{1,9},{9,1},{2,10},{10,2},{3,11},{11,3},{4,12},{12,4},... | collective-permute-start | bytes 2088968 | tf_op jit(solution)/shard_map/ppermute | solution.py:762
  15.0 8.5 %copy-start.3 = (bf16[1152,256]{1,0:T(8,128)(2,1)S(1)}, bf16[1152,256]{1,0:T(8,128)(2,1)}, u32[]{:S(2)}) copy-start(bf16[1152,256]{1,0:T(8,128)(2,1)} %refs_8_.1) | copy-start | bytes 1769476
  15.0 8.5 %copy-start.7 = (bf16[12,32,256]{2,1,0:T(8,128)(2,1)S(1)}, bf16[12,32,256]{2,1,0:T(8,128)(2,1)}, u32[]{:S(2)}) copy-start(bf16[12,32,256]{2,1,0:T(8,128)(2,1)} %refs_4_.3) | copy-start | bytes 589828
  38.8 2.2 %collective-permute-start.4 = (bf16[64,40,128]{2,1,0:T(8,128)(2,1)S(1)}, bf16[64,40,128]{2,1,0:T(8,128)(2,1)S(1)}, u32[]{:S(2)}, u32[]{:S(2)}) collective-permute-start(bf16[64,40,128]{2,1,0:T(8,128)(2,1)S(1)} %get-tuple-element.49), channel_id=1, source_target_pairs={{0,8},{8,0},{1,9},{9,1},{2,10},{10,2},{3,11},{11,3},{4,12},{12,4},... | collective-permute-start | bytes 1966088 | tf_op jit(solution)/shard_map/ppermute | solution.py:770
  42.0 31.0 %all-to-all-start = ((bf16[64,40,128]{2,1,0:T(8,128)(2,1)}), bf16[64,40,128]{2,1,0:T(8,128)(2,1)S(1)}, u32[]{:S(2)}, u32[]{:S(2)}) async-start(bf16[64,40,128]{2,1,0:T(8,128)(2,1)} %add_convert_fusion), calls=%async_computation | async-start | bytes 1310720 | tf_op jit(solution)/shard_map/all_to_all | solution.py:772
  58.0 1.1 %copy-start.5 = (bf16[256,1536]{1,0:T(8,128)(2,1)S(1)}, bf16[256,1536]{1,0:T(8,128)(2,1)}, u32[]{:S(2)}) copy-start(bf16[256,1536]{1,0:T(8,128)(2,1)} %copy-done.4) | copy-start | bytes 2359300

commit v8 on v7

--- a/solution.py
+++ b/solution.py
@@ -12,6 +12,7 @@
 KP = 40
 KW = 48
 HALO = 16
+SENT = 15
 ROWS = 48
 PAD_ROWS = ROWS + 2 * HALO
 PAIRS = PAD_ROWS // 2
@@ -79,7 +80,7 @@
     )(inputs, cot)
 
 
-def rim_kernel(inputs, cots, one, two, _, off, near, sems):
+def rim_kernel(inputs, cots, two, one, _, off, near, sems):
     core = lax.axis_index("core")
     copies = []
 
@@ -88,14 +89,14 @@
         copy.start()
         copies.append(copy)
 
-    body = pl.ds(0, HALO)
+    body = pl.ds(0, SENT)
     for target, low in ((off, core), (near, 1 - core)):
-        row = (ROWS - HALO) * low
-        fetch(inputs.at[pl.ds(row, HALO)], target.at[body, pl.ds(0, 8)])
-        fetch(cots.at[1 - low], target.at[HALO, pl.ds(0, 8)])
+        row = (ROWS - SENT) * low
+        fetch(inputs.at[pl.ds(row, SENT)], target.at[body, pl.ds(0, 8)])
+        fetch(cots.at[1 - low], target.at[SENT, pl.ds(0, 8)])
         for unit, side in ((8, one), (9, two)):
-            fetch(side.at[pl.ds(1 + row, HALO)], target.at[body, unit])
-            fetch(side.at[(3 + ROWS) * low], target.at[HALO, unit])
+            fetch(side.at[pl.ds(1 + row, SENT)], target.at[body, unit])
+            fetch(side.at[(3 + ROWS) * low], target.at[SENT, unit])
     for copy in copies:
         copy.wait()
 
@@ -103,7 +104,7 @@
 def rims(*args):
     return pl.pallas_call(
         rim_kernel,
-        out_shape=[jax.ShapeDtypeStruct((HALO + 1, 10, 16, 128), BF16)] * 2,
+        out_shape=[jax.ShapeDtypeStruct((SENT + 1, 10, 16, 128), BF16)] * 2,
         in_specs=[any_spec()] * len(args),
         out_specs=[vmem_spec()] * 2,
         scratch_shapes=[pltpu.SemaphoreType.DMA((12,))],
@@ -316,7 +317,7 @@
 
 def own_kernel(
     grid_rows, grid_cols,
-    noise_index, rows_sc, cols_sc, noise, inputs, w1t, w2t, one, two,
+    noise_index, rows_sc, cols_sc, noise, inputs, w1t, w2t, two, one,
     x1_out, d1_out, x2_out, x3_out, d2_out,
     x1, stage, d1, x2, mask, side, z0, z1, x3, d2, sems,
 ):
@@ -424,7 +425,7 @@
 def lines_kernel(
     grid_rows, grid_cols,
     noise_index, rows_sc, cols_sc, noise,
-    cot, w1t, w2t, w2b, w3, w3b, off, near, one, two, x1_in, d1_in, x2_in, x3_in, d2_in,
+    cot, w1t, w2t, w2b, w3, w3b, off, near, two, one, x1_in, d1_in, x2_in, x3_in, d2_in,
     coarse_out, g1_out, keep_out, give_out,
     rim, stage, x1, d1, x2, d2, x3, cp, side, side32, g3, xb2, g2, g1, coarse,
     acc, acc3, gw, msg, mask, z0, z1, sems,
@@ -437,7 +438,11 @@
         copy.start()
         return copy
 
-    got_rims = [fetch(off, rim.at[core], 0), fetch(near, rim.at[1 - core], 1)]
+    got_rims = []
+    for n, (source, below) in enumerate(((off, core), (near, 1 - core))):
+        rows = pl.ds(1 - below, SENT)
+        got_rims.append(fetch(source.at[pl.ds(0, SENT)], rim.at[below, rows], n))
+        got_rims.append(fetch(source.at[SENT], rim.at[below, HALO], 11 + n))
     got_edges = [
         fetch(x1_in.at[pl.ds(0, 4)], x1.at[pl.ds(16, 4)], 2),
         fetch(x1_in.at[pl.ds(44, 4)], x1.at[pl.ds(60, 4)], 3),
@@ -454,6 +459,8 @@
     scale, shift = modulation(noise, noise_index)
     for copy in got_rims:
         copy.wait()
+    rim[0, 0] = jnp.zeros((10, 16, 128), BF16)
+    rim[1, SENT] = jnp.zeros((10, 16, 128), BF16)
 
     def first(n):
         below, start = n // 4, 4 * (n % 4)
@@ -589,24 +596,14 @@
                 term = acc[0:128, left : left + 128] + acc[128:256, left + 128 : left + 256]
                 gw[at, pl.ds(8 + (3 * u + v) * 128, 128), :] = term.T
 
-    def one_chunk(t):
-        grads = jnp.concatenate(
-            [g1[4 + 16 * t : 20 + 16 * t, :, lanes].reshape(512, 256) for lanes in (slice(128, 384), slice(384, 640))],
-            axis=0,
-        )
-        fields = jnp.concatenate(
-            [around(x1, 16 + 16 * t, 16, lanes, KO) for lanes in (slice(0, 512), slice(256, 768))], axis=0
-        )
-        return weight_terms(grads, fields)
-
     fold_weights(1)
-    acc[...] = one_chunk(0)
     for tap in range(9):
         turned = acc3[:, tap * 128 : (tap + 1) * 128].T
         gw[2, pl.ds(8 + tap * 128, 128), :] = turned[:, 0:128]
         gw[3, pl.ds(8 + tap * 128, 128), :] = turned[:, 128:256]
-    acc[...] += one_chunk(1)
-    acc[...] += one_chunk(2)
+    grads = [g1[4:52, :, lanes].reshape(ROWS * KO, 256) for lanes in (slice(128, 384), slice(384, 640))]
+    fields = [around(x1, 16, ROWS, lanes, KO) for lanes in (slice(0, 512), slice(256, 768))]
+    acc[...] = weight_terms(jnp.concatenate(grads, axis=0), jnp.concatenate(fields, axis=0))
     fold_weights(0)
     line = lax.broadcasted_iota(jnp.int32, (8, 128), 0)
     none = jnp.zeros((8, 128), F32)
@@ -665,7 +662,7 @@
             vm((LOWS, KP, 128), F32),
             vm((8 * KW, 256), F32),
             vm((8 * KW, 256), F32),
-            pltpu.SemaphoreType.DMA((11,)),
+            pltpu.SemaphoreType.DMA((13,)),
         ],
         compiler_params=pltpu.CompilerParams(vmem_limit_bytes=36 * MIB),
         name="encoder_levels",
@@ -757,15 +754,15 @@
     two = swapped(two, "tx", True)
     one = swapped(one, "tx", False)
     w1t, w1b, w2t, w2b, w3b, rows_sc, cols_sc = prep(*grid, anchor, weight_one, weight_two, weight_three, frequency)
-    off, near = rims(inputs, cots, one, two, rows_sc)
+    off, near = rims(inputs, cots, two, one, rows_sc)
     off = swapped(off, ROW_AXES, True)
     near = lax.ppermute(near, "core", [(0, 1), (1, 0)])
     x1, d1, x2, x3, d2 = own_rows(
-        *grid, noise_index, rows_sc, cols_sc, noise_table, inputs, w1t, w2t, one, two
+        *grid, noise_index, rows_sc, cols_sc, noise_table, inputs, w1t, w2t, two, one
     )
     coarse, g1, keep_msg, give_msg = levels(
         *grid, noise_index, rows_sc, cols_sc, noise_table,
-        cotangent, w1t, w2t, w2b, weight_three, w3b, off, near, one, two, x1, d1, x2, x3, d2,
+        cotangent, w1t, w2t, w2b, weight_three, w3b, off, near, two, one, x1, d1, x2, x3, d2,
     )
     other = lax.ppermute(give_msg, "core", [(0, 1), (1, 0)])
     msg = (keep_msg.astype(F32) + other.astype(F32)).astype(BF16)

time: 75.2 us -> 74.2 us (0.987)
  starting transfers between devices: 22.3 us -> 21.1 us
    all_to_all x1, starting transfers between devices: 16 us -> 12.1 us  [body(): got = lax.all_to_all(msg, ('chip', 'tx'), 0, 0, tiled=True)]
    ppermute x3, starting transfers between devices: 3.02 us -> 5.89 us  [swapped(): return lax.ppermute(block, axis, pairs)]
  transfers between devices with their start and end apart: 6 -> 6, of which waited for: 3 -> 3; matrix products, arithmetic and copies ran while one was open for 0% -> 0% of each run, Pallas kernels for 19% -> 20%
where the time goes in v8:
time: 74.2 us; the launch traced here: 73.8 us
  Pallas kernels  31.7 us (43%)
  starting transfers between devices  21.1 us (28%)
  waiting for transfers between devices  11.9 us (16%)
  local copies, waits for them, and re-layouts  6.49 us (9%)
  between operations  1.63 us (2%)
  other arithmetic  1.03 us (1%)
    pallas_call x1, Pallas kernels, levels(): pl.pallas_call(kernel, out_shape=[jax.ShapeDtypeStruct((12, KO, 256), BF1...  15.2 us
    all_to_all x1, starting transfers between devices, body(): got = lax.all_to_all(msg, ('chip', 'tx'), 0, 0, tiled=True)  12.1 us
    all_to_all x1, waiting for transfers between devices, body(): got = lax.all_to_all(msg, ('chip', 'tx'), 0, 0, tiled=True)  9.29 us
    pallas_call x1, Pallas kernels, own_rows(): pl.pallas_call(kernel, out_shape=[shape((48, KW, 768), BF16), shape((44,...  8.39 us
    unnamed x26, local copies, waits for them, and re-layouts  6.49 us
    ppermute x3, starting transfers between devices, swapped(): return lax.ppermute(block, axis, pairs)  5.89 us
    pallas_call x1, Pallas kernels, input_grad(): pl.pallas_call(input_kernel, grid=(6,), out_shape=jax.ShapeDtypeStruct((R...  4.62 us
    ppermute x1, starting transfers between devices, body(): near = lax.ppermute(near, 'core', [(0, 1), (1, 0)])  2.98 us
  transfers between devices with their start and end apart: 6, of which 3 were waited for; matrix products, arithmetic and copies ran while one was open for 0% of the time, Pallas kernels for 20%

profile of v8, /device:TPU:0, one launch (start us, length us, event | category | flops | bytes accessed | tf_op | source)
XLA Modules:
  0.0 73.8 jit_solution(10481878801514322433)
XLA Ops:
  0.7 1.4 %copy-done = bf16[48,128,128]{2,1,0:T(8,128)(2,1)S(1)} copy-done((bf16[48,128,128]{2,1,0:T(8,128)(2,1)S(1)}, bf16[48,128,128]{2,1,0:T(8,128)(2,1)}, u32[]{:S(2)}) %copy-start) | copy-done | bytes 1572888
  2.1 0.9 %copy-done.6 = bf16[12,32,256]{2,1,0:T(8,128)(2,1)S(1)} copy-done((bf16[12,32,256]{2,1,0:T(8,128)(2,1)S(1)}, bf16[12,32,256]{2,1,0:T(8,128)(2,1)}, u32[]{:S(2)}) %copy-start.6) | copy-done | bytes 196632
  3.0 0.1 pack_columns.1
  3.1 0.8 %collective-permute-start = (bf16[52,16,128]{2,1,0:T(8,128)(2,1)S(1)}, bf16[52,16,128]{2,1,0:T(8,128)(2,1)S(1)}, u32[]{:S(2)}, u32[]{:S(2)}) collective-permute-start(bf16[52,16,128]{2,1,0:T(8,128)(2,1)S(1)} %get-tuple-element.36), channel_id=1, source_target_pairs={{1,2},{2,1},{3,4},{4,3},{5,6},{6,5},{9,10},{10,9},{11,12},{12,11},... | collective-permute-start | bytes 638984 | tf_op jit(solution)/shard_map/ppermute | solution.py:747
  3.9 4.4 %collective-permute-start.1 = (bf16[52,16,128]{2,1,0:T(8,128)(2,1)S(1)}, bf16[52,16,128]{2,1,0:T(8,128)(2,1)S(1)}, u32[]{:S(2)}, u32[]{:S(2)}) collective-permute-start(bf16[52,16,128]{2,1,0:T(8,128)(2,1)S(1)} %get-tuple-element.37), channel_id=1, source_target_pairs={{0,1},{1,0},{2,3},{3,2},{4,5},{5,4},{6,7},{7,6},{8,9},{9,8},{10,11... | collective-permute-start | bytes 638984 | tf_op jit(solution)/shard_map/ppermute | solution.py:747
  8.3 1.1 %copy-done.2 = bf16[1152,256]{1,0:T(8,128)(2,1)S(1)} copy-done((bf16[1152,256]{1,0:T(8,128)(2,1)S(1)}, bf16[1152,256]{1,0:T(8,128)(2,1)}, u32[]{:S(2)}) %copy-start.2) | copy-done | bytes 589848
  9.4 1.0 %copy-done.8 = bf16[1152,128]{1,0:T(8,128)(2,1)S(1)} copy-done((bf16[1152,128]{1,0:T(8,128)(2,1)S(1)}, bf16[1152,128]{1,0:T(8,128)(2,1)}, u32[]{:S(2)}) %copy-start.8) | copy-done | bytes 294936
  10.4 1.0 %copy-done.9 = bf16[1152,128]{1,0:T(8,128)(2,1)S(1)} copy-done((bf16[1152,128]{1,0:T(8,128)(2,1)S(1)}, bf16[1152,128]{1,0:T(8,128)(2,1)}, u32[]{:S(2)}) %copy-start.9) | copy-done | bytes 294936
  11.3 1.5 %weight_forms.1 = (bf16[1536,256]{1,0:T(8,128)(2,1)S(1)}, bf16[256,1536]{1,0:T(8,128)(2,1)S(1)}, bf16[1536,256]{1,0:T(8,128)(2,1)S(1)}, bf16[256,1536]{1,0:T(8,1...) custom-call(s32[2]{0:T(128)S(1)} %copy-done.12, ...), custom_call_target="tpu_custom_call" | custom-call | tf_op jit(solution)/shard_map/weight_forms/pallas_call | solution.py:164
  12.8 0.0 copy-start.4
  12.8 0.0 collective-permute-done.two.refs_7_.refs_12_
  12.8 0.5 collective-permute-done.1.one.refs_8_.refs_13_
  13.3 0.3 pack_rows.1
  13.6 0.7 collective-permute-start.2
  14.3 3.0 %collective-permute-start.3 = (bf16[16,10,16,128]{3,2,1,0:T(8,128)(2,1)S(1)}, bf16[16,10,16,128]{3,2,1,0:T(8,128)(2,1)S(1)}, u32[]{:S(2)}, u32[]{:S(2)}) collective-permute-start(bf16[16,10,16,128]{3,2,1,0:T(8,128)(2,1)S(1)} %get-tuple-element.39), channel_id=1, source_target_pairs={{0,8},{8,0},{1,9},{9,1},{2,10},{10,2},{3,11},{11,3},{4,12},{12,4},... | collective-permute-start | bytes 1966088 | tf_op jit(solution)/shard_map/ppermute | solution.py:759
  18.0 0.0 copy-done.4
  18.0 0.0 copy-done.10
  18.0 0.0 copy-start.3
  18.0 0.0 copy-start.7
  18.0 8.4 %own_rows.1 = (bf16[48,48,768]{2,1,0:T(8,128)(2,1)S(1)}, bf16[44,48,512]{2,1,0:T(8,128)(2,1)S(1)}, bf16[22,48,512]{2,1,0:T(8,128)(2,1)S(1)}, bf16[10,48,384]{2,1,0:T(8,128)(2,1)S(1)}, f32[20,40,256]{2,1,0:T(8,128)S(1)}) custom-call(s32[1]{0:T(128)S(6)} %copy.14.refs_0_, f32[2,80,128]{2,1,0:T(8,128)S(1)} %get-tuple-element.29._.refs_1_, ...), custom_call_target="tpu_custom_call" | custom-call | flops 4000000000 | bytes 30000000 | tf_op jit(solution)/shard_map/own_rows/pallas_call | solution.py:395
  26.4 0.0 collective-permute-done.2.refs_10_
  26.4 0.0 collective-permute-done.3.refs_11_
  26.5 15.2 %encoder_levels.1 = (bf16[12,32,256]{2,1,0:T(8,128)(2,1)}, bf16[50,32,768]{2,1,0:T(8,128)(2,1)S(1)}, bf16[64,40,128]{2,1,0:T(8,128)(2,1)S(1)}, bf16[64,40,128]{2,1,0:T(8,128)(2,1)S(1)}) custom-call(s32[1]{0:T(128)S(6)} %copy.14.refs_0_, f32[2,80,128]{2,1,0:T(8,128)S(1)} %get-tuple-element.29._.refs_1_, f32[2,4,40,128]{3,2,1,0:T(8,128)S(1)} %get-tuple-element.30.refs_2_, ...), custom_call_target="tpu_custom_call" | custom-call | tf_op jit(solution)/shard_map/encoder_levels/pallas_call | solution.py:632
  41.7 0.1 collective-permute-start.4
  41.8 2.1 %collective-permute-done.4 = bf16[64,40,128]{2,1,0:T(8,128)(2,1)S(1)} collective-permute-done((bf16[64,40,128]{2,1,0:T(8,128)(2,1)S(1)}, bf16[64,40,128]{2,1,0:T(8,128)(2,1)S(1)}, u32[]{:S(2)}, u32[]{:S(2)}) %collective-permute-start.4) | collective-permute-done | bytes 655392 | tf_op jit(solution)/shard_map/ppermute | solution.py:767
  43.8 1.0 %add_convert_fusion = bf16[64,40,128]{2,1,0:T(8,128)(2,1)} fusion(bf16[64,40,128]{2,1,0:T(8,128)(2,1)S(1)} %collective-permute-done.4, bf16[64,40,128]{2,1,0:T(8,128)(2,1)S(1)} %get-tuple-element.48), kind=kLoop, calls=%fused_computation | loop fusion | flops 1310720 | bytes 1966080 | tf_op jit(solution)/shard_map/convert_element_type | solution.py:768
  44.9 12.1 %all-to-all-start = ((bf16[64,40,128]{2,1,0:T(8,128)(2,1)}), bf16[64,40,128]{2,1,0:T(8,128)(2,1)S(1)}, u32[]{:S(2)}, u32[]{:S(2)}) async-start(bf16[64,40,128]{2,1,0:T(8,128)(2,1)} %add_convert_fusion), calls=%async_computation | async-start | bytes 1310720 | tf_op jit(solution)/shard_map/all_to_all | solution.py:769
  57.0 0.0 copy-start.5
  57.0 1.1 %copy-done.5 = bf16[256,1536]{1,0:T(8,128)(2,1)S(1)} copy-done((bf16[256,1536]{1,0:T(8,128)(2,1)S(1)}, bf16[256,1536]{1,0:T(8,128)(2,1)}, u32[]{:S(2)}) %copy-start.5) | copy-done | bytes 786456
  58.1 4.6 %input_grad.1 = bf16[48,128,128]{2,1,0:T(8,128)(2,1)} custom-call(bf16[50,32,768]{2,1,0:T(8,128)(2,1)S(1)} %get-tuple-element.46.g1.g1_next, bf16[50,32,768]{2,1,0:T(8,128)(2,1)S(1)} %get-tuple-element.46.g1.g1_next, bf16[256,1536]{1,0:T(8,128)(2,1)S(1)} %copy-done.5), custom_call_target="tpu_custom_call" | custom-call | flops 1811939328 | bytes 8388608 | tf_op jit(solution)/shard_map/input_grad/pallas_call | solution.py:689
  62.7 9.3 %all-to-all-done.got = bf16[64,40,128]{2,1,0:T(8,128)(2,1)S(1)} async-done(((bf16[64,40,128]{2,1,0:T(8,128)(2,1)}), bf16[64,40,128]{2,1,0:T(8,128)(2,1)S(1)}, u32[]{:S(2)}, u32[]{:S(2)}) %all-to-all-start) | async-done | bytes 655392 | tf_op jit(solution)/shard_map/all_to_all | solution.py:769
  72.0 1.6 %collect_weights.1 = (f32[9,128]{1,0:T(8,128)}, f32[9,128]{1,0:T(8,128)}, f32[9,256]{1,0:T(8,128)}) custom-call(bf16[64,40,128]{2,1,0:T(8,128)(2,1)S(1)} %all-to-all-done.got), custom_call_target="tpu_custom_call" | custom-call | tf_op jit(solution)/shard_map/collect_weights/pallas_call | solution.py:727
  (14 shorter events, 0.0 us)
Async XLA Ops:
  0.6 7.7 %copy-start.12 = (s32[2]{0:T(128)S(1)}, s32[2]{0:T(128)}, u32[]{:S(2)}) copy-start(s32[2]{0:T(128)} %refs_0_.3) | copy-start | bytes 28
  0.6 7.7 %copy-start.11 = (f32[2,128]{1,0:T(2,128)S(1)}, f32[2,128]{1,0:T(2,128)}, u32[]{:S(2)}) copy-start(f32[2,128]{1,0:T(2,128)} %refs_4_.2) | copy-start | bytes 3076
  0.7 1.4 %copy-start = (bf16[48,128,128]{2,1,0:T(8,128)(2,1)S(1)}, bf16[48,128,128]{2,1,0:T(8,128)(2,1)}, u32[]{:S(2)}) copy-start(bf16[48,128,128]{2,1,0:T(8,128)(2,1)} %param.9) | copy-start | bytes 4718596
  2.1 0.9 %copy-start.6 = (bf16[12,32,256]{2,1,0:T(8,128)(2,1)S(1)}, bf16[12,32,256]{2,1,0:T(8,128)(2,1)}, u32[]{:S(2)}) copy-start(bf16[12,32,256]{2,1,0:T(8,128)(2,1)} %refs_4_.3) | copy-start | bytes 589828
  3.0 10.3 %copy-start.1 = (bf16[48,128,128]{2,1,0:T(8,128)(2,1)S(1)}, bf16[48,128,128]{2,1,0:T(8,128)(2,1)}, u32[]{:S(2)}) copy-start(bf16[48,128,128]{2,1,0:T(8,128)(2,1)} %param.9) | copy-start | bytes 4718596
  3.1 9.7 %collective-permute-start = (bf16[52,16,128]{2,1,0:T(8,128)(2,1)S(1)}, bf16[52,16,128]{2,1,0:T(8,128)(2,1)S(1)}, u32[]{:S(2)}, u32[]{:S(2)}) collective-permute-start(bf16[52,16,128]{2,1,0:T(8,128)(2,1)S(1)} %get-tuple-element.36), channel_id=1, source_target_pairs={{1,2},{2,1},{3,4},{4,3},{5,6},{6,5},{9,10},{10,9},{11,12},{12,11},... | collective-permute-start | bytes 638984 | tf_op jit(solution)/shard_map/ppermute | solution.py:747
  3.9 9.4 %collective-permute-start.1 = (bf16[52,16,128]{2,1,0:T(8,128)(2,1)S(1)}, bf16[52,16,128]{2,1,0:T(8,128)(2,1)S(1)}, u32[]{:S(2)}, u32[]{:S(2)}) collective-permute-start(bf16[52,16,128]{2,1,0:T(8,128)(2,1)S(1)} %get-tuple-element.37), channel_id=1, source_target_pairs={{0,1},{1,0},{2,3},{3,2},{4,5},{5,4},{6,7},{7,6},{8,9},{9,8},{10,11... | collective-permute-start | bytes 638984 | tf_op jit(solution)/shard_map/ppermute | solution.py:747
  8.3 1.1 %copy-start.2 = (bf16[1152,256]{1,0:T(8,128)(2,1)S(1)}, bf16[1152,256]{1,0:T(8,128)(2,1)}, u32[]{:S(2)}) copy-start(bf16[1152,256]{1,0:T(8,128)(2,1)} %refs_8_.1) | copy-start | bytes 1769476
  9.4 1.0 %copy-start.8 = (bf16[1152,128]{1,0:T(8,128)(2,1)S(1)}, bf16[1152,128]{1,0:T(8,128)(2,1)}, u32[]{:S(2)}) copy-start(bf16[1152,128]{1,0:T(8,128)(2,1)} %refs_1_.1) | copy-start | bytes 884740
  10.3 1.0 %copy-start.9 = (bf16[1152,128]{1,0:T(8,128)(2,1)S(1)}, bf16[1152,128]{1,0:T(8,128)(2,1)}, u32[]{:S(2)}) copy-start(bf16[1152,128]{1,0:T(8,128)(2,1)} %refs_2_.1) | copy-start | bytes 884740
  11.3 6.7 %copy-start.10 = (f32[64,256]{1,0:T(8,128)S(1)}, f32[64,256]{1,0:T(8,128)}, u32[]{:S(2)}) copy-start(f32[64,256]{1,0:T(8,128)} %refs_3_.5) | copy-start | bytes 196612
  12.8 5.2 %copy-start.4 = (bf16[256,1536]{1,0:T(8,128)(2,1)}, bf16[256,1536]{1,0:T(8,128)(2,1)S(1)}, u32[]{:S(2)}) copy-start(bf16[256,1536]{1,0:T(8,128)(2,1)S(1)} %get-tuple-element.47.w1b) | copy-start | bytes 2359300
  13.6 12.8 %collective-permute-start.2 = (bf16[16,10,16,128]{3,2,1,0:T(8,128)(2,1)S(1)}, bf16[16,10,16,128]{3,2,1,0:T(8,128)(2,1)S(1)}, u32[]{:S(2)}, u32[]{:S(2)}) collective-permute-start(bf16[16,10,16,128]{3,2,1,0:T(8,128)(2,1)S(1)} %get-tuple-element.38), channel_id=1, source_target_pairs={{8,16},{16,8},{24,32},{32,24},{40,48},{48,40},{56,64},{64,56},{72,... | collective-permute-start | bytes 1966088 | tf_op jit(solution)/shard_map/ppermute | solution.py:747
  14.3 12.1 %collective-permute-start.3 = (bf16[16,10,16,128]{3,2,1,0:T(8,128)(2,1)S(1)}, bf16[16,10,16,128]{3,2,1,0:T(8,128)(2,1)S(1)}, u32[]{:S(2)}, u32[]{:S(2)}) collective-permute-start(bf16[16,10,16,128]{3,2,1,0:T(8,128)(2,1)S(1)} %get-tuple-element.39), channel_id=1, source_target_pairs={{0,8},{8,0},{1,9},{9,1},{2,10},{10,2},{3,11},{11,3},{4,12},{12,4},... | collective-permute-start | bytes 1966088 | tf_op jit(solution)/shard_map/ppermute | solution.py:759
  18.0 8.4 %copy-start.3 = (bf16[1152,256]{1,0:T(8,128)(2,1)S(1)}, bf16[1152,256]{1,0:T(8,128)(2,1)}, u32[]{:S(2)}) copy-start(bf16[1152,256]{1,0:T(8,128)(2,1)} %refs_8_.1) | copy-start | bytes 1769476
  18.0 8.4 %copy-start.7 = (bf16[12,32,256]{2,1,0:T(8,128)(2,1)S(1)}, bf16[12,32,256]{2,1,0:T(8,128)(2,1)}, u32[]{:S(2)}) copy-start(bf16[12,32,256]{2,1,0:T(8,128)(2,1)} %refs_4_.3) | copy-start | bytes 589828
  41.7 2.2 %collective-permute-start.4 = (bf16[64,40,128]{2,1,0:T(8,128)(2,1)S(1)}, bf16[64,40,128]{2,1,0:T(8,128)(2,1)S(1)}, u32[]{:S(2)}, u32[]{:S(2)}) collective-permute-start(bf16[64,40,128]{2,1,0:T(8,128)(2,1)S(1)} %get-tuple-element.49), channel_id=1, source_target_pairs={{0,8},{8,0},{1,9},{9,1},{2,10},{10,2},{3,11},{11,3},{4,12},{12,4},... | collective-permute-start | bytes 1966088 | tf_op jit(solution)/shard_map/ppermute | solution.py:767
  44.9 27.2 %all-to-all-start = ((bf16[64,40,128]{2,1,0:T(8,128)(2,1)}), bf16[64,40,128]{2,1,0:T(8,128)(2,1)S(1)}, u32[]{:S(2)}, u32[]{:S(2)}) async-start(bf16[64,40,128]{2,1,0:T(8,128)(2,1)} %add_convert_fusion), calls=%async_computation | async-start | bytes 1310720 | tf_op jit(solution)/shard_map/all_to_all | solution.py:769
  57.0 1.1 %copy-start.5 = (bf16[256,1536]{1,0:T(8,128)(2,1)S(1)}, bf16[256,1536]{1,0:T(8,128)(2,1)}, u32[]{:S(2)}) copy-start(bf16[256,1536]{1,0:T(8,128)(2,1)} %copy-done.4) | copy-start | bytes 2359300

commit v9 on v8

--- a/solution.py
+++ b/solution.py
@@ -422,10 +422,109 @@
     )(*args)
 
 
+def halo_steps(below, rim, odd, rows_sc, cols_sc, stage, x1, mask, w1t, scale, shift, d1, x2, z0, z1):
+    def first(n):
+        start = 4 * n
+        base = start + (HALO + ROWS) * below
+
+        def load(i):
+            row = start + i
+            return flat(rim[below, row, 0:8]), rim[below, row, 8 + odd], rim[below, row, 9 - odd]
+
+        first_lines(load, base, base, (rows_sc, cols_sc), stage, x1)
+
+    def dot(t):
+        return conv_one_dot(x1, 2 * (1 + 2 * t + 30 * below), w1t)
+
+    def post(t, z):
+        m = 1 + 2 * t + 30 * below
+        conv_one_post(z, scale, shift, [mask[m // 2], mask[(m + 1) // 2]], d1, 2 * m, x2, m)
+
+    first(0)
+    first(1)
+    z = (z0, z1)
+    for t in range(4):
+        z[t % 2][0 : 8 * KW, :] = dot(t)
+        if t + 2 < 4:
+            first(t + 2)
+        if t > 0:
+            post(t - 1, z[(t - 1) % 2])
+    post(3, z1)
+
+
+def near_kernel(
+    grid_rows, grid_cols,
+    noise_index, rows_sc, cols_sc, noise, w1t, near, x1_in,
+    x1_out, d1_out, x2_out,
+    rim, stage, x1, d1, x2, mask, z0, z1, sems,
+):
+    core = lax.axis_index("core")
+    odd = odd_column()
+    under = 1 - core
+
+    def fetch(source, target, at):
+        copy = pltpu.make_async_copy(source, target, sems.at[at])
+        copy.start()
+        return copy
+
+    gets = [
+        fetch(near.at[pl.ds(0, SENT)], rim.at[under, pl.ds(1 - under, SENT)], 0),
+        fetch(x1_in.at[pl.ds(0, 4)], x1.at[pl.ds(16, 4)], 1),
+        fetch(x1_in.at[pl.ds(44, 4)], x1.at[pl.ds(60, 4)], 2),
+    ]
+    fill_mask(grid_rows // 4, grid_cols // 4, mask)
+    scale, shift = modulation(noise, noise_index)
+    for copy in gets:
+        copy.wait()
+    rim[0, 0] = jnp.zeros((10, 16, 128), BF16)
+    rim[1, SENT] = jnp.zeros((10, 16, 128), BF16)
+    for below in range(2):
+
+        @pl.when(under == below)
+        def _():
+            halo_steps(below, rim, odd, rows_sc, cols_sc, stage, x1, mask, w1t, scale, shift, d1, x2, z0, z1)
+
+    puts = [
+        fetch(x2.at[pl.ds(1 + 30 * under, 8)], x2_out, 0),
+        fetch(d1.at[pl.ds(12 + 50 * under, 6)], d1_out, 1),
+        fetch(x1.at[pl.ds(15 + 49 * under, 1)], x1_out, 2),
+    ]
+    for copy in puts:
+        copy.wait()
+
+
+def near_rows(grid_rows, grid_cols, *args):
+    def kernel(*refs):
+        near_kernel(grid_rows, grid_cols, *refs)
+
+    vm = pltpu.VMEM
+    shape = jax.ShapeDtypeStruct
+    return pl.pallas_call(
+        kernel,
+        out_shape=[shape((1, KW, 768), BF16), shape((6, KW, 512), BF16), shape((8, KW, 512), BF16)],
+        in_specs=[smem_spec()] + [vmem_spec()] * 4 + [any_spec()] * 2,
+        out_specs=[any_spec()] * 3,
+        scratch_shapes=[
+            vm((2, HALO, 10, 16, 128), BF16),
+            vm((4, 160, 128), F32),
+            vm((PAD_ROWS, KW, 768), BF16),
+            vm((PAD_ROWS, KW, 512), BF16),
+            vm((PAIRS, KW, 512), BF16),
+            vm((LOWS, KP, 128), F32),
+            vm((8 * KW, 256), F32),
+            vm((8 * KW, 256), F32),
+            pltpu.SemaphoreType.DMA((3,)),
+        ],
+        compiler_params=pltpu.CompilerParams(vmem_limit_bytes=20 * MIB),
+        cost_estimate=pl.CostEstimate(flops=2 * 10**9, bytes_accessed=8 * 10**6, transcendentals=0),
+        name="near_rows",
+    )(*args)
+
+
 def lines_kernel(
     grid_rows, grid_cols,
     noise_index, rows_sc, cols_sc, noise,
-    cot, w1t, w2t, w2b, w3, w3b, off, near, two, one, x1_in, d1_in, x2_in, x3_in, d2_in,
+    cot, w1t, w2t, w2b, w3, w3b, off, near, two, one, x1_in, d1_in, x2_in, x3_in, d2_in, x1_near, d1_near, x2_near,
     coarse_out, g1_out, keep_out, give_out,
     rim, stage, x1, d1, x2, d2, x3, cp, side, side32, g3, xb2, g2, g1, coarse,
     acc, acc3, gw, msg, mask, z0, z1, sems,
@@ -448,6 +547,12 @@
         fetch(x1_in.at[pl.ds(44, 4)], x1.at[pl.ds(60, 4)], 3),
     ]
     got_x2 = fetch(x2_in, x2.at[pl.ds(9, 22)], 4)
+    under = 1 - core
+    got_near = [
+        fetch(x2_near, x2.at[pl.ds(1 + 30 * under, 8)], 13),
+        fetch(d1_near, d1.at[pl.ds(12 + 50 * under, 6)], 14),
+        fetch(x1_near, x1.at[pl.ds(15 + 49 * under, 1)], 15),
+    ]
     units = pl.ds(ROWS + 1, 3)
     got_sides = [fetch(one.at[units], side.at[1 - odd], 5), fetch(two.at[units], side.at[odd], 6)]
     got_low = [fetch(x3_in, x3.at[pl.ds(5, 10)], 7), fetch(d2_in, d2.at[pl.ds(10, 20)], 10)]
@@ -457,44 +562,20 @@
     gw[:, 0:8, :] = jnp.zeros((4, 8, 128), F32)
     gw[:, 1160:1168, :] = jnp.zeros((4, 8, 128), F32)
     scale, shift = modulation(noise, noise_index)
-    for copy in got_rims:
+    for copy in (*got_rims, *got_edges):
         copy.wait()
     rim[0, 0] = jnp.zeros((10, 16, 128), BF16)
     rim[1, SENT] = jnp.zeros((10, 16, 128), BF16)
 
-    def first(n):
-        below, start = n // 4, 4 * (n % 4)
-        base = start + (HALO + ROWS) * below
-
-        def load(i):
-            row = start + i
-            return flat(rim[below, row, 0:8]), rim[below, row, 8 + odd], rim[below, row, 9 - odd]
-
-        first_lines(load, base, base, (rows_sc, cols_sc), stage, x1)
-
-    def mid_of(t):
-        return 1 + 2 * t if t < 4 else 23 + 2 * t
-
-    def dot(t):
-        return conv_one_dot(x1, 2 * mid_of(t), w1t)
-
-    def post(t, z):
-        m = mid_of(t)
-        conv_one_post(z, scale, shift, [mask[m // 2], mask[(m + 1) // 2]], d1, 2 * m, x2, m)
-
-    first(0)
-    first(1)
-    for copy in got_edges:
-        copy.wait()
-    z = (z0, z1)
-    for t in range(8):
-        z[t % 2][0 : 8 * KW, :] = dot(t)
-        if t + 2 < 8:
-            first(t + 2)
-        if t > 0:
-            post(t - 1, z[(t - 1) % 2])
-    post(7, z1)
+    for below in range(2):
+
+        @pl.when(core == below)
+        def _():
+            halo_steps(below, rim, odd, rows_sc, cols_sc, stage, x1, mask, w1t, scale, shift, d1, x2, z0, z1)
+
     got_x2.wait()
+    for copy in got_near:
+        copy.wait()
 
     def conv_two_dot(t):
         return product(around(x2, 2 + 28 * t, 8, slice(0, 512)), w2t[...])
@@ -601,21 +682,30 @@
         turned = acc3[:, tap * 128 : (tap + 1) * 128].T
         gw[2, pl.ds(8 + tap * 128, 128), :] = turned[:, 0:128]
         gw[3, pl.ds(8 + tap * 128, 128), :] = turned[:, 128:256]
+    line = lax.broadcasted_iota(jnp.int32, (8, 128), 0)
+    none = jnp.zeros((8, 128), F32)
+    order = (1, 2, 3, 0)
+
+    def message(parts):
+        for owner in range(128):
+            at = 8 + 9 * owner
+            rows = []
+            for t in parts:
+                start = gw[order[t], at - t : at + 8 - t, :] if t < 4 else none
+                if t > 0:
+                    rest = gw[order[t - 1], at + 9 - t : at + 17 - t, :]
+                    start = jnp.where(line < t, rest, start)
+                rows.append(start)
+            row, col = divmod(owner, 8)
+            to = slice(8 * parts[0], 8 * parts[-1] + 8)
+            msg[row % 2, (row // 2) * 8 + col, to] = jnp.concatenate(rows, axis=0).astype(BF16)
+
     grads = [g1[4:52, :, lanes].reshape(ROWS * KO, 256) for lanes in (slice(128, 384), slice(384, 640))]
     fields = [around(x1, 16, ROWS, lanes, KO) for lanes in (slice(0, 512), slice(256, 768))]
     acc[...] = weight_terms(jnp.concatenate(grads, axis=0), jnp.concatenate(fields, axis=0))
+    message((0, 1))
     fold_weights(0)
-    line = lax.broadcasted_iota(jnp.int32, (8, 128), 0)
-    none = jnp.zeros((8, 128), F32)
-    for owner in range(128):
-        at = 8 + 9 * owner
-        parts = [gw[0, at : at + 8, :]]
-        for t in range(1, 5):
-            rest = gw[t - 1, at + 9 - t : at + 17 - t, :]
-            start = gw[t, at - t : at + 8 - t, :] if t < 4 else none
-            parts.append(jnp.where(line < t, rest, start))
-        row, col = divmod(owner, 8)
-        msg[row % 2, (row // 2) * 8 + col] = jnp.concatenate(parts, axis=0).astype(BF16)
+    message((2, 3, 4))
     put_keep = fetch(msg.at[core], keep_out, 2)
     put_give = fetch(msg.at[1 - core], give_out, 3)
     put_keep.wait()
@@ -637,7 +727,7 @@
             jax.ShapeDtypeStruct((64, 40, 128), BF16),
             jax.ShapeDtypeStruct((64, 40, 128), BF16),
         ],
-        in_specs=[smem_spec()] + [vmem_spec()] * 9 + [any_spec()] * 9,
+        in_specs=[smem_spec()] + [vmem_spec()] * 9 + [any_spec()] * 12,
         out_specs=[any_spec()] * 4,
         scratch_shapes=[
             vm((2, HALO + 1, 10, 16, 128), BF16),
@@ -662,7 +752,7 @@
             vm((LOWS, KP, 128), F32),
             vm((8 * KW, 256), F32),
             vm((8 * KW, 256), F32),
-            pltpu.SemaphoreType.DMA((13,)),
+            pltpu.SemaphoreType.DMA((16,)),
         ],
         compiler_params=pltpu.CompilerParams(vmem_limit_bytes=36 * MIB),
         name="encoder_levels",
@@ -716,10 +806,10 @@
             term = held[16 * n + i].astype(F32)
             sums = term if sums is None else sums + term
     total[...] = sums
-    one[...] = total[0:9, :]
-    two[...] = total[9:18, :]
-    three[:, 0:128] = total[18:27, :]
-    three[:, 128:256] = total[27:36, :]
+    two[...] = total[0:9, :]
+    three[:, 0:128] = total[9:18, :]
+    three[:, 128:256] = total[18:27, :]
+    one[...] = total[27:36, :]
 
 
 def collect(got):
@@ -760,9 +850,10 @@
     x1, d1, x2, x3, d2 = own_rows(
         *grid, noise_index, rows_sc, cols_sc, noise_table, inputs, w1t, w2t, two, one
     )
+    x1_near, d1_near, x2_near = near_rows(*grid, noise_index, rows_sc, cols_sc, noise_table, w1t, near, x1)
     coarse, g1, keep_msg, give_msg = levels(
         *grid, noise_index, rows_sc, cols_sc, noise_table,
-        cotangent, w1t, w2t, w2b, weight_three, w3b, off, near, two, one, x1, d1, x2, x3, d2,
+        cotangent, w1t, w2t, w2b, weight_three, w3b, off, near, two, one, x1, d1, x2, x3, d2, x1_near, d1_near, x2_near,
     )
     other = lax.ppermute(give_msg, "core", [(0, 1), (1, 0)])
     msg = (keep_msg.astype(F32) + other.astype(F32)).astype(BF16)

time: 74.2 us -> 74.2 us (level)
    ppermute x1, starting transfers between devices: 2.98 us -> 0.09 us  [body(): near = lax.ppermute(near, 'core', [(0, 1), (1, 0)])]
    ppermute x1, starting transfers between devices: 0.09 us -> 2.96 us  [body(): other = lax.ppermute(give_msg, 'core', [(0, 1), (1, 0)])]
    pallas_call x0 -> x1, Pallas kernels: none -> 2.53 us  [near_rows(): pl.pallas_call(kernel, out_shape=[shape((1, KW, 768), BF16), shape((6, KW...]
    pallas_call x1, Pallas kernels: 15.2 us -> 13.5 us  [levels(): pl.pallas_call(kernel, out_shape=[jax.ShapeDtypeStruct((12, KO, 256), BF1...]
  transfers between devices with their start and end apart: 6 -> 6, of which waited for: 3 -> 3; matrix products, arithmetic and copies ran while one was open for 0% -> 0% of each run, Pallas kernels for 20% -> 23%
where the time goes in v9:
time: 74.2 us; the launch traced here: 73.7 us
  Pallas kernels  32.2 us (43%)
  starting transfers between devices  20.7 us (28%)
  waiting for transfers between devices  11.7 us (16%)
  local copies, waits for them, and re-layouts  6.49 us (9%)
  between operations  1.64 us (2%)
  other arithmetic  1.02 us (1%)
    pallas_call x1, Pallas kernels, levels(): pl.pallas_call(kernel, out_shape=[jax.ShapeDtypeStruct((12, KO, 256), BF1...  13.5 us
    all_to_all x1, starting transfers between devices, body(): got = lax.all_to_all(msg, ('chip', 'tx'), 0, 0, tiled=True)  11.7 us
    all_to_all x1, waiting for transfers between devices, body(): got = lax.all_to_all(msg, ('chip', 'tx'), 0, 0, tiled=True)  9.52 us
    pallas_call x1, Pallas kernels, own_rows(): pl.pallas_call(kernel, out_shape=[shape((48, KW, 768), BF16), shape((44,...  8.12 us
    unnamed x26, local copies, waits for them, and re-layouts  6.49 us
    ppermute x3, starting transfers between devices, swapped(): return lax.ppermute(block, axis, pairs)  5.89 us
    pallas_call x1, Pallas kernels, input_grad(): pl.pallas_call(input_kernel, grid=(6,), out_shape=jax.ShapeDtypeStruct((R...  4.62 us
    ppermute x1, starting transfers between devices, body(): other = lax.ppermute(give_msg, 'core', [(0, 1), (1, 0)])  2.96 us
  transfers between devices with their start and end apart: 6, of which 3 were waited for; matrix products, arithmetic and copies ran while one was open for 0% of the time, Pallas kernels for 23%

profile of v9, /device:TPU:0, one launch (start us, length us, event | category | flops | bytes accessed | tf_op | source)
XLA Modules:
  0.0 73.7 jit_solution(10443867584807631586)
XLA Ops:
  0.6 0.0 copy-start.12
  0.7 1.4 %copy-done = bf16[48,128,128]{2,1,0:T(8,128)(2,1)S(1)} copy-done((bf16[48,128,128]{2,1,0:T(8,128)(2,1)S(1)}, bf16[48,128,128]{2,1,0:T(8,128)(2,1)}, u32[]{:S(2)}) %copy-start) | copy-done | bytes 1572888
  2.1 0.9 %copy-done.4 = bf16[12,32,256]{2,1,0:T(8,128)(2,1)S(1)} copy-done((bf16[12,32,256]{2,1,0:T(8,128)(2,1)S(1)}, bf16[12,32,256]{2,1,0:T(8,128)(2,1)}, u32[]{:S(2)}) %copy-start.4) | copy-done | bytes 196632
  3.0 0.1 pack_columns.1
  3.1 0.8 %collective-permute-start = (bf16[52,16,128]{2,1,0:T(8,128)(2,1)S(1)}, bf16[52,16,128]{2,1,0:T(8,128)(2,1)S(1)}, u32[]{:S(2)}, u32[]{:S(2)}) collective-permute-start(bf16[52,16,128]{2,1,0:T(8,128)(2,1)S(1)} %get-tuple-element.39), channel_id=1, source_target_pairs={{1,2},{2,1},{3,4},{4,3},{5,6},{6,5},{9,10},{10,9},{11,12},{12,11},... | collective-permute-start | bytes 638984 | tf_op jit(solution)/shard_map/ppermute | solution.py:837
  3.9 4.4 %collective-permute-start.1 = (bf16[52,16,128]{2,1,0:T(8,128)(2,1)S(1)}, bf16[52,16,128]{2,1,0:T(8,128)(2,1)S(1)}, u32[]{:S(2)}, u32[]{:S(2)}) collective-permute-start(bf16[52,16,128]{2,1,0:T(8,128)(2,1)S(1)} %get-tuple-element.40), channel_id=1, source_target_pairs={{0,1},{1,0},{2,3},{3,2},{4,5},{5,4},{6,7},{7,6},{8,9},{9,8},{10,11... | collective-permute-start | bytes 638984 | tf_op jit(solution)/shard_map/ppermute | solution.py:837
  8.3 1.1 %copy-done.2 = bf16[1152,256]{1,0:T(8,128)(2,1)S(1)} copy-done((bf16[1152,256]{1,0:T(8,128)(2,1)S(1)}, bf16[1152,256]{1,0:T(8,128)(2,1)}, u32[]{:S(2)}) %copy-start.2) | copy-done | bytes 589848
  9.4 1.0 %copy-done.8 = bf16[1152,128]{1,0:T(8,128)(2,1)S(1)} copy-done((bf16[1152,128]{1,0:T(8,128)(2,1)S(1)}, bf16[1152,128]{1,0:T(8,128)(2,1)}, u32[]{:S(2)}) %copy-start.8) | copy-done | bytes 294936
  10.4 1.0 %copy-done.9 = bf16[1152,128]{1,0:T(8,128)(2,1)S(1)} copy-done((bf16[1152,128]{1,0:T(8,128)(2,1)S(1)}, bf16[1152,128]{1,0:T(8,128)(2,1)}, u32[]{:S(2)}) %copy-start.9) | copy-done | bytes 294936
  11.3 1.5 %weight_forms.1 = (bf16[1536,256]{1,0:T(8,128)(2,1)S(1)}, bf16[256,1536]{1,0:T(8,128)(2,1)S(1)}, bf16[1536,256]{1,0:T(8,128)(2,1)S(1)}, bf16[256,1536]{1,0:T(8,1...) custom-call(s32[2]{0:T(128)S(1)} %copy-done.12, ...), custom_call_target="tpu_custom_call" | custom-call | tf_op jit(solution)/shard_map/weight_forms/pallas_call | solution.py:164
  12.8 0.0 copy-start.6
  12.8 0.0 collective-permute-done.two.refs_7_.refs_12_
  12.8 0.5 collective-permute-done.1.one.refs_8_.refs_13_
  13.3 0.3 pack_rows.1
  13.6 0.1 collective-permute-start.3
  13.7 0.7 collective-permute-start.2
  15.1 8.1 %own_rows.1 = (bf16[48,48,768]{2,1,0:T(8,128)(2,1)S(1)}, bf16[44,48,512]{2,1,0:T(8,128)(2,1)S(1)}, bf16[22,48,512]{2,1,0:T(8,128)(2,1)S(1)}, bf16[10,48,384]{2,1,0:T(8,128)(2,1)S(1)}, f32[20,40,256]{2,1,0:T(8,128)S(1)}) custom-call(s32[1]{0:T(128)S(6)} %copy.14.refs_0_, f32[2,80,128]{2,1,0:T(8,128)S(1)} %get-tuple-element.32._.refs_1_, ...), custom_call_target="tpu_custom_call" | custom-call | flops 4000000000 | bytes 30000000 | tf_op jit(solution)/shard_map/own_rows/pallas_call | solution.py:395
  23.2 0.0 collective-permute-done.3.refs_5_.refs_11_
  23.2 0.0 copy-start.3
  23.3 0.0 copy-start.5
  23.3 2.5 %near_rows.1 = (bf16[1,48,768]{2,1,0:T(8,128)(2,1)S(1)}, bf16[6,48,512]{2,1,0:T(8,128)(2,1)S(1)}, bf16[8,48,512]{2,1,0:T(8,128)(2,1)S(1)}) custom-call(s32[1]{0:T(128)S(6)} %copy.14.refs_0_, f32[2,80,128]{2,1,0:T(8,128)S(1)} %get-tuple-element.32._.refs_1_, f32[2,4,40,128]{3,2,1,0:T(8,128)S(1)} %get-tuple-element.33.refs_2_, f32[64,256]{1,0:T(8,128)S(1)} %copy-done.10, ...), custom_call_target="tpu_custom_call" | custom-call | flops 2000000000 | bytes 8000000 | tf_op jit(solution)/shard_map/near_rows/pallas_call | solution.py:502
  25.8 0.0 collective-permute-done.2.refs_10_
  25.8 13.5 %encoder_levels.1 = (bf16[12,32,256]{2,1,0:T(8,128)(2,1)}, bf16[50,32,768]{2,1,0:T(8,128)(2,1)S(1)}, bf16[64,40,128]{2,1,0:T(8,128)(2,1)S(1)}, bf16[64,40,128]{2,1,0:T(8,128)(2,1)S(1)}) custom-call(s32[1]{0:T(128)S(6)} %copy.14.refs_0_, f32[2,80,128]{2,1,0:T(8,128)S(1)} %get-tuple-element.32._.refs_1_, f32[2,4,40,128]{3,2,1,0:T(8,128)S(1)} %get-tuple-element.33.refs_2_, ...), custom_call_target="tpu_custom_call" | custom-call | tf_op jit(solution)/shard_map/encoder_levels/pallas_call | solution.py:722
  39.3 3.0 %collective-permute-start.4 = (bf16[64,40,128]{2,1,0:T(8,128)(2,1)S(1)}, bf16[64,40,128]{2,1,0:T(8,128)(2,1)S(1)}, u32[]{:S(2)}, u32[]{:S(2)}) collective-permute-start(bf16[64,40,128]{2,1,0:T(8,128)(2,1)S(1)} %get-tuple-element.55), channel_id=1, source_target_pairs={{0,8},{8,0},{1,9},{9,1},{2,10},{10,2},{3,11},{11,3},{4,12},{12,4},... | collective-permute-start | bytes 1966088 | tf_op jit(solution)/shard_map/ppermute | solution.py:858
  42.3 1.7 %collective-permute-done.4 = bf16[64,40,128]{2,1,0:T(8,128)(2,1)S(1)} collective-permute-done((bf16[64,40,128]{2,1,0:T(8,128)(2,1)S(1)}, bf16[64,40,128]{2,1,0:T(8,128)(2,1)S(1)}, u32[]{:S(2)}, u32[]{:S(2)}) %collective-permute-start.4) | collective-permute-done | bytes 655392 | tf_op jit(solution)/shard_map/ppermute | solution.py:858
  44.0 1.0 %add_convert_fusion = bf16[64,40,128]{2,1,0:T(8,128)(2,1)} fusion(bf16[64,40,128]{2,1,0:T(8,128)(2,1)S(1)} %collective-permute-done.4, bf16[64,40,128]{2,1,0:T(8,128)(2,1)S(1)} %get-tuple-element.54), kind=kLoop, calls=%fused_computation | loop fusion | flops 1310720 | bytes 1966080 | tf_op jit(solution)/shard_map/convert_element_type | solution.py:859
  45.0 11.7 %all-to-all-start = ((bf16[64,40,128]{2,1,0:T(8,128)(2,1)}), bf16[64,40,128]{2,1,0:T(8,128)(2,1)S(1)}, u32[]{:S(2)}, u32[]{:S(2)}) async-start(bf16[64,40,128]{2,1,0:T(8,128)(2,1)} %add_convert_fusion), calls=%async_computation | async-start | bytes 1310720 | tf_op jit(solution)/shard_map/all_to_all | solution.py:860
  56.7 0.0 copy-start.7
  56.8 1.1 %copy-done.7 = bf16[256,1536]{1,0:T(8,128)(2,1)S(1)} copy-done((bf16[256,1536]{1,0:T(8,128)(2,1)S(1)}, bf16[256,1536]{1,0:T(8,128)(2,1)}, u32[]{:S(2)}) %copy-start.7) | copy-done | bytes 786456
  57.9 4.6 %input_grad.1 = bf16[48,128,128]{2,1,0:T(8,128)(2,1)} custom-call(bf16[50,32,768]{2,1,0:T(8,128)(2,1)S(1)} %get-tuple-element.52.g1.g1_next, bf16[50,32,768]{2,1,0:T(8,128)(2,1)S(1)} %get-tuple-element.52.g1.g1_next, bf16[256,1536]{1,0:T(8,128)(2,1)S(1)} %copy-done.7), custom_call_target="tpu_custom_call" | custom-call | flops 1811939328 | bytes 8388608 | tf_op jit(solution)/shard_map/input_grad/pallas_call | solution.py:779
  62.5 9.5 %all-to-all-done.got = bf16[64,40,128]{2,1,0:T(8,128)(2,1)S(1)} async-done(((bf16[64,40,128]{2,1,0:T(8,128)(2,1)}), bf16[64,40,128]{2,1,0:T(8,128)(2,1)S(1)}, u32[]{:S(2)}, u32[]{:S(2)}) %all-to-all-start) | async-done | bytes 655392 | tf_op jit(solution)/shard_map/all_to_all | solution.py:860
  72.0 1.6 %collect_weights.1 = (f32[9,128]{1,0:T(8,128)}, f32[9,128]{1,0:T(8,128)}, f32[9,256]{1,0:T(8,128)}) custom-call(bf16[64,40,128]{2,1,0:T(8,128)(2,1)S(1)} %all-to-all-done.got), custom_call_target="tpu_custom_call" | custom-call | tf_op jit(solution)/shard_map/collect_weights/pallas_call | solution.py:817
  (15 shorter events, 0.0 us)
Async XLA Ops:
  0.6 7.7 %copy-start.12 = (s32[2]{0:T(128)S(1)}, s32[2]{0:T(128)}, u32[]{:S(2)}) copy-start(s32[2]{0:T(128)} %refs_0_.4) | copy-start | bytes 28
  0.6 7.7 %copy-start.11 = (f32[2,128]{1,0:T(2,128)S(1)}, f32[2,128]{1,0:T(2,128)}, u32[]{:S(2)}) copy-start(f32[2,128]{1,0:T(2,128)} %refs_4_.2) | copy-start | bytes 3076
  0.7 1.4 %copy-start = (bf16[48,128,128]{2,1,0:T(8,128)(2,1)S(1)}, bf16[48,128,128]{2,1,0:T(8,128)(2,1)}, u32[]{:S(2)}) copy-start(bf16[48,128,128]{2,1,0:T(8,128)(2,1)} %param.9) | copy-start | bytes 4718596
  2.1 0.9 %copy-start.4 = (bf16[12,32,256]{2,1,0:T(8,128)(2,1)S(1)}, bf16[12,32,256]{2,1,0:T(8,128)(2,1)}, u32[]{:S(2)}) copy-start(bf16[12,32,256]{2,1,0:T(8,128)(2,1)} %refs_4_.3) | copy-start | bytes 589828
  3.0 10.3 %copy-start.1 = (bf16[48,128,128]{2,1,0:T(8,128)(2,1)S(1)}, bf16[48,128,128]{2,1,0:T(8,128)(2,1)}, u32[]{:S(2)}) copy-start(bf16[48,128,128]{2,1,0:T(8,128)(2,1)} %param.9) | copy-start | bytes 4718596
  3.1 9.7 %collective-permute-start = (bf16[52,16,128]{2,1,0:T(8,128)(2,1)S(1)}, bf16[52,16,128]{2,1,0:T(8,128)(2,1)S(1)}, u32[]{:S(2)}, u32[]{:S(2)}) collective-permute-start(bf16[52,16,128]{2,1,0:T(8,128)(2,1)S(1)} %get-tuple-element.39), channel_id=1, source_target_pairs={{1,2},{2,1},{3,4},{4,3},{5,6},{6,5},{9,10},{10,9},{11,12},{12,11},... | collective-permute-start | bytes 638984 | tf_op jit(solution)/shard_map/ppermute | solution.py:837
  3.9 9.4 %collective-permute-start.1 = (bf16[52,16,128]{2,1,0:T(8,128)(2,1)S(1)}, bf16[52,16,128]{2,1,0:T(8,128)(2,1)S(1)}, u32[]{:S(2)}, u32[]{:S(2)}) collective-permute-start(bf16[52,16,128]{2,1,0:T(8,128)(2,1)S(1)} %get-tuple-element.40), channel_id=1, source_target_pairs={{0,1},{1,0},{2,3},{3,2},{4,5},{5,4},{6,7},{7,6},{8,9},{9,8},{10,11... | collective-permute-start | bytes 638984 | tf_op jit(solution)/shard_map/ppermute | solution.py:837
  8.3 1.1 %copy-start.2 = (bf16[1152,256]{1,0:T(8,128)(2,1)S(1)}, bf16[1152,256]{1,0:T(8,128)(2,1)}, u32[]{:S(2)}) copy-start(bf16[1152,256]{1,0:T(8,128)(2,1)} %refs_8_.1) | copy-start | bytes 1769476
  9.4 1.0 %copy-start.8 = (bf16[1152,128]{1,0:T(8,128)(2,1)S(1)}, bf16[1152,128]{1,0:T(8,128)(2,1)}, u32[]{:S(2)}) copy-start(bf16[1152,128]{1,0:T(8,128)(2,1)} %refs_1_.1) | copy-start | bytes 884740
  10.3 1.0 %copy-start.9 = (bf16[1152,128]{1,0:T(8,128)(2,1)S(1)}, bf16[1152,128]{1,0:T(8,128)(2,1)}, u32[]{:S(2)}) copy-start(bf16[1152,128]{1,0:T(8,128)(2,1)} %refs_2_.1) | copy-start | bytes 884740
  11.3 3.8 %copy-start.10 = (f32[64,256]{1,0:T(8,128)S(1)}, f32[64,256]{1,0:T(8,128)}, u32[]{:S(2)}) copy-start(f32[64,256]{1,0:T(8,128)} %refs_3_.7) | copy-start | bytes 196612
  12.8 2.3 %copy-start.6 = (bf16[256,1536]{1,0:T(8,128)(2,1)}, bf16[256,1536]{1,0:T(8,128)(2,1)S(1)}, u32[]{:S(2)}) copy-start(bf16[256,1536]{1,0:T(8,128)(2,1)S(1)} %get-tuple-element.53.w1b) | copy-start | bytes 2359300
  13.6 9.6 %collective-permute-start.3 = (bf16[16,10,16,128]{3,2,1,0:T(8,128)(2,1)S(1)}, bf16[16,10,16,128]{3,2,1,0:T(8,128)(2,1)S(1)}, u32[]{:S(2)}, u32[]{:S(2)}) collective-permute-start(bf16[16,10,16,128]{3,2,1,0:T(8,128)(2,1)S(1)} %get-tuple-element.42), channel_id=1, source_target_pairs={{0,8},{8,0},{1,9},{9,1},{2,10},{10,2},{3,11},{11,3},{4,12},{12,4},... | collective-permute-start | bytes 1966088 | tf_op jit(solution)/shard_map/ppermute | solution.py:849
  13.7 12.1 %collective-permute-start.2 = (bf16[16,10,16,128]{3,2,1,0:T(8,128)(2,1)S(1)}, bf16[16,10,16,128]{3,2,1,0:T(8,128)(2,1)S(1)}, u32[]{:S(2)}, u32[]{:S(2)}) collective-permute-start(bf16[16,10,16,128]{3,2,1,0:T(8,128)(2,1)S(1)} %get-tuple-element.41), channel_id=1, source_target_pairs={{8,16},{16,8},{24,32},{32,24},{40,48},{48,40},{56,64},{64,56},{72,... | collective-permute-start | bytes 1966088 | tf_op jit(solution)/shard_map/ppermute | solution.py:837
  23.2 2.6 %copy-start.3 = (bf16[1152,256]{1,0:T(8,128)(2,1)S(1)}, bf16[1152,256]{1,0:T(8,128)(2,1)}, u32[]{:S(2)}) copy-start(bf16[1152,256]{1,0:T(8,128)(2,1)} %refs_8_.1) | copy-start | bytes 1769476
  23.3 2.6 %copy-start.5 = (bf16[12,32,256]{2,1,0:T(8,128)(2,1)S(1)}, bf16[12,32,256]{2,1,0:T(8,128)(2,1)}, u32[]{:S(2)}) copy-start(bf16[12,32,256]{2,1,0:T(8,128)(2,1)} %refs_4_.3) | copy-start | bytes 589828
  39.3 4.7 %collective-permute-start.4 = (bf16[64,40,128]{2,1,0:T(8,128)(2,1)S(1)}, bf16[64,40,128]{2,1,0:T(8,128)(2,1)S(1)}, u32[]{:S(2)}, u32[]{:S(2)}) collective-permute-start(bf16[64,40,128]{2,1,0:T(8,128)(2,1)S(1)} %get-tuple-element.55), channel_id=1, source_target_pairs={{0,8},{8,0},{1,9},{9,1},{2,10},{10,2},{3,11},{11,3},{4,12},{12,4},... | collective-permute-start | bytes 1966088 | tf_op jit(solution)/shard_map/ppermute | solution.py:858
  45.0 27.0 %all-to-all-start = ((bf16[64,40,128]{2,1,0:T(8,128)(2,1)}), bf16[64,40,128]{2,1,0:T(8,128)(2,1)S(1)}, u32[]{:S(2)}, u32[]{:S(2)}) async-start(bf16[64,40,128]{2,1,0:T(8,128)(2,1)} %add_convert_fusion), calls=%async_computation | async-start | bytes 1310720 | tf_op jit(solution)/shard_map/all_to_all | solution.py:860
  56.7 1.1 %copy-start.7 = (bf16[256,1536]{1,0:T(8,128)(2,1)S(1)}, bf16[256,1536]{1,0:T(8,128)(2,1)}, u32[]{:S(2)}) copy-start(bf16[256,1536]{1,0:T(8,128)(2,1)} %copy-done.6) | copy-start | bytes 2359300
